TPU v7x, 128 devices: a whole 4x4x4 slice. The times are simulated.
128 devices in a mesh: wide: 16 (over y, x_hi, core), narrow: 8 (over z, x_lo).
Axes of the slice: x: 4 (x_hi: 2, x_lo: 2; x = x_hi * 2 + x_lo), y: 4, z: 4, core: 2. Of those that a mesh axis runs over, the one named last changes fastest.
Arguments:
- features: bfloat16 [524288, 512], P(('wide', 'narrow')), may hold values from -6 to 6
- adjacency: bfloat16 [12288, 128, 128], P(('wide', 'narrow')), may hold values from -0.375 to 0.375
- block_rows: int32 [128, 96], P(('wide', 'narrow')), may hold values from 0 to 31, as said below
- block_cols: int32 [128, 96], P(('wide', 'narrow')), may hold values from 0 to 39, as said below
- block_count: int32 [128], P(('wide', 'narrow')), may hold values from 40 to 96, as said below
- node_count: int32 [128], P(('wide', 'narrow')), may hold values from 2048 to 4096, as said below
- halo_index: int32 [128, 4, 256], P(('wide', 'narrow')), may hold values from 0 to 2047, as said below
- weight: bfloat16 [512, 512], replicated, may hold values from -0.25 to 0.25
- bias: float32 [512], replicated, may hold values from -3 to 3
- out_grad: bfloat16 [524288, 512], P(('wide', 'narrow')), may hold values from -6 to 6
Outputs:
- output: bfloat16 [524288, 512], P(('wide', 'narrow'))
- input_grad: bfloat16 [524288, 512], P(('wide', 'narrow'))
- weight_grad: float32 [512, 512], replicated
- bias_grad: float32 [512], replicated
Inputs may be any that keep to these rules, and one draw needn't show every extreme that they name: `block_count`: each device's live slots include every one of its 32 diagonal blocks and every one of its 8 halo column blocks at least once; some device has all 96 slots live. `block_rows`: within range for live and non-live slots. `block_cols`: within range for live and non-live slots. `node_count`: some device has all 4096 slots live. `halo_index`: the 1024 rows of one device are distinct and all live.
All inputs are finite; a program needn't handle non-finite values.
Results may differ from a plain program's by a relative error of at most 0.0062.
Values may be sent and summed in bfloat16 or wider, within the bound.
No kernel may reach another device: no remote copies, remote signals or barrier semaphores. Data moves between devices by JAX's collectives and lax.ppermute only.
A program may use at most 192 MiB of HBM per device.

v0:
```python
import math

import jax
import jax.numpy as jnp
from jax import lax
from jax.sharding import PartitionSpec as P


def with_halo(cells, sides, width):
    for axis, dim in sides:
        count = lax.axis_size(axis)
        ends = count - 1
        head = lax.slice_in_dim(cells, 0, width, axis=dim)
        tail = lax.slice_in_dim(cells, cells.shape[dim] - width, cells.shape[dim], axis=dim)
        cells = jnp.concatenate(
            [
                lax.ppermute(tail, axis, [(i, (i + 1) % count) for i in range(ends)]),
                cells,
                lax.ppermute(head, axis, [((i + 1) % count, i) for i in range(ends)]),
            ],
            axis=dim,
        )
    return cells


def local(
    features,
    adjacency,
    block_rows,
    block_cols,
    block_count,
    node_count,
    halo_index,
    weight,
    bias,
    out_grad,
):
    nodes, width = features.shape
    side = adjacency.shape[1]
    row_blocks = nodes // side
    slots = adjacency.shape[0]
    rows = block_rows[0]
    cols = block_cols[0]
    live = jnp.arange(slots) < block_count[0]
    keep = (jnp.arange(nodes) < node_count[0])[:, None]
    masked = jnp.where(keep, features, jnp.zeros_like(features))
    picks = halo_index[0]
    packed = masked[picks]
    got_wide = with_halo(packed[0:2], (("wide", 0),), 1)
    got_narrow = with_halo(packed[2:4], (("narrow", 0),), 1)
    extended = jnp.concatenate([masked, got_wide[0], got_wide[3], got_narrow[0], got_narrow[3]], 0)
    col_blocks = extended.shape[0] // side
    tiles = extended.reshape(col_blocks, side, width)[cols]
    terms = jnp.einsum("bij,bjf->bif", adjacency, tiles, preferred_element_type=jnp.float32)
    row_target = jnp.where(live, rows, row_blocks)
    summed = (
        jnp.zeros((row_blocks + 1, side, width), jnp.float32).at[row_target].add(terms)[:row_blocks]
    )
    aggregated = summed.reshape(nodes, width).astype(jnp.bfloat16)
    pre = jnp.dot(aggregated, weight, preferred_element_type=jnp.float32) + bias
    sig = jax.nn.sigmoid(pre)
    output = jnp.where(keep, pre * sig, jnp.float32(0.0)).astype(jnp.bfloat16)
    dpre = jnp.where(
        keep, out_grad.astype(jnp.float32) * sig * (1.0 + pre * (1.0 - sig)), jnp.float32(0.0)
    ).astype(jnp.bfloat16)
    weight_part = jnp.dot(aggregated.T, dpre, preferred_element_type=jnp.float32)
    bias_part = jnp.sum(dpre.astype(jnp.float32), 0)
    weight_total, bias_total = lax.psum((weight_part, bias_part), ("wide", "narrow"))
    scale = 1.0 / math.sqrt(nodes * lax.axis_size("wide") * lax.axis_size("narrow"))
    back = jnp.dot(dpre, weight.T, preferred_element_type=jnp.float32).astype(jnp.bfloat16)
    back_tiles = back.reshape(row_blocks, side, width)[rows]
    back_terms = jnp.einsum(
        "bji,bjf->bif", adjacency, back_tiles, preferred_element_type=jnp.float32
    )
    col_target = jnp.where(live, cols, col_blocks)
    spread = (
        jnp.zeros((col_blocks + 1, side, width), jnp.float32)
        .at[col_target]
        .add(back_terms)[:col_blocks]
    )
    own_part = spread[:row_blocks].reshape(nodes, width)
    halo_part = spread[row_blocks:].reshape(4, picks.shape[1], width).astype(jnp.bfloat16)
    ret_wide = with_halo(halo_part[0:2], (("wide", 0),), 1)
    ret_narrow = with_halo(halo_part[2:4], (("narrow", 0),), 1)
    incoming = jnp.concatenate([ret_wide[0], ret_wide[3], ret_narrow[0], ret_narrow[3]], 0).astype(
        jnp.float32
    )
    total_grad = own_part.at[picks.reshape(-1)].add(incoming)
    input_grad = jnp.where(keep, total_grad, jnp.float32(0.0)).astype(jnp.bfloat16)
    return (output, input_grad, weight_total * scale, bias_total * scale)


def solution(mesh):
    placed = (
        P(("wide", "narrow"), None),
        P(("wide", "narrow"), None, None),
        P(("wide", "narrow"), None),
        P(("wide", "narrow"), None),
        P(("wide", "narrow")),
        P(("wide", "narrow")),
        P(("wide", "narrow"), None, None),
        P(),
        P(),
        P(("wide", "narrow"), None),
    )
    return jax.shard_map(
        local,
        mesh=mesh,
        in_specs=placed,
        out_specs=(P(("wide", "narrow"), None), P(("wide", "narrow"), None), P(), P()),
        check_vma=False,
    )
```

profile of v0, /device:TPU:1, one launch (start us, length us, event | category | flops | bytes accessed | tf_op | source)
XLA Modules:
  0.0 472.8 jit_solution(16790919941629463699)
XLA Ops:
  8.8 5.4 %constant_dynamic-update-slice_fusion = (bf16[5120,512]{1,0:T(8,128)(2,1)}, bf16[4096,512]{1,0:T(8,128)(2,1)}) fusion(bf16[4096,512]{1,0:T(8,128)(2,1)} %param.10, pred[4096]{0:T(1024)(128)(4,1)S(1)} %iota_compare_fusion), kind=kLoop, calls=%fused_computation.37 | loop fusion | flops 2097151 | bytes 12587008
  14.2 7.9 %gather_fusion = bf16[1024,512]{1,0:T(8,128)(2,1)} fusion(bf16[4096,512]{1,0:T(8,128)(2,1)} %get-tuple-element.7, s32[1024]{0:T(1024)S(1)} %broadcast_clamp_fusion), kind=kCustom, calls=%fused_computation | custom fusion | bytes 2101248 | tf_op jit(solution)/shard_map/gather | solution.py:48
  23.3 6.0 %collective-permute-start = (bf16[1,256,512]{2,1,0:T(8,128)(2,1)S(1)}, bf16[1,256,512]{2,1,0:T(8,128)(2,1)S(1)}, u32[]{:S(2)}, u32[]{:S(2)}) collective-permute-start(bf16[1,256,512]{2,1,0:T(8,128)(2,1)S(1)} %get-tuple-element.16), channel_id=1, source_target_pairs={{0,8},{8,16},{16,24},{24,32},{32,40},{40,48},{48,56},{56,64},{64,7... | collective-permute-start | bytes 786440 | tf_op jit(solution)/shard_map/ppermute | solution.py:17
  46.0 9.5 %gather_fusion.1 = bf16[96,128,512]{2,1,0:T(8,128)(2,1)} fusion(bf16[40,128,512]{2,1,0:T(8,128)(2,1)} %bitcast.70, s32[1024]{0:T(1024)S(1)} %pad_clamp_fusion.1), kind=kCustom, calls=%fused_computation.1 | custom fusion | bytes 25166208 | tf_op jit(solution)/shard_map/gather | solution.py:53
  55.5 12.9 %convolution_bitcast_fusion.1 = f32[96,128,512]{1,2,0:T(8,128)} fusion(bf16[96,128,512]{2,1,0:T(8,128)(2,1)} %gather_fusion.1, bf16[96,128,128]{2,1,0:T(8,128)(2,1)S(1)} %copy-done), kind=kOutput, calls=%fused_computation.7 | convolution fusion | flops 1610612736 | bytes 40894464 | tf_op jit(solution)/shard_map/bij,bjf->bif/dot_general | solution.py:54
  68.4 24.7 %copy.17 = f32[96,128,512]{2,1,0:T(8,128)} copy(f32[96,128,512]{1,2,0:T(8,128)} %convolution_bitcast_fusion.1) | data formatting | bytes 50331648 | tf_op jit(solution)/shard_map/bij,bjf->bif/dot_general | solution.py:54
  93.0 4.4 broadcast_in_dim.49
  97.5 54.1 %scatter_fusion = f32[33,128,512]{2,1,0:T(8,128)} fusion(f32[33,128,512]{2,1,0:T(8,128)} %broadcast_in_dim.49, s32[96]{0:T(128)S(1)} %get-tuple-element.21, f32[96,128,512]{2,1,0:T(8,128)} %copy.17), kind=kCustom, calls=%fused_computation.3 | custom fusion | flops 6291456 | bytes 75497856 | tf_op jit(solution)/shard_map/scatter-add | solution.py:57
  151.6 4.2 slice.103
  156.3 7.9 %convert_reduce_fusion = (f32[512]{0:T(512)S(1)}, bf16[4096,512]{1,0:T(8,128)(2,1)S(1)}, bf16[4096,512]{1,0:T(8,128)(2,1)}) fusion(f32[512]{0:T(512)S(1)} %copy-done.10, bf16[4096,512]{1,0:T(8,128)(2,1)S(1)} %copy-done.8, pred[4096]{0:T(1024)(128)(4,1)S(1)} %iota_compare_fusion, bf16[4096,512]{1,0:T(8,128)(2,1)S(1)} %bitcast.73, ...), kind=kOutput, calls=%fused_computation.9 | convolution fusion | flops 2183134720 | bytes 17309696 | tf_op jit(solution)/shard_map/dot_general | solution.py:60
  164.1 4.4 convolution_convert_fusion
  168.5 9.0 %gather_fusion.2 = bf16[96,128,512]{2,1,0:T(8,128)(2,1)} fusion(bf16[32,128,512]{2,1,0:T(8,128)(2,1)} %bitcast.71, s32[1024]{0:T(1024)S(1)} %pad_clamp_fusion), kind=kCustom, calls=%fused_computation.2 | custom fusion | bytes 25166208 | tf_op jit(solution)/shard_map/gather | solution.py:71
  177.6 12.9 %convolution_bitcast_fusion = f32[96,128,512]{1,2,0:T(8,128)} fusion(bf16[96,128,512]{2,1,0:T(8,128)(2,1)} %gather_fusion.2, bf16[96,128,128]{2,1,0:T(8,128)(2,1)S(1)} %copy-done), kind=kOutput, calls=%fused_computation.6 | convolution fusion | flops 1610612736 | bytes 40894464 | tf_op jit(solution)/shard_map/bji,bjf->bif/dot_general | solution.py:72
  190.4 24.7 %copy.19 = f32[96,128,512]{2,1,0:T(8,128)} copy(f32[96,128,512]{1,2,0:T(8,128)} %convolution_bitcast_fusion) | data formatting | bytes 50331648 | tf_op jit(solution)/shard_map/bji,bjf->bif/dot_general | solution.py:72
  215.1 5.4 %broadcast_in_dim.53 = f32[41,128,512]{2,1,0:T(8,128)} broadcast(f32[]{:T(128)} %constant.10.clone.1), dimensions={} | broadcast | bytes 10747908 | tf_op jit(solution)/shard_map/broadcast_in_dim | solution.py:77
  220.5 55.2 %scatter_fusion.1 = f32[41,128,512]{2,1,0:T(8,128)} fusion(f32[41,128,512]{2,1,0:T(8,128)} %broadcast_in_dim.53, s32[96]{0:T(128)S(1)} %get-tuple-element.19, f32[96,128,512]{2,1,0:T(8,128)} %copy.19), kind=kCustom, calls=%fused_computation.4 | custom fusion | flops 6291456 | bytes 75497856 | tf_op jit(solution)/shard_map/scatter-add | solution.py:79
  275.7 7.4 %convert.7 = bf16[41,128,512]{2,1,0:T(8,128)(2,1)} convert(f32[41,128,512]{2,1,0:T(8,128)} %scatter_fusion.1) | non-fusion elementwise | flops 2686976 | bytes 16121856 | tf_op jit(solution)/shard_map/convert
  285.3 7.3 %collective-permute-start.4 = (bf16[1,256,512]{2,1,0:T(8,128)(2,1)}, bf16[1,256,512]{2,1,0:T(8,128)(2,1)S(1)}, u32[]{:S(2)}, u32[]{:S(2)}) collective-permute-start(bf16[1,256,512]{2,1,0:T(8,128)(2,1)} %bitcast.24), channel_id=1, source_target_pairs={{0,8},{8,16},{16,24},{24,32},{32,40},{40,48},{48,56},{56,64},{64,7... | collective-permute-start | bytes 786440 | tf_op jit(solution)/shard_map/ppermute | solution.py:17
  294.5 4.0 collective-permute-start.6
  303.2 8.2 %slice.93 = f32[32,128,512]{2,1,0:T(8,128)} slice(f32[41,128,512]{2,1,0:T(8,128)} %scatter_fusion.1), slice={[0:32], [0:128], [0:512]} | slice | bytes 16777216 | tf_op jit(solution)/shard_map/slice | solution.py:81
  311.4 68.3 %psum.15 = f32[512]{0:T(512)S(1)} all-reduce(f32[512]{0:T(512)S(1)} %get-tuple-element.4), channel_id=1, replica_groups=mesh['wide'=16,'narrow'=8] {'wide','narrow'}, use_global_device_ids=true, to_apply=%region_5.6 | all-reduce | flops 512 | bytes 4096 | tf_op jit(solution)/shard_map/psum | solution.py:68
  380.3 14.3 %scatter_custom_fusion.2 = f32[4096,512]{1,0:T(8,128)} fusion(f32[4096,512]{1,0:T(8,128)} %bitcast.72, s32[1024]{0:T(1024)} %bitcast.79, bf16[256,512]{1,0:T(8,128)(2,1)} %bitcast.31, bf16[]{:T(256)} %constant.8, bf16[256,512]{1,0:T(8,128)(2,1)} %bitcast.29, bf16[256,512]{1,0:T(8,128)(2,1)} %bitcast.27, bf16[256,512]{1,0:T(8,128)(2,1)S(1)} %bitcast.75), kind=kCustom, calls=%fused_computation.16 | custom fusion | flops 4718592 | bytes 9437696 | tf_op jit(solution)/shard_map/scatter-add | solution.py:88
  394.5 5.2 %select_convert_fusion = bf16[4096,512]{1,0:T(8,128)(2,1)} fusion(f32[4096,512]{1,0:T(8,128)} %scatter_custom_fusion.2, pred[4096]{0:T(1024)(128)(4,1)S(1)} %iota_compare_fusion), kind=kLoop, calls=%fused_computation.10 | loop fusion | flops 2097152 | bytes 12587008 | tf_op jit(solution)/shard_map/convert_element_type | solution.py:89
  399.7 64.0 %all-reduce.2.cloned.1.call-done = f32[512,512]{1,0:T(8,128)} async-done(((f32[512,512]{1,0:T(8,128)}), f32[512,512]{1,0:T(8,128)}) %all-reduce.2.cloned.1.call-update) | async-done | bytes 1048592 | tf_op jit(solution)/shard_map/psum | solution.py:68
  (55 shorter events, 30.1 us)
Async XLA Ops:
  7.2 48.3 %copy-start = (bf16[96,128,128]{2,1,0:T(8,128)(2,1)S(1)}, bf16[96,128,128]{2,1,0:T(8,128)(2,1)}, u32[]{:S(2)}) copy-start(bf16[96,128,128]{2,1,0:T(8,128)(2,1)} %param.11) | copy-start | bytes 9437188
  7.2 456.5 %all-reduce.2.cloned.1.call-start = ((), (), s32[]{:S(2)}) async-start(), calls=%async_computation | async-start | bytes 2097152 | tf_op jit(solution)/shard_map/psum | solution.py:68
  14.2 21.3 %copy-start.5 = (s32[1,4,256]{2,1,0:T(4,128)S(1)}, s32[1,4,256]{2,1,0:T(4,128)}, u32[]{:S(2)}) copy-start(s32[1,4,256]{2,1,0:T(4,128)} %param.16) | copy-start | bytes 12292
  14.2 21.9 %copy-start.6 = (s32[1,96]{1,0:T(1,128)S(1)}, s32[1,96]{1,0:T(1,128)}, u32[]{:S(2)}) copy-start(s32[1,96]{1,0:T(1,128)} %param.13) | copy-start | bytes 1156
  14.2 21.9 %copy-start.7 = (s32[1,96]{1,0:T(1,128)S(1)}, s32[1,96]{1,0:T(1,128)}, u32[]{:S(2)}) copy-start(s32[1,96]{1,0:T(1,128)} %param.12) | copy-start | bytes 1156
  23.3 12.8 %collective-permute-start = (bf16[1,256,512]{2,1,0:T(8,128)(2,1)S(1)}, bf16[1,256,512]{2,1,0:T(8,128)(2,1)S(1)}, u32[]{:S(2)}, u32[]{:S(2)}) collective-permute-start(bf16[1,256,512]{2,1,0:T(8,128)(2,1)S(1)} %get-tuple-element.16), channel_id=1, source_target_pairs={{0,8},{8,16},{16,24},{24,32},{32,40},{40,48},{48,56},{56,64},{64,7... | collective-permute-start | bytes 786440 | tf_op jit(solution)/shard_map/ppermute | solution.py:17
  29.4 10.5 %collective-permute-start.1 = (bf16[1,256,512]{2,1,0:T(8,128)(2,1)S(1)}, bf16[1,256,512]{2,1,0:T(8,128)(2,1)S(1)}, u32[]{:S(2)}, u32[]{:S(2)}) collective-permute-start(bf16[1,256,512]{2,1,0:T(8,128)(2,1)S(1)} %get-tuple-element.15), channel_id=1, source_target_pairs={{8,0},{16,8},{24,16},{32,24},{40,32},{48,40},{56,48},{64,56},{72,6... | collective-permute-start | bytes 786440 | tf_op jit(solution)/shard_map/ppermute | solution.py:19
  31.3 9.3 %collective-permute-start.2 = (bf16[1,256,512]{2,1,0:T(8,128)(2,1)S(1)}, bf16[1,256,512]{2,1,0:T(8,128)(2,1)S(1)}, u32[]{:S(2)}, u32[]{:S(2)}) collective-permute-start(bf16[1,256,512]{2,1,0:T(8,128)(2,1)S(1)} %get-tuple-element.14), channel_id=1, source_target_pairs={{0,1},{1,2},{2,3},{3,4},{4,5},{5,6},{6,7},{8,9},{9,10},{10,11},{11... | collective-permute-start | bytes 786440 | tf_op jit(solution)/shard_map/ppermute | solution.py:17
  33.6 11.7 %collective-permute-start.3 = (bf16[1,256,512]{2,1,0:T(8,128)(2,1)S(1)}, bf16[1,256,512]{2,1,0:T(8,128)(2,1)S(1)}, u32[]{:S(2)}, u32[]{:S(2)}) collective-permute-start(bf16[1,256,512]{2,1,0:T(8,128)(2,1)S(1)} %get-tuple-element.13), channel_id=1, source_target_pairs={{1,0},{2,1},{3,2},{4,3},{5,4},{6,5},{7,6},{9,8},{10,9},{11,10},{12... | collective-permute-start | bytes 786440 | tf_op jit(solution)/shard_map/ppermute | solution.py:19
  151.6 4.6 copy-start.8
  151.6 4.7 copy-start.9
  151.6 4.7 copy-start.10
  155.8 8.4 %copy-start.1 = (bf16[32,128,512]{2,1,0:T(8,128)(2,1)}, bf16[32,128,512]{2,1,0:T(8,128)(2,1)S(1)}, u32[]{:S(2)}) copy-start(bf16[32,128,512]{2,1,0:T(8,128)(2,1)S(1)} %slice.103) | copy-start | bytes 12582916
  164.1 4.4 copy-start.3
  275.7 24.1 %copy-start.2 = (bf16[32,128,512]{2,1,0:T(8,128)(2,1)S(1)}, bf16[32,128,512]{2,1,0:T(8,128)(2,1)}, u32[]{:S(2)}) copy-start(bf16[32,128,512]{2,1,0:T(8,128)(2,1)} %copy-done.1) | copy-start | bytes 12582916
  275.7 24.1 %copy-start.4 = (bf16[4096,512]{1,0:T(8,128)(2,1)S(1)}, bf16[4096,512]{1,0:T(8,128)(2,1)}, u32[]{:S(2)}) copy-start(bf16[4096,512]{1,0:T(8,128)(2,1)} %copy-done.3) | copy-start | bytes 12582916
  285.3 95.0 %collective-permute-start.4 = (bf16[1,256,512]{2,1,0:T(8,128)(2,1)}, bf16[1,256,512]{2,1,0:T(8,128)(2,1)S(1)}, u32[]{:S(2)}, u32[]{:S(2)}) collective-permute-start(bf16[1,256,512]{2,1,0:T(8,128)(2,1)} %bitcast.24), channel_id=1, source_target_pairs={{0,8},{8,16},{16,24},{24,32},{32,40},{40,48},{48,56},{56,64},{64,7... | collective-permute-start | bytes 786440 | tf_op jit(solution)/shard_map/ppermute | solution.py:17
  292.6 87.7 %collective-permute-start.5 = (bf16[1,256,512]{2,1,0:T(8,128)(2,1)}, bf16[1,256,512]{2,1,0:T(8,128)(2,1)}, u32[]{:S(2)}, u32[]{:S(2)}) collective-permute-start(bf16[1,256,512]{2,1,0:T(8,128)(2,1)} %bitcast.26), channel_id=1, source_target_pairs={{8,0},{16,8},{24,16},{32,24},{40,32},{48,40},{56,48},{64,56},{72,6... | collective-permute-start | bytes 786440 | tf_op jit(solution)/shard_map/ppermute | solution.py:19
  294.5 85.7 %collective-permute-start.6 = (bf16[1,256,512]{2,1,0:T(8,128)(2,1)}, bf16[1,256,512]{2,1,0:T(8,128)(2,1)}, u32[]{:S(2)}, u32[]{:S(2)}) collective-permute-start(bf16[1,256,512]{2,1,0:T(8,128)(2,1)} %bitcast.28), channel_id=1, source_target_pairs={{0,1},{1,2},{2,3},{3,4},{4,5},{5,6},{6,7},{8,9},{9,10},{10,11},{11... | collective-permute-start | bytes 786440 | tf_op jit(solution)/shard_map/ppermute | solution.py:17
  298.5 81.7 %collective-permute-start.7 = (bf16[1,256,512]{2,1,0:T(8,128)(2,1)}, bf16[1,256,512]{2,1,0:T(8,128)(2,1)}, u32[]{:S(2)}, u32[]{:S(2)}) collective-permute-start(bf16[1,256,512]{2,1,0:T(8,128)(2,1)} %bitcast.30), channel_id=1, source_target_pairs={{1,0},{2,1},{3,2},{4,3},{5,4},{6,5},{7,6},{9,8},{10,9},{11,10},{12... | collective-permute-start | bytes 786440 | tf_op jit(solution)/shard_map/ppermute | solution.py:19
Sparse Core Ops, SparseCore 0:
  311.5 152.1 all-reduce.1
where the time goes:
time: 474 us; the launch traced here: 473 us
  other arithmetic  146 us (31%)
  local copies, waits for them, and re-layouts  105 us (22%)
  waiting for transfers between devices  70.9 us (15%)
  blocking collectives  68.3 us (14%)
  matrix products  41.3 us (9%)
  starting transfers between devices  26.1 us (6%)
  between operations  15.7 us (3%)
    psum x1, blocking collectives, local(): lax.psum((weight_part, bias_part), ('wide', 'narrow'))  68.3 us
    psum x1, waiting for transfers between devices, local(): lax.psum((weight_part, bias_part), ('wide', 'narrow'))  64 us
    scatter-add x1, other arithmetic, local(): spread = jnp.zeros((col_blocks + 1, side, width), jnp.float32).at[col_tar...  55.2 us
    scatter-add x1, other arithmetic, local(): jnp.zeros((row_blocks + 1, side, width), jnp.float32).at[row_target]  54.1 us
    dot_general x1, local copies, waits for them, and re-layouts, local(): jnp.einsum('bji,bjf->bif', adjacency, back_tiles, preferred_element_type=...  24.7 us
    dot_general x1, local copies, waits for them, and re-layouts, local(): jnp.einsum('bij,bjf->bif', adjacency, tiles, preferred_element_type=jnp.f...  24.7 us
    ppermute x4, starting transfers between devices, with_halo(): lax.ppermute(tail, axis, [(i, (i + 1) % count) for i in range(ends)])  19.6 us
    scatter-add x1, other arithmetic, local(): total_grad = own_part.at[picks.reshape(-1)].add(incoming)  14.3 us
  transfers between devices with their start and end apart: 9, of which 3 were waited for; matrix products, arithmetic and copies ran while one was open for 7% of the time, Pallas kernels for 0%

commit v1 on v0

v1 whole, which is shorter than its diff:
```python
import math

import jax
import jax.numpy as jnp
from jax import lax
from jax.experimental import pallas as pl
from jax.experimental.pallas import tpu as pltpu
from jax.sharding import PartitionSpec as P

F = 512
BS = 128
NODES = 4096
HALO = 256
RB = 32
ECB = 40
BLK = 96
HALF = 2048
CHUNK = 512
PEERS = 128
UNROLL = 4
BF = jnp.bfloat16
F32 = jnp.float32
VMEM_BYTES = 56 * 1024 * 1024
AXES = ("wide", "narrow")


def pack_kernel(picks, feats, out0, out1, out2, out3):
    outs = (out0, out1, out2, out3)
    lane = lax.broadcasted_iota(jnp.int32, (BS, BS), 1)
    for k in range(4):
        parts = []
        for h in range(2):
            row = picks[k : k + 1, h * BS : (h + 1) * BS]
            parts.append(jnp.transpose(jnp.broadcast_to(row.astype(F32), (BS, BS))).astype(jnp.int32))
        onehot = jnp.concatenate(
            [
                jnp.concatenate([jnp.where(t == lane + c * BS, F32(1.0), F32(0.0)).astype(BF) for c in range(HALF // BS)], 1)
                for t in parts
            ],
            0,
        )
        outs[k][...] = jnp.dot(onehot, feats[...], preferred_element_type=F32).astype(BF)


def pack(picks, features):
    return pl.pallas_call(
        pack_kernel,
        grid=(1,),
        in_specs=[
            pl.BlockSpec((4, HALO), lambda i: (0, 0)),
            pl.BlockSpec((HALF, F), lambda i: (0, 0)),
        ],
        out_specs=[pl.BlockSpec((HALO, F), lambda i: (0, 0))] * 4,
        out_shape=[jax.ShapeDtypeStruct((HALO, F), BF)] * 4,
        compiler_params=pltpu.CompilerParams(vmem_limit_bytes=VMEM_BYTES),
        name="pack",
    )(picks, features)


def main_kernel(
    rows,
    cols,
    count,
    nodes,
    feats,
    adj_in,
    h0,
    h1,
    h2,
    h3,
    weight_in,
    bias,
    grads_in,
    output,
    input_grad,
    own,
    ret0,
    ret1,
    ret2,
    ret3,
    terms,
    ext,
    adj,
    acc,
    spread,
    weight,
    grads,
    outbuf,
    back,
    wacc,
    bacc,
    sems,
    osems,
):
    live = count[0]
    alive = nodes[0]
    loads = [
        pltpu.make_async_copy(adj_in, adj, sems.at[0]),
        pltpu.make_async_copy(feats, ext.at[pl.ds(0, NODES)], sems.at[1]),
    ]
    for k, h in enumerate((h0, h1, h2, h3)):
        loads.append(pltpu.make_async_copy(h, ext.at[pl.ds(NODES + k * HALO, HALO)], sems.at[2 + k]))
    late = [
        pltpu.make_async_copy(weight_in, weight, sems.at[6]),
        pltpu.make_async_copy(grads_in, grads, sems.at[7]),
    ]
    for c in loads + late:
        c.start()

    @pl.loop(0, RB + 1)
    def _(r):
        acc[pl.ds(pl.multiple_of(r * BS, BS), BS), :] = jnp.zeros((BS, F), F32)

    @pl.loop(0, ECB + 1)
    def _(r):
        spread[pl.ds(pl.multiple_of(r * BS, BS), BS), :] = jnp.zeros((BS, F), F32)

    wacc[...] = jnp.zeros_like(wacc)
    bacc[...] = jnp.zeros_like(bacc)
    for c in loads:
        c.wait()

    @pl.loop(alive // BS, RB)
    def _(r):
        at = pl.ds(pl.multiple_of(r * BS, BS), BS)
        line = lax.broadcasted_iota(jnp.int32, (BS, F), 0) + r * BS
        ext[at, :] = jnp.where(line < alive, ext[at, :].astype(F32), F32(0.0)).astype(BF)

    def block(ref, i):
        return ref[pl.ds(pl.multiple_of(i * BS, BS), BS), :]

    @pl.loop(0, BLK // UNROLL)
    def _(i):
        prods, targets = [], []
        for u in range(UNROLL):
            b = i * UNROLL + u
            prods.append(jnp.dot(adj[b], block(ext, cols[0, b]), preferred_element_type=F32))
            targets.append(jnp.where(b < live, rows[0, b], RB))
        for prod, r in zip(prods, targets):
            at = pl.ds(pl.multiple_of(r * BS, BS), BS)
            acc[at, :] += prod

    for c in late:
        c.wait()

    @pl.loop(0, NODES // CHUNK)
    def _(i):
        base = pl.multiple_of(i * CHUNK, CHUNK)
        at = pl.ds(base, CHUNK)
        agg = acc[at, :].astype(BF)
        pre = jnp.dot(agg, weight[...], preferred_element_type=F32) + bias[...]
        sig = jax.nn.sigmoid(pre)
        keep = lax.broadcasted_iota(jnp.int32, (CHUNK, F), 0) + base < alive
        outbuf[at, :] = jnp.where(keep, pre * sig, F32(0.0)).astype(BF)
        pltpu.make_async_copy(outbuf.at[at], output.at[at], osems.at[0]).start()
        g = grads[at, :].astype(F32)
        dpre = jnp.where(keep, g * sig * (1.0 + pre * (1.0 - sig)), F32(0.0)).astype(BF)
        bacc[...] += jnp.sum(dpre.astype(F32).reshape(CHUNK // 8, 8, F), 0)
        wacc[...] += lax.dot_general(agg, dpre, (((0,), (0,)), ((), ())), preferred_element_type=F32)
        back[at, :] = lax.dot_general(
            dpre, weight[...], (((1,), (1,)), ((), ())), preferred_element_type=F32
        ).astype(BF)

    for p in range(PEERS):
        a, c = p // 4, p % 4
        terms[p, 0:16, :] = wacc[a * 16 : (a + 1) * 16, c * BS : (c + 1) * BS].astype(BF)
    total = jnp.sum(bacc[...], 0, keepdims=True)
    high = total.astype(BF).astype(F32)
    low = total - high
    lines = jnp.concatenate(
        [high[:, c * BS : (c + 1) * BS] for c in range(4)] + [low[:, c * BS : (c + 1) * BS] for c in range(4)], 0
    ).astype(BF)
    terms[:, 16:24, :] = jnp.broadcast_to(lines[None], (PEERS, 8, BS))

    @pl.loop(0, BLK // UNROLL)
    def _(i):
        prods, targets = [], []
        for u in range(UNROLL):
            b = i * UNROLL + u
            prods.append(
                lax.dot_general(
                    adj[b], block(back, rows[0, b]), (((0,), (0,)), ((), ())), preferred_element_type=F32
                )
            )
            targets.append(jnp.where(b < live, cols[0, b], ECB))
        for prod, c in zip(prods, targets):
            at = pl.ds(pl.multiple_of(c * BS, BS), BS)
            spread[at, :] += prod

    for k, ret in enumerate((ret0, ret1, ret2, ret3)):
        ret[...] = spread[NODES + k * HALO : NODES + (k + 1) * HALO, :].astype(BF)
    low_rows = pltpu.make_async_copy(spread.at[pl.ds(0, HALF)], own, osems.at[1])
    low_rows.start()
    pltpu.make_async_copy(outbuf, output, osems.at[0]).wait()

    @pl.loop(HALF // BS, RB)
    def _(r):
        at = pl.ds(pl.multiple_of(r * BS, BS), BS)
        line = lax.broadcasted_iota(jnp.int32, (BS, F), 0) + r * BS
        outbuf[at, :] = jnp.where(line < alive, spread[at, :], F32(0.0)).astype(BF)

    high_rows = pltpu.make_async_copy(
        outbuf.at[pl.ds(HALF, HALF)], input_grad.at[pl.ds(HALF, HALF)], osems.at[2]
    )
    high_rows.start()
    high_rows.wait()
    low_rows.wait()


def main(rows, cols, count, nodes, features, adjacency, halos, weight, bias, out_grad):
    smem = pl.BlockSpec(memory_space=pltpu.SMEM)
    vmem = pl.BlockSpec(memory_space=pltpu.VMEM)
    hbm = pl.BlockSpec(memory_space=pl.ANY)
    return pl.pallas_call(
        main_kernel,
        in_specs=[smem] * 4 + [hbm] * 7 + [vmem, hbm],
        out_specs=[hbm] * 3 + [vmem] * 5,
        out_shape=[
            jax.ShapeDtypeStruct((NODES, F), BF),
            jax.ShapeDtypeStruct((NODES, F), BF),
            jax.ShapeDtypeStruct((HALF, F), F32),
        ]
        + [jax.ShapeDtypeStruct((HALO, F), BF)] * 4
        + [jax.ShapeDtypeStruct((PEERS, 24, BS), BF)],
        scratch_shapes=[
            pltpu.VMEM((ECB * BS, F), BF),
            pltpu.VMEM((BLK, BS, BS), BF),
            pltpu.VMEM(((RB + 1) * BS, F), F32),
            pltpu.VMEM(((ECB + 1) * BS, F), F32),
            pltpu.VMEM((F, F), BF),
            pltpu.VMEM((NODES, F), BF),
            pltpu.VMEM((NODES, F), BF),
            pltpu.VMEM((NODES, F), BF),
            pltpu.VMEM((F, F), F32),
            pltpu.VMEM((8, F), F32),
            pltpu.SemaphoreType.DMA((8,)),
            pltpu.SemaphoreType.DMA((3,)),
        ],
        compiler_params=pltpu.CompilerParams(vmem_limit_bytes=VMEM_BYTES),
        name="main",
    )(rows, cols, count, nodes, features, adjacency, *halos, weight, bias, out_grad)


def finish_kernel(picks, own, r0, r1, r2, r3, held, input_grad, buf, sem):
    line = lax.broadcasted_iota(jnp.int32, (HALO, HALO), 0)
    copies = []
    for i in range(HALF // HALO):
        hit = [
            jnp.where(line + i * HALO == picks[k : k + 1, :], F32(1.0), F32(0.0)).astype(BF) for k in range(4)
        ]
        got = own[i * HALO : (i + 1) * HALO, :]
        for k, r in enumerate((r0, r1, r2, r3)):
            got = got + jnp.dot(hit[k], r[...], preferred_element_type=F32)
        buf[i * HALO : (i + 1) * HALO, :] = got.astype(BF)
        at = pl.ds(i * HALO, HALO)
        copies.append(pltpu.make_async_copy(buf.at[at], input_grad.at[at], sem.at[i]))
        copies[-1].start()
    for c in copies:
        c.wait()


def finish(picks, own, returned, input_grad):
    vmem = pl.BlockSpec(memory_space=pltpu.VMEM)
    hbm = pl.BlockSpec(memory_space=pl.ANY)
    return pl.pallas_call(
        finish_kernel,
        in_specs=[vmem] * 6 + [hbm],
        out_specs=hbm,
        out_shape=jax.ShapeDtypeStruct((NODES, F), BF),
        input_output_aliases={6: 0},
        scratch_shapes=[pltpu.VMEM((HALF, F), BF), pltpu.SemaphoreType.DMA((HALF // HALO,))],
        compiler_params=pltpu.CompilerParams(vmem_limit_bytes=VMEM_BYTES),
        name="finish",
    )(picks, own, *returned, input_grad)


def exchange(parts):
    got = []
    for k in range(4):
        axis = AXES[k // 2]
        count = lax.axis_size(axis)
        if k % 2 == 0:
            pairs = [(i, i + 1) for i in range(count - 1)]
        else:
            pairs = [(i + 1, i) for i in range(count - 1)]
        got.append(lax.ppermute(parts[k ^ 1], axis, pairs))
    return got


def local(features, adjacency, block_rows, block_cols, block_count, node_count, halo_index, weight, bias, out_grad):
    picks = halo_index.reshape(4, HALO)
    halos = exchange(pack(picks, features))
    output, partial_grad, own, r0, r1, r2, r3, terms = main(
        block_rows, block_cols, block_count, node_count, features, adjacency, halos, weight, bias.reshape(1, F), out_grad
    )
    returned = exchange((r0, r1, r2, r3))
    scale = 1.0 / math.sqrt(NODES * PEERS)
    gathered = lax.all_to_all(terms, AXES, 0, 0, tiled=True).astype(F32)
    sums = jnp.sum(gathered, 0) * scale
    share = sums[0:16].astype(BF)
    bias_grad = (sums[16:20] + sums[20:24]).reshape(F)
    spread_out = lax.all_to_all(jnp.broadcast_to(share[None], (PEERS, 16, BS)), AXES, 0, 0, tiled=True)
    weight_grad = spread_out.astype(F32).reshape(32, 4, 16, BS).transpose(0, 2, 1, 3).reshape(F, F)
    input_grad = finish(picks, own, returned, partial_grad)
    return (output, input_grad, weight_grad, bias_grad)


def solution(mesh):
    placed = (
        P(AXES, None),
        P(AXES, None, None),
        P(AXES, None),
        P(AXES, None),
        P(AXES),
        P(AXES),
        P(AXES, None, None),
        P(),
        P(),
        P(AXES, None),
    )
    return jax.shard_map(
        local,
        mesh=mesh,
        in_specs=placed,
        out_specs=(P(AXES, None), P(AXES, None), P(), P()),
        check_vma=False,
    )
```

time: 474 us -> 132 us (0.28)
  the two profiles are of different devices: /device:TPU:1 before, /device:TPU:10 now
where the time goes in v1:
time: 132 us; the launch traced here: 131 us
  Pallas kernels  44.8 us (34%)
  starting transfers between devices  33.4 us (25%)
  blocking collectives  24.6 us (19%)
  waiting for transfers between devices  22 us (17%)
  local copies, waits for them, and re-layouts  3.75 us (3%)
  between operations  2.11 us (2%)
    pallas_call x1, Pallas kernels, main(): pl.pallas_call(main_kernel, in_specs=[smem] * 4 + [hbm] * 7 + [vmem, hbm]...  34.5 us
    ppermute x8, starting transfers between devices, exchange(): got.append(lax.ppermute(parts[k ^ 1], axis, pairs))  27.6 us
    all_to_all x1, blocking collectives, local(): gathered = lax.all_to_all(terms, AXES, 0, 0, tiled=True).astype(F32)  24.6 us
    ppermute x8, waiting for transfers between devices, exchange(): got.append(lax.ppermute(parts[k ^ 1], axis, pairs))  22 us
    all_to_all x1, starting transfers between devices, local(): lax.all_to_all(jnp.broadcast_to(share[None], (PEERS, 16, BS)), AXES, 0, 0...  5.77 us
    pallas_call x1, Pallas kernels, finish(): pl.pallas_call(finish_kernel, in_specs=[vmem] * 6 + [hbm], out_specs=hbm,...  5.57 us
    pallas_call x1, Pallas kernels, pack(): pl.pallas_call(pack_kernel, grid=(1,), in_specs=[pl.BlockSpec((4, HALO),...  4.67 us
  transfers between devices with their start and end apart: 9, of which 4 were waited for; matrix products, arithmetic and copies ran while one was open for 0% of the time, Pallas kernels for 4%

profile of v1, /device:TPU:10, one launch (start us, length us, event | category | flops | bytes accessed | tf_op | source)
XLA Modules:
  0.0 131.5 jit_solution(15144349533763780399)
XLA Ops:
  0.6 4.7 %pack.1 = (bf16[256,512]{1,0:T(8,128)(2,1)}, bf16[256,512]{1,0:T(8,128)(2,1)}, bf16[256,512]{1,0:T(8,128)(2,1)}, bf16[256,512]{1,0:T(8,128)(2,1)}) custom-call(s32[4,256]{1,0:T(4,128)} %bitcast.16, bf16[4096,512]{1,0:T(8,128)(2,1)} %feats.3), custom_call_target="tpu_custom_call" | custom-call | tf_op jit(solution)/shard_map/pack/pallas_call | solution.py:46
  5.3 1.9 %collective-permute-start = (bf16[256,512]{1,0:T(8,128)(2,1)}, bf16[256,512]{1,0:T(8,128)(2,1)S(1)}, u32[]{:S(2)}, u32[]{:S(2)}) collective-permute-start(bf16[256,512]{1,0:T(8,128)(2,1)} %get-tuple-element.16), channel_id=1, source_target_pairs={{0,8},{8,16},{16,24},{24,32},{32,40},{40,48},{48,56},{56,64},{64,7... | collective-permute-start | bytes 786440 | tf_op jit(solution)/shard_map/ppermute | solution.py:286
  7.2 6.0 %collective-permute-start.1 = (bf16[256,512]{1,0:T(8,128)(2,1)}, bf16[256,512]{1,0:T(8,128)(2,1)S(1)}, u32[]{:S(2)}, u32[]{:S(2)}) collective-permute-start(bf16[256,512]{1,0:T(8,128)(2,1)} %get-tuple-element.17), channel_id=1, source_target_pairs={{8,0},{16,8},{24,16},{32,24},{40,32},{48,40},{56,48},{64,56},{72,6... | collective-permute-start | bytes 786440 | tf_op jit(solution)/shard_map/ppermute | solution.py:286
  13.3 3.8 %collective-permute-start.2 = (bf16[256,512]{1,0:T(8,128)(2,1)}, bf16[256,512]{1,0:T(8,128)(2,1)S(1)}, u32[]{:S(2)}, u32[]{:S(2)}) collective-permute-start(bf16[256,512]{1,0:T(8,128)(2,1)} %get-tuple-element.18), channel_id=1, source_target_pairs={{0,1},{1,2},{2,3},{3,4},{4,5},{5,6},{6,7},{8,9},{9,10},{10,11},{11... | collective-permute-start | bytes 786440 | tf_op jit(solution)/shard_map/ppermute | solution.py:286
  17.1 2.1 %collective-permute-start.3 = (bf16[256,512]{1,0:T(8,128)(2,1)}, bf16[256,512]{1,0:T(8,128)(2,1)S(1)}, u32[]{:S(2)}, u32[]{:S(2)}) collective-permute-start(bf16[256,512]{1,0:T(8,128)(2,1)} %get-tuple-element.19), channel_id=1, source_target_pairs={{1,0},{2,1},{3,2},{4,3},{5,4},{6,5},{7,6},{9,8},{10,9},{11,10},{12... | collective-permute-start | bytes 786440 | tf_op jit(solution)/shard_map/ppermute | solution.py:286
  20.5 3.7 %collective-permute-done.2.h2 = bf16[256,512]{1,0:T(8,128)(2,1)S(1)} collective-permute-done((bf16[256,512]{1,0:T(8,128)(2,1)}, bf16[256,512]{1,0:T(8,128)(2,1)S(1)}, u32[]{:S(2)}, u32[]{:S(2)}) %collective-permute-start.2) | collective-permute-done | bytes 262176 | tf_op jit(solution)/shard_map/ppermute | solution.py:286
  24.1 6.8 %collective-permute-done.3.h3 = bf16[256,512]{1,0:T(8,128)(2,1)S(1)} collective-permute-done((bf16[256,512]{1,0:T(8,128)(2,1)}, bf16[256,512]{1,0:T(8,128)(2,1)S(1)}, u32[]{:S(2)}, u32[]{:S(2)}) %collective-permute-start.3) | collective-permute-done | bytes 262176 | tf_op jit(solution)/shard_map/ppermute | solution.py:286
  30.9 0.7 copy-done.4
  31.6 34.5 %main.1 = (bf16[4096,512]{1,0:T(8,128)(2,1)}, bf16[4096,512]{1,0:T(8,128)(2,1)}, f32[2048,512]{1,0:T(8,128)}, bf16[256,512]{1,0:T(8,128)(2,1)}, bf16[256,512]{1,...) custom-call(s32[1,96]{1,0:T(1,128)} %rows.1, s32[1,96]{1,0:T(1,128)} %cols.1, ...), custom_call_target="tpu_custom_call" | custom-call | tf_op jit(solution)/shard_map/main/pallas_call | solution.py:214
  66.2 24.6 %all_to_all.10 = bf16[128,24,128]{2,1,0:T(8,128)(2,1)S(1)} all-to-all(bf16[128,24,128]{2,1,0:T(8,128)(2,1)} %get-tuple-element.27), channel_id=1, replica_groups=mesh['wide'=16,'narrow'=8] {'wide','narrow'}, dimensions={0} | all-to-all | bytes 1572864 | tf_op jit(solution)/shard_map/all_to_all | solution.py:298
  90.7 0.2 convert_reduce_fusion
  90.9 0.9 broadcast_in_dim.2
  91.8 5.8 %all-to-all-start.1 = ((bf16[128,16,128]{2,1,0:T(8,128)(2,1)}), bf16[128,16,128]{2,1,0:T(8,128)(2,1)S(1)}, u32[]{:S(2)}, u32[]{:S(2)}) async-start(bf16[128,16,128]{2,1,0:T(8,128)(2,1)} %broadcast_in_dim.2), calls=%async_computation.1 | async-start | bytes 1048576 | tf_op jit(solution)/shard_map/all_to_all | solution.py:302
  97.6 2.1 %collective-permute-start.4 = (bf16[256,512]{1,0:T(8,128)(2,1)}, bf16[256,512]{1,0:T(8,128)(2,1)S(1)}, u32[]{:S(2)}, u32[]{:S(2)}) collective-permute-start(bf16[256,512]{1,0:T(8,128)(2,1)} %get-tuple-element.22), channel_id=1, source_target_pairs={{0,8},{8,16},{16,24},{24,32},{32,40},{40,48},{48,56},{56,64},{64,7... | collective-permute-start | bytes 786440 | tf_op jit(solution)/shard_map/ppermute | solution.py:286
  99.6 5.9 %collective-permute-start.5 = (bf16[256,512]{1,0:T(8,128)(2,1)}, bf16[256,512]{1,0:T(8,128)(2,1)S(1)}, u32[]{:S(2)}, u32[]{:S(2)}) collective-permute-start(bf16[256,512]{1,0:T(8,128)(2,1)} %get-tuple-element.23), channel_id=1, source_target_pairs={{8,0},{16,8},{24,16},{32,24},{40,32},{48,40},{56,48},{64,56},{72,6... | collective-permute-start | bytes 786440 | tf_op jit(solution)/shard_map/ppermute | solution.py:286
  105.5 3.6 %collective-permute-start.6 = (bf16[256,512]{1,0:T(8,128)(2,1)}, bf16[256,512]{1,0:T(8,128)(2,1)S(1)}, u32[]{:S(2)}, u32[]{:S(2)}) collective-permute-start(bf16[256,512]{1,0:T(8,128)(2,1)} %get-tuple-element.24), channel_id=1, source_target_pairs={{0,1},{1,2},{2,3},{3,4},{4,5},{5,6},{6,7},{8,9},{9,10},{10,11},{11... | collective-permute-start | bytes 786440 | tf_op jit(solution)/shard_map/ppermute | solution.py:286
  109.2 2.2 %collective-permute-start.7 = (bf16[256,512]{1,0:T(8,128)(2,1)}, bf16[256,512]{1,0:T(8,128)(2,1)S(1)}, u32[]{:S(2)}, u32[]{:S(2)}) collective-permute-start(bf16[256,512]{1,0:T(8,128)(2,1)} %get-tuple-element.25), channel_id=1, source_target_pairs={{1,0},{2,1},{3,2},{4,3},{5,4},{6,5},{7,6},{9,8},{10,9},{11,10},{12... | collective-permute-start | bytes 786440 | tf_op jit(solution)/shard_map/ppermute | solution.py:286
  111.4 5.0 %collective-permute-done.6.r2 = bf16[256,512]{1,0:T(8,128)(2,1)S(1)} collective-permute-done((bf16[256,512]{1,0:T(8,128)(2,1)}, bf16[256,512]{1,0:T(8,128)(2,1)S(1)}, u32[]{:S(2)}, u32[]{:S(2)}) %collective-permute-start.6) | collective-permute-done | bytes 262176 | tf_op jit(solution)/shard_map/ppermute | solution.py:286
  116.4 6.6 %collective-permute-done.7.r3 = bf16[256,512]{1,0:T(8,128)(2,1)S(1)} collective-permute-done((bf16[256,512]{1,0:T(8,128)(2,1)}, bf16[256,512]{1,0:T(8,128)(2,1)S(1)}, u32[]{:S(2)}, u32[]{:S(2)}) %collective-permute-start.7) | collective-permute-done | bytes 262176 | tf_op jit(solution)/shard_map/ppermute | solution.py:286
  123.0 0.7 copy-done.7
  123.7 5.6 %finish.1 = bf16[4096,512]{1,0:T(8,128)(2,1)} custom-call(s32[4,256]{1,0:T(4,128)} %bitcast.17, f32[2048,512]{1,0:T(8,128)} %get-tuple-element.21.own, bf16[256,512]{1,0:T(8,128)(2,1)} %copy-done.3, bf16[256,512]{1,0:T(8,128)(2,1)} %copy-done.5, bf16[256,512]{1,0:T(8,128)(2,1)} %copy-done.6, ...), custom_call_target="tpu_custom_call", output_to_operand_aliasing={{}: (6, {})} | custom-call | tf_op jit(solution)/shard_map/finish/pallas_call | solution.py:265
  129.3 0.6 fusion
  130.0 0.4 copy.15
  130.4 1.0 copy.18
  (22 shorter events, 0.2 us)
Async XLA Ops:
  5.3 15.1 %collective-permute-start = (bf16[256,512]{1,0:T(8,128)(2,1)}, bf16[256,512]{1,0:T(8,128)(2,1)S(1)}, u32[]{:S(2)}, u32[]{:S(2)}) collective-permute-start(bf16[256,512]{1,0:T(8,128)(2,1)} %get-tuple-element.16), channel_id=1, source_target_pairs={{0,8},{8,16},{16,24},{24,32},{32,40},{40,48},{48,56},{56,64},{64,7... | collective-permute-start | bytes 786440 | tf_op jit(solution)/shard_map/ppermute | solution.py:286
  7.2 13.2 %collective-permute-start.1 = (bf16[256,512]{1,0:T(8,128)(2,1)}, bf16[256,512]{1,0:T(8,128)(2,1)S(1)}, u32[]{:S(2)}, u32[]{:S(2)}) collective-permute-start(bf16[256,512]{1,0:T(8,128)(2,1)} %get-tuple-element.17), channel_id=1, source_target_pairs={{8,0},{16,8},{24,16},{32,24},{40,32},{48,40},{56,48},{64,56},{72,6... | collective-permute-start | bytes 786440 | tf_op jit(solution)/shard_map/ppermute | solution.py:286
  13.3 10.9 %collective-permute-start.2 = (bf16[256,512]{1,0:T(8,128)(2,1)}, bf16[256,512]{1,0:T(8,128)(2,1)S(1)}, u32[]{:S(2)}, u32[]{:S(2)}) collective-permute-start(bf16[256,512]{1,0:T(8,128)(2,1)} %get-tuple-element.18), channel_id=1, source_target_pairs={{0,1},{1,2},{2,3},{3,4},{4,5},{5,6},{6,7},{8,9},{9,10},{10,11},{11... | collective-permute-start | bytes 786440 | tf_op jit(solution)/shard_map/ppermute | solution.py:286
  17.1 13.9 %collective-permute-start.3 = (bf16[256,512]{1,0:T(8,128)(2,1)}, bf16[256,512]{1,0:T(8,128)(2,1)S(1)}, u32[]{:S(2)}, u32[]{:S(2)}) collective-permute-start(bf16[256,512]{1,0:T(8,128)(2,1)} %get-tuple-element.19), channel_id=1, source_target_pairs={{1,0},{2,1},{3,2},{4,3},{5,4},{6,5},{7,6},{9,8},{10,9},{11,10},{12... | collective-permute-start | bytes 786440 | tf_op jit(solution)/shard_map/ppermute | solution.py:286
  20.4 10.5 %copy-start = (bf16[256,512]{1,0:T(8,128)(2,1)}, bf16[256,512]{1,0:T(8,128)(2,1)S(1)}, u32[]{:S(2)}) copy-start(bf16[256,512]{1,0:T(8,128)(2,1)S(1)} %collective-permute-done.h0) | copy-start | bytes 786436
  20.5 10.5 %copy-start.1 = (bf16[256,512]{1,0:T(8,128)(2,1)}, bf16[256,512]{1,0:T(8,128)(2,1)S(1)}, u32[]{:S(2)}) copy-start(bf16[256,512]{1,0:T(8,128)(2,1)S(1)} %collective-permute-done.1.h1) | copy-start | bytes 786436
  24.1 6.8 %copy-start.2 = (bf16[256,512]{1,0:T(8,128)(2,1)}, bf16[256,512]{1,0:T(8,128)(2,1)S(1)}, u32[]{:S(2)}) copy-start(bf16[256,512]{1,0:T(8,128)(2,1)S(1)} %collective-permute-done.2.h2) | copy-start | bytes 786436
  30.9 0.7 copy-start.4
  91.8 38.1 %all-to-all-start.1 = ((bf16[128,16,128]{2,1,0:T(8,128)(2,1)}), bf16[128,16,128]{2,1,0:T(8,128)(2,1)S(1)}, u32[]{:S(2)}, u32[]{:S(2)}) async-start(bf16[128,16,128]{2,1,0:T(8,128)(2,1)} %broadcast_in_dim.2), calls=%async_computation.1 | async-start | bytes 1048576 | tf_op jit(solution)/shard_map/all_to_all | solution.py:302
  97.6 13.9 %collective-permute-start.4 = (bf16[256,512]{1,0:T(8,128)(2,1)}, bf16[256,512]{1,0:T(8,128)(2,1)S(1)}, u32[]{:S(2)}, u32[]{:S(2)}) collective-permute-start(bf16[256,512]{1,0:T(8,128)(2,1)} %get-tuple-element.22), channel_id=1, source_target_pairs={{0,8},{8,16},{16,24},{24,32},{32,40},{40,48},{48,56},{56,64},{64,7... | collective-permute-start | bytes 786440 | tf_op jit(solution)/shard_map/ppermute | solution.py:286
  99.6 11.8 %collective-permute-start.5 = (bf16[256,512]{1,0:T(8,128)(2,1)}, bf16[256,512]{1,0:T(8,128)(2,1)S(1)}, u32[]{:S(2)}, u32[]{:S(2)}) collective-permute-start(bf16[256,512]{1,0:T(8,128)(2,1)} %get-tuple-element.23), channel_id=1, source_target_pairs={{8,0},{16,8},{24,16},{32,24},{40,32},{48,40},{56,48},{64,56},{72,6... | collective-permute-start | bytes 786440 | tf_op jit(solution)/shard_map/ppermute | solution.py:286
  105.5 10.9 %collective-permute-start.6 = (bf16[256,512]{1,0:T(8,128)(2,1)}, bf16[256,512]{1,0:T(8,128)(2,1)S(1)}, u32[]{:S(2)}, u32[]{:S(2)}) collective-permute-start(bf16[256,512]{1,0:T(8,128)(2,1)} %get-tuple-element.24), channel_id=1, source_target_pairs={{0,1},{1,2},{2,3},{3,4},{4,5},{5,6},{6,7},{8,9},{9,10},{10,11},{11... | collective-permute-start | bytes 786440 | tf_op jit(solution)/shard_map/ppermute | solution.py:286
  109.2 13.9 %collective-permute-start.7 = (bf16[256,512]{1,0:T(8,128)(2,1)}, bf16[256,512]{1,0:T(8,128)(2,1)S(1)}, u32[]{:S(2)}, u32[]{:S(2)}) collective-permute-start(bf16[256,512]{1,0:T(8,128)(2,1)} %get-tuple-element.25), channel_id=1, source_target_pairs={{1,0},{2,1},{3,2},{4,3},{5,4},{6,5},{7,6},{9,8},{10,9},{11,10},{12... | collective-permute-start | bytes 786440 | tf_op jit(solution)/shard_map/ppermute | solution.py:286
  111.4 11.6 %copy-start.3 = (bf16[256,512]{1,0:T(8,128)(2,1)}, bf16[256,512]{1,0:T(8,128)(2,1)S(1)}, u32[]{:S(2)}) copy-start(bf16[256,512]{1,0:T(8,128)(2,1)S(1)} %collective-permute-done.4.r0) | copy-start | bytes 786436
  111.4 11.6 %copy-start.5 = (bf16[256,512]{1,0:T(8,128)(2,1)}, bf16[256,512]{1,0:T(8,128)(2,1)S(1)}, u32[]{:S(2)}) copy-start(bf16[256,512]{1,0:T(8,128)(2,1)S(1)} %collective-permute-done.5.r1) | copy-start | bytes 786436
  116.4 6.6 %copy-start.6 = (bf16[256,512]{1,0:T(8,128)(2,1)}, bf16[256,512]{1,0:T(8,128)(2,1)S(1)}, u32[]{:S(2)}) copy-start(bf16[256,512]{1,0:T(8,128)(2,1)S(1)} %collective-permute-done.6.r2) | copy-start | bytes 786436
  123.0 0.7 copy-start.7

commit v2 on v1

v2 whole, which is shorter than its diff:
```python
import math

import jax
import jax.numpy as jnp
from jax import lax
from jax.experimental import pallas as pl
from jax.experimental.pallas import tpu as pltpu
from jax.sharding import PartitionSpec as P

F = 512
BS = 128
NODES = 4096
HALO = 256
RB = 32
ECB = 40
BLK = 96
HALF = 2048
CHUNK = 1024
PEERS = 128
UNROLL = 16
BF = jnp.bfloat16
F32 = jnp.float32
VMEM_BYTES = 24 * 1024 * 1024
VMEM_OWN = 20 * 1024 * 1024
VMEM_DENSE = 36 * 1024 * 1024
VMEM_BACK = 28 * 1024 * 1024
AXES = ("wide", "narrow")


SMEM = pl.BlockSpec(memory_space=pltpu.SMEM)
VMEM = pl.BlockSpec(memory_space=pltpu.VMEM)
HBM = pl.BlockSpec(memory_space=pl.ANY)


def cost(us):
    return pl.CostEstimate(flops=int(us * 1e9), bytes_accessed=int(us * 3e6), transcendentals=0)


def held(x):
    return pltpu.with_memory_space_constraint(x, pltpu.VMEM)


def in_hbm(x):
    return pltpu.with_memory_space_constraint(x, pltpu.HBM)


def pack_kernel(picks, feats_in, out0, out1, out2, out3, onehot, feats, sem):
    outs = (out0, out1, out2, out3)
    load = pltpu.make_async_copy(feats_in.at[pl.ds(0, HALF)], feats, sem.at[0])
    load.start()
    lane = lax.broadcasted_iota(jnp.int32, (BS, BS), 1)

    def build(k):
        for h in range(2):
            row = picks[k : k + 1, h * BS : (h + 1) * BS]
            t = jnp.transpose(jnp.broadcast_to(row.astype(F32), (BS, BS))).astype(jnp.int32)
            for c in range(HALF // BS):
                hit = jnp.where(t == lane + c * BS, F32(1.0), F32(0.0)).astype(BF)
                onehot[k * HALO + h * BS : k * HALO + (h + 1) * BS, c * BS : (c + 1) * BS] = hit

    build(0)
    build(1)
    load.wait()
    for k in range(4):
        if k >= 2:
            build(k)
        outs[k][...] = jnp.dot(onehot[k * HALO : (k + 1) * HALO, :], feats[...], preferred_element_type=F32).astype(BF)


def pack(picks, features):
    return pl.pallas_call(
        pack_kernel,
        in_specs=[VMEM, HBM],
        out_specs=[VMEM] * 4,
        out_shape=[jax.ShapeDtypeStruct((HALO, F), BF)] * 4,
        scratch_shapes=[
            pltpu.VMEM((4 * HALO, HALF), BF),
            pltpu.VMEM((HALF, F), BF),
            pltpu.SemaphoreType.DMA((1,)),
        ],
        compiler_params=pltpu.CompilerParams(vmem_limit_bytes=VMEM_BYTES),
        cost_estimate=cost(3),
        name="pack",
    )(picks, in_hbm(features))


def block(ref, i):
    return ref[pl.ds(pl.multiple_of(i * BS, BS), BS), :]


def tail_mask(ref, start, alive):
    @pl.loop(start, RB)
    def _(r):
        at = pl.ds(pl.multiple_of(r * BS, BS), BS)
        line = lax.broadcasted_iota(jnp.int32, (BS, F), 0) + r * BS
        ref[at, :] = jnp.where(line < alive, ref[at, :].astype(F32), F32(0.0)).astype(BF)


def zero_blocks(ref, count):
    @pl.loop(0, count)
    def _(r):
        ref[pl.ds(pl.multiple_of(r * BS, BS), BS), :] = jnp.zeros((BS, F), F32)


def slot_list(table, rows, cols, live, halo, spare):
    def step(b, n):
        c = cols[0, b]
        take = jnp.logical_and(b < live, (c >= RB) == (halo == 1))
        table[n] = b + (rows[0, b] << 8) + (c << 16)
        return n + take.astype(jnp.int32)

    n = lax.fori_loop(0, BLK, step, jnp.int32(0))
    for u in range(UNROLL):
        table[n + u] = jnp.int32(spare)
    return (n + UNROLL - 1) // UNROLL


def unpack(code):
    return code & 255, (code >> 8) & 255, code >> 16


def own_kernel(rows, cols, count, nodes, feats, adj_in, acc, adj, ext, table, sems):
    loads = [
        pltpu.make_async_copy(adj_in, adj, sems.at[0]),
        pltpu.make_async_copy(feats, ext, sems.at[1]),
    ]
    for c in loads:
        c.start()
    zero_blocks(acc, RB + 1)
    groups = slot_list(table, rows, cols, count[0], 0, RB << 8)
    for c in loads:
        c.wait()
    tail_mask(ext, nodes[0] // BS, nodes[0])

    @pl.loop(0, groups)
    def _(i):
        prods, targets = [], []
        for u in range(UNROLL):
            b, r, c = unpack(table[i * UNROLL + u])
            prods.append(jnp.dot(adj[b], block(ext, c), preferred_element_type=F32))
            targets.append(r)
        for prod, r in zip(prods, targets):
            at = pl.ds(pl.multiple_of(r * BS, BS), BS)
            acc[at, :] += prod


def own_part(rows, cols, count, nodes, features, adjacency):
    return pl.pallas_call(
        own_kernel,
        in_specs=[SMEM] * 4 + [HBM] * 2,
        out_specs=[VMEM] * 2,
        out_shape=[pltpu.VMEM(((RB + 1) * BS, F), F32), pltpu.VMEM((BLK, BS, BS), BF)],
        scratch_shapes=[
            pltpu.VMEM((NODES, F), BF),
            pltpu.SMEM((BLK + UNROLL,), jnp.int32),
            pltpu.SemaphoreType.DMA((2,)),
        ],
        compiler_params=pltpu.CompilerParams(vmem_limit_bytes=VMEM_OWN),
        cost_estimate=cost(8),
        name="own_part",
    )(rows, cols, count, nodes, in_hbm(features), in_hbm(adjacency))


def dense_kernel(
    rows, cols, count, nodes, acc_in, adj, h0, h1, h2, h3, weight, bias, grads_in,
    acc, output, back_out, ret0, ret1, ret2, ret3, terms,
    back, received, spread, grads, outbuf, wacc, bacc, table, gsems, osems,
):
    alive = nodes[0]
    halos = (h0, h1, h2, h3)

    def grad_copy(i):
        at = pl.ds(pl.multiple_of(i * CHUNK, CHUNK), CHUNK)
        return pltpu.make_async_copy(grads_in.at[at], grads.at[at], gsems.at[i])

    for i in range(NODES // CHUNK):
        grad_copy(i).start()
    groups = slot_list(table, rows, cols, count[0], 1, (RB << 8) + (ECB << 16))
    zero_blocks(spread, ECB - RB + 1)
    wacc[...] = jnp.zeros_like(wacc)
    bacc[...] = jnp.zeros_like(bacc)
    for k in range(4):
        hal_at = pl.ds(k * HALO, HALO)
        received[hal_at, :] = halos[k][...]

    @pl.loop(0, groups)
    def _(i):
        prods, targets = [], []
        for u in range(UNROLL):
            b, r, c = unpack(table[i * UNROLL + u])
            prods.append(jnp.dot(adj[b], block(received, c - RB), preferred_element_type=F32))
            targets.append(r)
        for prod, r in zip(prods, targets):
            at = pl.ds(pl.multiple_of(r * BS, BS), BS)
            acc[at, :] += prod

    @pl.loop(0, NODES // CHUNK)
    def _(i):
        base = pl.multiple_of(i * CHUNK, CHUNK)
        at = pl.ds(base, CHUNK)
        grad_copy(i).wait()
        agg = acc[at, :].astype(BF)
        pre = jnp.dot(agg, weight[...], preferred_element_type=F32) + bias[...]
        sig = jax.nn.sigmoid(pre)
        keep = lax.broadcasted_iota(jnp.int32, (CHUNK, F), 0) + base < alive
        outbuf[at, :] = jnp.where(keep, pre * sig, F32(0.0)).astype(BF)
        pltpu.make_async_copy(outbuf.at[at], output.at[at], osems.at[0]).start()
        g = grads[at, :].astype(F32)
        dpre = jnp.where(keep, g * sig * (1.0 + pre * (1.0 - sig)), F32(0.0)).astype(BF)
        bacc[...] += jnp.sum(dpre.astype(F32).reshape(CHUNK // 8, 8, F), 0)
        wacc[...] += lax.dot_general(agg, dpre, (((0,), (0,)), ((), ())), preferred_element_type=F32)
        back[at, :] = lax.dot_general(
            dpre, weight[...], (((1,), (1,)), ((), ())), preferred_element_type=F32
        ).astype(BF)
        pltpu.make_async_copy(back.at[at], back_out.at[at], osems.at[1]).start()

    for p in range(PEERS):
        for t in range(2):
            a, c = p // 2, p % 2 * 2 + t
            terms[p, 8 * t : 8 * t + 8, :] = wacc[a * 8 : (a + 1) * 8, c * BS : (c + 1) * BS].astype(BF)
    total = jnp.sum(bacc[...], 0, keepdims=True)
    high = total.astype(BF).astype(F32)
    low = total - high
    lines = jnp.concatenate(
        [high[:, c * BS : (c + 1) * BS] for c in range(4)] + [low[:, c * BS : (c + 1) * BS] for c in range(4)], 0
    ).astype(BF)
    terms[:, 16:24, :] = jnp.broadcast_to(lines[None], (PEERS, 8, BS))

    @pl.loop(0, groups)
    def _(i):
        prods, targets = [], []
        for u in range(UNROLL):
            b, r, c = unpack(table[i * UNROLL + u])
            r = jnp.where(r < RB, r, 0)
            prods.append(
                lax.dot_general(adj[b], block(back, r), (((0,), (0,)), ((), ())), preferred_element_type=F32)
            )
            targets.append(c - RB)
        for prod, c in zip(prods, targets):
            at = pl.ds(pl.multiple_of(c * BS, BS), BS)
            spread[at, :] += prod

    for k, ret in enumerate((ret0, ret1, ret2, ret3)):
        ret[...] = spread[k * HALO : (k + 1) * HALO, :].astype(BF)
    pltpu.make_async_copy(outbuf, output, osems.at[0]).wait()
    pltpu.make_async_copy(back, back_out, osems.at[1]).wait()


def dense_part(rows, cols, count, nodes, acc, adj, halos, weight, bias, out_grad):
    return pl.pallas_call(
        dense_kernel,
        in_specs=[SMEM] * 4 + [VMEM] * 8 + [HBM],
        out_specs=[VMEM, HBM, HBM] + [VMEM] * 5,
        out_shape=[
            pltpu.VMEM(((RB + 1) * BS, F), F32),
            jax.ShapeDtypeStruct((NODES, F), BF),
            jax.ShapeDtypeStruct((NODES, F), BF),
        ]
        + [jax.ShapeDtypeStruct((HALO, F), BF)] * 4
        + [jax.ShapeDtypeStruct((PEERS, 24, BS), BF)],
        input_output_aliases={4: 0},
        scratch_shapes=[
            pltpu.VMEM((NODES, F), BF),
            pltpu.VMEM(((ECB - RB + 1) * BS, F), BF),
            pltpu.VMEM(((ECB - RB + 1) * BS, F), F32),
            pltpu.VMEM((NODES, F), BF),
            pltpu.VMEM((NODES, F), BF),
            pltpu.VMEM((F, F), F32),
            pltpu.VMEM((8, F), F32),
            pltpu.SMEM((BLK + UNROLL,), jnp.int32),
            pltpu.SemaphoreType.DMA((NODES // CHUNK,)),
            pltpu.SemaphoreType.DMA((2,)),
        ],
        compiler_params=pltpu.CompilerParams(vmem_limit_bytes=VMEM_DENSE),
        cost_estimate=cost(16),
        name="dense_part",
    )(rows, cols, count, nodes, held(acc), held(adj), *halos, weight, bias, in_hbm(out_grad))[1:]


def back_kernel(
    rows, cols, count, nodes, adj_in, back_in, picks, r0, r1, r2, r3, input_grad, adj, back, spread, outbuf, table, sems
):
    alive = nodes[0]
    loads = [
        pltpu.make_async_copy(adj_in, adj, sems.at[2]),
        pltpu.make_async_copy(back_in, back, sems.at[3]),
    ]
    for c in loads:
        c.start()
    zero_blocks(spread, RB + 1)
    groups = slot_list(table, rows, cols, count[0], 0, RB << 16)
    for c in loads:
        c.wait()

    @pl.loop(0, groups)
    def _(i):
        prods, targets = [], []
        for u in range(UNROLL):
            b, r, c = unpack(table[i * UNROLL + u])
            prods.append(
                lax.dot_general(adj[b], block(back, r), (((0,), (0,)), ((), ())), preferred_element_type=F32)
            )
            targets.append(c)
        for prod, c in zip(prods, targets):
            at = pl.ds(pl.multiple_of(c * BS, BS), BS)
            spread[at, :] += prod

    @pl.loop(HALF // BS, RB)
    def _(r):
        at = pl.ds(pl.multiple_of(r * BS, BS), BS)
        line = lax.broadcasted_iota(jnp.int32, (BS, F), 0) + r * BS
        outbuf[at, :] = jnp.where(line < alive, spread[at, :], F32(0.0)).astype(BF)

    top = pltpu.make_async_copy(outbuf.at[pl.ds(HALF, HALF)], input_grad.at[pl.ds(HALF, HALF)], sems.at[0])
    top.start()
    line = lax.broadcasted_iota(jnp.int32, (HALO, HALO), 0)

    @pl.loop(0, HALF // HALO)
    def _(i):
        at = pl.ds(pl.multiple_of(i * HALO, HALO), HALO)
        got = spread[at, :]
        for k, r in enumerate((r0, r1, r2, r3)):
            hit = jnp.where(line + i * HALO == picks[k : k + 1, :], F32(1.0), F32(0.0)).astype(BF)
            got = got + jnp.dot(hit, r[...], preferred_element_type=F32)
        outbuf[at, :] = got.astype(BF)
        pltpu.make_async_copy(outbuf.at[at], input_grad.at[at], sems.at[1]).start()

    low = pl.ds(0, HALF)
    pltpu.make_async_copy(outbuf.at[low], input_grad.at[low], sems.at[1]).wait()
    top.wait()


def back_part(rows, cols, count, nodes, adj, back, picks, returned):
    return pl.pallas_call(
        back_kernel,
        in_specs=[SMEM] * 4 + [HBM] * 2 + [VMEM] * 5,
        out_specs=HBM,
        out_shape=jax.ShapeDtypeStruct((NODES, F), BF),
        scratch_shapes=[
            pltpu.VMEM((BLK, BS, BS), BF),
            pltpu.VMEM((NODES, F), BF),
            pltpu.VMEM(((RB + 1) * BS, F), F32),
            pltpu.VMEM((NODES, F), BF),
            pltpu.SMEM((BLK + UNROLL,), jnp.int32),
            pltpu.SemaphoreType.DMA((4,)),
        ],
        compiler_params=pltpu.CompilerParams(vmem_limit_bytes=VMEM_BACK),
        cost_estimate=cost(12),
        name="back_part",
    )(rows, cols, count, nodes, in_hbm(adj), in_hbm(back), picks, *returned)


def exchange(parts):
    got = []
    for k in range(4):
        axis = AXES[k // 2]
        count = lax.axis_size(axis)
        if k % 2 == 0:
            pairs = [(i, i + 1) for i in range(count - 1)]
        else:
            pairs = [(i + 1, i) for i in range(count - 1)]
        got.append(lax.ppermute(parts[k ^ 1], axis, pairs))
    return got


def local(features, adjacency, block_rows, block_cols, block_count, node_count, halo_index, weight, bias, out_grad):
    picks = halo_index.reshape(4, HALO)
    tables = (block_rows, block_cols, block_count, node_count)
    packed = pack(picks, features)
    packed, adjacency = lax.optimization_barrier((packed, adjacency))
    acc, adj = own_part(*tables, features, adjacency)
    halos = exchange(packed)
    output, back, r0, r1, r2, r3, terms = dense_part(
        *tables, acc, adj, halos, weight, bias.reshape(1, F), out_grad
    )
    returned = exchange((r0, r1, r2, r3))
    scale = 1.0 / math.sqrt(NODES * PEERS)
    gathered = lax.all_to_all(terms, AXES, 0, 0, tiled=True).astype(F32)
    sums = jnp.sum(gathered, 0) * scale
    share = sums[0:16].astype(BF)
    bias_grad = (sums[16:20] + sums[20:24]).reshape(F)
    tiles = jnp.broadcast_to(share[None], (PEERS, 16, BS))
    tiles, picks = lax.optimization_barrier((tiles, picks))
    tiles = lax.all_to_all(tiles, AXES, 0, 0, tiled=True)
    weight_grad = tiles.astype(F32).reshape(64, 4, 8, BS).transpose(0, 2, 1, 3).reshape(F, F)
    input_grad = back_part(*tables, adjacency, back, picks, returned)
    return (output, input_grad, weight_grad, bias_grad)


def solution(mesh):
    placed = (
        P(AXES, None),
        P(AXES, None, None),
        P(AXES, None),
        P(AXES, None),
        P(AXES),
        P(AXES),
        P(AXES, None, None),
        P(),
        P(),
        P(AXES, None),
    )
    return jax.shard_map(
        local,
        mesh=mesh,
        in_specs=placed,
        out_specs=(P(AXES, None), P(AXES, None), P(), P()),
        check_vma=False,
    )
```

time: 132 us -> 97.4 us (0.74)
  the two profiles are of different devices: /device:TPU:10 before, /device:TPU:1 now
where the time goes in v2:
time: 97.4 us; the launch traced here: 96.6 us
  starting transfers between devices  43.6 us (45%)
  Pallas kernels  34.6 us (36%)
  waiting for transfers between devices  12.8 us (13%)
  between operations  2.15 us (2%)
  other arithmetic  1.84 us (2%)
  local copies, waits for them, and re-layouts  1.57 us (2%)
    ppermute x8, starting transfers between devices, exchange(): got.append(lax.ppermute(parts[k ^ 1], axis, pairs))  21.9 us
    pallas_call x1, Pallas kernels, dense_part(): pl.pallas_call(dense_kernel, in_specs=[SMEM] * 4 + [VMEM] * 8 + [HBM], ou...  15.2 us
    all_to_all x1, starting transfers between devices, local(): gathered = lax.all_to_all(terms, AXES, 0, 0, tiled=True).astype(F32)  13.7 us
    pallas_call x1, Pallas kernels, back_part(): pl.pallas_call(back_kernel, in_specs=[SMEM] * 4 + [HBM] * 2 + [VMEM] * 5,...  9.9 us
    all_to_all x1, starting transfers between devices, local(): tiles = lax.all_to_all(tiles, AXES, 0, 0, tiled=True)  7.99 us
    all_to_all x1, waiting for transfers between devices, local(): gathered = lax.all_to_all(terms, AXES, 0, 0, tiled=True).astype(F32)  6.06 us
    pallas_call x1, Pallas kernels, own_part(): pl.pallas_call(own_kernel, in_specs=[SMEM] * 4 + [HBM] * 2, out_specs=[VM...  5.48 us
    pallas_call x1, Pallas kernels, pack(): pl.pallas_call(pack_kernel, in_specs=[VMEM, HBM], out_specs=[VMEM] * 4, o...  3.99 us
  transfers between devices with their start and end apart: 10, of which 3 were waited for; matrix products, arithmetic and copies ran while one was open for 2% of the time, Pallas kernels for 16%

profile of v2, /device:TPU:1, one launch (start us, length us, event | category | flops | bytes accessed | tf_op | source)
XLA Modules:
  0.0 96.6 jit_solution(1922840546566436118)
XLA Ops:
  0.6 0.0 copy-start.1
  0.6 0.7 copy-done.1
  1.3 4.0 %pack.1 = (bf16[256,512]{1,0:T(8,128)(2,1)S(1)}, bf16[256,512]{1,0:T(8,128)(2,1)S(1)}, bf16[256,512]{1,0:T(8,128)(2,1)S(1)}, bf16[256,512]{1,0:T(8,128)(2,1)S(1)}) custom-call(s32[4,256]{1,0:T(4,128)S(1)} %bitcast.10, bf16[4096,512]{1,0:T(8,128)(2,1)} %feats.1), custom_call_target="tpu_custom_call" | custom-call | flops 3000000000 | bytes 9000000 | tf_op jit(solution)/shard_map/pack/pallas_call | solution.py:71
  5.3 6.0 %collective-permute-start = (bf16[256,512]{1,0:T(8,128)(2,1)S(1)}, bf16[256,512]{1,0:T(8,128)(2,1)S(1)}, u32[]{:S(2)}, u32[]{:S(2)}) collective-permute-start(bf16[256,512]{1,0:T(8,128)(2,1)S(1)} %get-tuple-element.31), channel_id=1, source_target_pairs={{0,8},{8,16},{16,24},{24,32},{32,40},{40,48},{48,56},{56,64},{64,7... | collective-permute-start | bytes 786440 | tf_op jit(solution)/shard_map/ppermute | solution.py:362
  11.4 1.9 %collective-permute-start.1 = (bf16[256,512]{1,0:T(8,128)(2,1)S(1)}, bf16[256,512]{1,0:T(8,128)(2,1)S(1)}, u32[]{:S(2)}, u32[]{:S(2)}) collective-permute-start(bf16[256,512]{1,0:T(8,128)(2,1)S(1)} %get-tuple-element.32), channel_id=1, source_target_pairs={{8,0},{16,8},{24,16},{32,24},{40,32},{48,40},{56,48},{64,56},{72,6... | collective-permute-start | bytes 786440 | tf_op jit(solution)/shard_map/ppermute | solution.py:362
  13.3 2.2 %collective-permute-start.2 = (bf16[256,512]{1,0:T(8,128)(2,1)S(1)}, bf16[256,512]{1,0:T(8,128)(2,1)S(1)}, u32[]{:S(2)}, u32[]{:S(2)}) collective-permute-start(bf16[256,512]{1,0:T(8,128)(2,1)S(1)} %get-tuple-element.33), channel_id=1, source_target_pairs={{0,1},{1,2},{2,3},{3,4},{4,5},{5,6},{6,7},{8,9},{9,10},{10,11},{11... | collective-permute-start | bytes 786440 | tf_op jit(solution)/shard_map/ppermute | solution.py:362
  15.5 1.3 %collective-permute-start.3 = (bf16[256,512]{1,0:T(8,128)(2,1)S(1)}, bf16[256,512]{1,0:T(8,128)(2,1)S(1)}, u32[]{:S(2)}, u32[]{:S(2)}) collective-permute-start(bf16[256,512]{1,0:T(8,128)(2,1)S(1)} %get-tuple-element.34), channel_id=1, source_target_pairs={{1,0},{2,1},{3,2},{4,3},{5,4},{6,5},{7,6},{9,8},{10,9},{11,10},{12... | collective-permute-start | bytes 786440 | tf_op jit(solution)/shard_map/ppermute | solution.py:362
  18.2 0.0 copy-start.3
  18.2 5.5 %own_part.1 = (f32[4224,512]{1,0:T(8,128)S(1)}, bf16[96,128,128]{2,1,0:T(8,128)(2,1)S(1)}) custom-call(s32[1,96]{1,0:T(1,128)S(1)} %copy-done.4, s32[1,96]{1,0:T(1,128)S(1)} %copy-done.5, s32[1]{0:T(128)S(6)} %copy.16.count, s32[1]{0:T(128)S(6)} %copy.17.nodes, bf16[4096,512]{1,0:T(8,128)(2,1)} %feats.1, bf16[96,128,128]{2,1,0:T(8,128)(2,1)} %adj_in.1), custom_call_target="tpu_custom_call" | custom-call | flops 8000000000 | bytes 24000000 | tf_op jit(solution)/shard_map/own_part/pallas_call | solution.py:148
  23.7 3.5 %collective-permute-done.3.h3 = bf16[256,512]{1,0:T(8,128)(2,1)S(1)} collective-permute-done((bf16[256,512]{1,0:T(8,128)(2,1)S(1)}, bf16[256,512]{1,0:T(8,128)(2,1)S(1)}, u32[]{:S(2)}, u32[]{:S(2)}) %collective-permute-start.3) | collective-permute-done | bytes 262176 | tf_op jit(solution)/shard_map/ppermute | solution.py:362
  27.3 15.2 %dense_part.1 = (f32[4224,512]{1,0:T(8,128)S(1)}, bf16[4096,512]{1,0:T(8,128)(2,1)}, bf16[4096,512]{1,0:T(8,128)(2,1)}, bf16[256,512]{1,0:T(8,128)(2,1)S(1)}, bf...) custom-call(s32[1,96]{1,0:T(1,128)S(1)} %copy-done.4, ...), custom_call_target="tpu_custom_call", output_to_operand_aliasing={{0}: (4, {})} | custom-call | flops 16000000000 | bytes 48000000 | tf_op jit(solution)/shard_map/dense_part/pallas_call | solution.py:250
  42.4 13.7 %all-to-all-start = ((bf16[128,24,128]{2,1,0:T(8,128)(2,1)}), bf16[128,24,128]{2,1,0:T(8,128)(2,1)S(1)}, u32[]{:S(2)}, u32[]{:S(2)}) async-start(bf16[128,24,128]{2,1,0:T(8,128)(2,1)} %get-tuple-element.37), calls=%async_computation | async-start | bytes 1572864 | tf_op jit(solution)/shard_map/all_to_all | solution.py:378
  56.1 5.0 %collective-permute-start.4 = (bf16[256,512]{1,0:T(8,128)(2,1)S(1)}, bf16[256,512]{1,0:T(8,128)(2,1)S(1)}, u32[]{:S(2)}, u32[]{:S(2)}) collective-permute-start(bf16[256,512]{1,0:T(8,128)(2,1)S(1)} %get-tuple-element.39), channel_id=1, source_target_pairs={{0,8},{8,16},{16,24},{24,32},{32,40},{40,48},{48,56},{56,64},{64,7... | collective-permute-start | bytes 786440 | tf_op jit(solution)/shard_map/ppermute | solution.py:362
  61.2 1.9 %collective-permute-start.5 = (bf16[256,512]{1,0:T(8,128)(2,1)S(1)}, bf16[256,512]{1,0:T(8,128)(2,1)S(1)}, u32[]{:S(2)}, u32[]{:S(2)}) collective-permute-start(bf16[256,512]{1,0:T(8,128)(2,1)S(1)} %get-tuple-element.40), channel_id=1, source_target_pairs={{8,0},{16,8},{24,16},{32,24},{40,32},{48,40},{56,48},{64,56},{72,6... | collective-permute-start | bytes 786440 | tf_op jit(solution)/shard_map/ppermute | solution.py:362
  63.1 2.2 %collective-permute-start.6 = (bf16[256,512]{1,0:T(8,128)(2,1)S(1)}, bf16[256,512]{1,0:T(8,128)(2,1)S(1)}, u32[]{:S(2)}, u32[]{:S(2)}) collective-permute-start(bf16[256,512]{1,0:T(8,128)(2,1)S(1)} %get-tuple-element.41), channel_id=1, source_target_pairs={{0,1},{1,2},{2,3},{3,4},{4,5},{5,6},{6,7},{8,9},{9,10},{10,11},{11... | collective-permute-start | bytes 786440 | tf_op jit(solution)/shard_map/ppermute | solution.py:362
  65.3 1.3 %collective-permute-start.7 = (bf16[256,512]{1,0:T(8,128)(2,1)S(1)}, bf16[256,512]{1,0:T(8,128)(2,1)S(1)}, u32[]{:S(2)}, u32[]{:S(2)}) collective-permute-start(bf16[256,512]{1,0:T(8,128)(2,1)S(1)} %get-tuple-element.42), channel_id=1, source_target_pairs={{1,0},{2,1},{3,2},{4,3},{5,4},{6,5},{7,6},{9,8},{10,9},{11,10},{12... | collective-permute-start | bytes 786440 | tf_op jit(solution)/shard_map/ppermute | solution.py:362
  66.6 6.1 %all-to-all-done = bf16[128,24,128]{2,1,0:T(8,128)(2,1)S(1)} async-done(((bf16[128,24,128]{2,1,0:T(8,128)(2,1)}), bf16[128,24,128]{2,1,0:T(8,128)(2,1)S(1)}, u32[]{:S(2)}, u32[]{:S(2)}) %all-to-all-start) | async-done | bytes 786464 | tf_op jit(solution)/shard_map/all_to_all | solution.py:378
  72.7 0.2 convert_reduce_fusion
  72.9 0.9 broadcast_in_dim.2
  73.7 8.0 %all-to-all-start.1 = ((bf16[128,16,128]{2,1,0:T(8,128)(2,1)}), bf16[128,16,128]{2,1,0:T(8,128)(2,1)S(1)}, u32[]{:S(2)}, u32[]{:S(2)}) async-start(bf16[128,16,128]{2,1,0:T(8,128)(2,1)} %broadcast_in_dim.2), calls=%async_computation.1 | async-start | bytes 1048576 | tf_op jit(solution)/shard_map/all_to_all | solution.py:384
  81.8 9.9 %back_part.1 = bf16[4096,512]{1,0:T(8,128)(2,1)} custom-call(s32[1,96]{1,0:T(1,128)S(1)} %copy-done.4, s32[1,96]{1,0:T(1,128)S(1)} %copy-done.5, s32[1]{0:T(128)S(6)} %copy.16.count, s32[1]{0:T(128)S(6)} %copy.17.nodes, bf16[96,128,128]{2,1,0:T(8,128)(2,1)} %adj_in.1, bf16[4096,512]{1,0:T(8,128)(2,1)} %get-tuple-element.36.back_in, s32[4,256]{1,0:T(4,128)S(1)} %bitcast.11, ...), custom_call_target="tpu_custom_call" | custom-call | flops 12000000000 | bytes 36000000 | tf_op jit(solution)/shard_map/back_part/pallas_call | solution.py:334
  91.7 0.6 fusion
  92.3 3.2 %all-to-all-done.1 = bf16[128,16,128]{2,1,0:T(8,128)(2,1)S(1)} async-done(((bf16[128,16,128]{2,1,0:T(8,128)(2,1)}), bf16[128,16,128]{2,1,0:T(8,128)(2,1)S(1)}, u32[]{:S(2)}, u32[]{:S(2)}) %all-to-all-start.1) | async-done | bytes 524320 | tf_op jit(solution)/shard_map/all_to_all | solution.py:384
  95.5 1.1 %convert_bitcast_fusion = f32[512,512]{1,0:T(8,128)} fusion(bf16[64,4,8,128]{3,2,1,0:T(8,128)(2,1)S(1)} %bitcast.13), kind=kLoop, calls=%fused_computation.1 | loop fusion | flops 262144 | bytes 1572864 | tf_op jit(solution)/shard_map/reshape | solution.py:385
  (18 shorter events, 0.1 us)
Async XLA Ops:
  0.6 0.7 copy-start.1
  1.3 16.8 %copy-start.4 = (s32[1,96]{1,0:T(1,128)S(1)}, s32[1,96]{1,0:T(1,128)}, u32[]{:S(2)}) copy-start(s32[1,96]{1,0:T(1,128)} %rows.5) | copy-start | bytes 1156
  1.3 16.8 %copy-start.5 = (s32[1,96]{1,0:T(1,128)S(1)}, s32[1,96]{1,0:T(1,128)}, u32[]{:S(2)}) copy-start(s32[1,96]{1,0:T(1,128)} %cols.5) | copy-start | bytes 1156
  5.3 18.4 %collective-permute-start = (bf16[256,512]{1,0:T(8,128)(2,1)S(1)}, bf16[256,512]{1,0:T(8,128)(2,1)S(1)}, u32[]{:S(2)}, u32[]{:S(2)}) collective-permute-start(bf16[256,512]{1,0:T(8,128)(2,1)S(1)} %get-tuple-element.31), channel_id=1, source_target_pairs={{0,8},{8,16},{16,24},{24,32},{32,40},{40,48},{48,56},{56,64},{64,7... | collective-permute-start | bytes 786440 | tf_op jit(solution)/shard_map/ppermute | solution.py:362
  11.4 12.3 %collective-permute-start.1 = (bf16[256,512]{1,0:T(8,128)(2,1)S(1)}, bf16[256,512]{1,0:T(8,128)(2,1)S(1)}, u32[]{:S(2)}, u32[]{:S(2)}) collective-permute-start(bf16[256,512]{1,0:T(8,128)(2,1)S(1)} %get-tuple-element.32), channel_id=1, source_target_pairs={{8,0},{16,8},{24,16},{32,24},{40,32},{48,40},{56,48},{64,56},{72,6... | collective-permute-start | bytes 786440 | tf_op jit(solution)/shard_map/ppermute | solution.py:362
  13.3 10.4 %collective-permute-start.2 = (bf16[256,512]{1,0:T(8,128)(2,1)S(1)}, bf16[256,512]{1,0:T(8,128)(2,1)S(1)}, u32[]{:S(2)}, u32[]{:S(2)}) collective-permute-start(bf16[256,512]{1,0:T(8,128)(2,1)S(1)} %get-tuple-element.33), channel_id=1, source_target_pairs={{0,1},{1,2},{2,3},{3,4},{4,5},{5,6},{6,7},{8,9},{9,10},{10,11},{11... | collective-permute-start | bytes 786440 | tf_op jit(solution)/shard_map/ppermute | solution.py:362
  15.5 11.7 %collective-permute-start.3 = (bf16[256,512]{1,0:T(8,128)(2,1)S(1)}, bf16[256,512]{1,0:T(8,128)(2,1)S(1)}, u32[]{:S(2)}, u32[]{:S(2)}) collective-permute-start(bf16[256,512]{1,0:T(8,128)(2,1)S(1)} %get-tuple-element.34), channel_id=1, source_target_pairs={{1,0},{2,1},{3,2},{4,3},{5,4},{6,5},{7,6},{9,8},{10,9},{11,10},{12... | collective-permute-start | bytes 786440 | tf_op jit(solution)/shard_map/ppermute | solution.py:362
  18.2 9.1 %copy-start = (bf16[512,512]{1,0:T(8,128)(2,1)S(1)}, bf16[512,512]{1,0:T(8,128)(2,1)}, u32[]{:S(2)}) copy-start(bf16[512,512]{1,0:T(8,128)(2,1)} %weight.1) | copy-start | bytes 1572868
  18.2 9.1 %copy-start.3 = (f32[512]{0:T(512)S(1)}, f32[512]{0:T(512)}, u32[]{:S(2)}) copy-start(f32[512]{0:T(512)} %param.18) | copy-start | bytes 6148
  27.3 54.5 %copy-start.2 = (s32[1,4,256]{2,1,0:T(4,128)S(1)}, s32[1,4,256]{2,1,0:T(4,128)}, u32[]{:S(2)}) copy-start(s32[1,4,256]{2,1,0:T(4,128)} %param.16) | copy-start | bytes 12292
  42.4 30.2 %all-to-all-start = ((bf16[128,24,128]{2,1,0:T(8,128)(2,1)}), bf16[128,24,128]{2,1,0:T(8,128)(2,1)S(1)}, u32[]{:S(2)}, u32[]{:S(2)}) async-start(bf16[128,24,128]{2,1,0:T(8,128)(2,1)} %get-tuple-element.37), calls=%async_computation | async-start | bytes 1572864 | tf_op jit(solution)/shard_map/all_to_all | solution.py:378
  56.1 25.6 %collective-permute-start.4 = (bf16[256,512]{1,0:T(8,128)(2,1)S(1)}, bf16[256,512]{1,0:T(8,128)(2,1)S(1)}, u32[]{:S(2)}, u32[]{:S(2)}) collective-permute-start(bf16[256,512]{1,0:T(8,128)(2,1)S(1)} %get-tuple-element.39), channel_id=1, source_target_pairs={{0,8},{8,16},{16,24},{24,32},{32,40},{40,48},{48,56},{56,64},{64,7... | collective-permute-start | bytes 786440 | tf_op jit(solution)/shard_map/ppermute | solution.py:362
  61.2 20.6 %collective-permute-start.5 = (bf16[256,512]{1,0:T(8,128)(2,1)S(1)}, bf16[256,512]{1,0:T(8,128)(2,1)S(1)}, u32[]{:S(2)}, u32[]{:S(2)}) collective-permute-start(bf16[256,512]{1,0:T(8,128)(2,1)S(1)} %get-tuple-element.40), channel_id=1, source_target_pairs={{8,0},{16,8},{24,16},{32,24},{40,32},{48,40},{56,48},{64,56},{72,6... | collective-permute-start | bytes 786440 | tf_op jit(solution)/shard_map/ppermute | solution.py:362
  63.1 18.6 %collective-permute-start.6 = (bf16[256,512]{1,0:T(8,128)(2,1)S(1)}, bf16[256,512]{1,0:T(8,128)(2,1)S(1)}, u32[]{:S(2)}, u32[]{:S(2)}) collective-permute-start(bf16[256,512]{1,0:T(8,128)(2,1)S(1)} %get-tuple-element.41), channel_id=1, source_target_pairs={{0,1},{1,2},{2,3},{3,4},{4,5},{5,6},{6,7},{8,9},{9,10},{10,11},{11... | collective-permute-start | bytes 786440 | tf_op jit(solution)/shard_map/ppermute | solution.py:362
  65.3 16.4 %collective-permute-start.7 = (bf16[256,512]{1,0:T(8,128)(2,1)S(1)}, bf16[256,512]{1,0:T(8,128)(2,1)S(1)}, u32[]{:S(2)}, u32[]{:S(2)}) collective-permute-start(bf16[256,512]{1,0:T(8,128)(2,1)S(1)} %get-tuple-element.42), channel_id=1, source_target_pairs={{1,0},{2,1},{3,2},{4,3},{5,4},{6,5},{7,6},{9,8},{10,9},{11,10},{12... | collective-permute-start | bytes 786440 | tf_op jit(solution)/shard_map/ppermute | solution.py:362
  73.7 21.7 %all-to-all-start.1 = ((bf16[128,16,128]{2,1,0:T(8,128)(2,1)}), bf16[128,16,128]{2,1,0:T(8,128)(2,1)S(1)}, u32[]{:S(2)}, u32[]{:S(2)}) async-start(bf16[128,16,128]{2,1,0:T(8,128)(2,1)} %broadcast_in_dim.2), calls=%async_computation.1 | async-start | bytes 1048576 | tf_op jit(solution)/shard_map/all_to_all | solution.py:384

commit v3 on v2

--- a/solution.py
+++ b/solution.py
@@ -18,6 +18,7 @@
 CHUNK = 1024
 PEERS = 128
 UNROLL = 16
+FEW = 8
 BF = jnp.bfloat16
 F32 = jnp.float32
 VMEM_BYTES = 24 * 1024 * 1024
@@ -44,15 +45,26 @@
     return pltpu.with_memory_space_constraint(x, pltpu.HBM)
 
 
+def flips():
+    return 1 - (lax.axis_index("wide") & 1), 1 - (lax.axis_index("narrow") & 1)
+
+
+def pick_row(picks, k, flip):
+    return picks[pl.ds((k & 2) + ((k & 1) ^ flip[k // 2]), 1), :]
+
+
 def pack_kernel(picks, feats_in, out0, out1, out2, out3, onehot, feats, sem):
     outs = (out0, out1, out2, out3)
     load = pltpu.make_async_copy(feats_in.at[pl.ds(0, HALF)], feats, sem.at[0])
     load.start()
     lane = lax.broadcasted_iota(jnp.int32, (BS, BS), 1)
 
+    flip = flips()
+
     def build(k):
+        line = pick_row(picks, k, flip)
         for h in range(2):
-            row = picks[k : k + 1, h * BS : (h + 1) * BS]
+            row = line[:, h * BS : (h + 1) * BS]
             t = jnp.transpose(jnp.broadcast_to(row.astype(F32), (BS, BS))).astype(jnp.int32)
             for c in range(HALF // BS):
                 hit = jnp.where(t == lane + c * BS, F32(1.0), F32(0.0)).astype(BF)
@@ -102,17 +114,20 @@
         ref[pl.ds(pl.multiple_of(r * BS, BS), BS), :] = jnp.zeros((BS, F), F32)
 
 
-def slot_list(table, rows, cols, live, halo, spare):
+def slot_list(table, rows, cols, live, halo, spare, unroll):
+    flip = flips()
+
     def step(b, n):
         c = cols[0, b]
         take = jnp.logical_and(b < live, (c >= RB) == (halo == 1))
-        table[n] = b + (rows[0, b] << 8) + (c << 16)
+        turn = jnp.where(c < RB, 0, jnp.where(c < RB + 4, flip[0], flip[1]) * 2)
+        table[n] = b + (rows[0, b] << 8) + ((c ^ turn) << 16)
         return n + take.astype(jnp.int32)
 
     n = lax.fori_loop(0, BLK, step, jnp.int32(0))
-    for u in range(UNROLL):
+    for u in range(unroll):
         table[n + u] = jnp.int32(spare)
-    return (n + UNROLL - 1) // UNROLL
+    return (n + unroll - 1) // unroll
 
 
 def unpack(code):
@@ -127,7 +142,7 @@
     for c in loads:
         c.start()
     zero_blocks(acc, RB + 1)
-    groups = slot_list(table, rows, cols, count[0], 0, RB << 8)
+    groups = slot_list(table, rows, cols, count[0], 0, RB << 8, UNROLL)
     for c in loads:
         c.wait()
     tail_mask(ext, nodes[0] // BS, nodes[0])
@@ -163,7 +178,7 @@
 
 def dense_kernel(
     rows, cols, count, nodes, acc_in, adj, h0, h1, h2, h3, weight, bias, grads_in,
-    acc, output, back_out, ret0, ret1, ret2, ret3, terms,
+    acc, output, back_out, ret0, ret1, ret2, ret3, terms, lines_out,
     back, received, spread, grads, outbuf, wacc, bacc, table, gsems, osems,
 ):
     alive = nodes[0]
@@ -175,7 +190,7 @@
 
     for i in range(NODES // CHUNK):
         grad_copy(i).start()
-    groups = slot_list(table, rows, cols, count[0], 1, (RB << 8) + (ECB << 16))
+    groups = slot_list(table, rows, cols, count[0], 1, (RB << 8) + (ECB << 16), FEW)
     zero_blocks(spread, ECB - RB + 1)
     wacc[...] = jnp.zeros_like(wacc)
     bacc[...] = jnp.zeros_like(bacc)
@@ -186,8 +201,8 @@
     @pl.loop(0, groups)
     def _(i):
         prods, targets = [], []
-        for u in range(UNROLL):
-            b, r, c = unpack(table[i * UNROLL + u])
+        for u in range(FEW):
+            b, r, c = unpack(table[i * FEW + u])
             prods.append(jnp.dot(adj[b], block(received, c - RB), preferred_element_type=F32))
             targets.append(r)
         for prod, r in zip(prods, targets):
@@ -224,13 +239,13 @@
     lines = jnp.concatenate(
         [high[:, c * BS : (c + 1) * BS] for c in range(4)] + [low[:, c * BS : (c + 1) * BS] for c in range(4)], 0
     ).astype(BF)
-    terms[:, 16:24, :] = jnp.broadcast_to(lines[None], (PEERS, 8, BS))
+    lines_out[...] = lines
 
     @pl.loop(0, groups)
     def _(i):
         prods, targets = [], []
-        for u in range(UNROLL):
-            b, r, c = unpack(table[i * UNROLL + u])
+        for u in range(FEW):
+            b, r, c = unpack(table[i * FEW + u])
             r = jnp.where(r < RB, r, 0)
             prods.append(
                 lax.dot_general(adj[b], block(back, r), (((0,), (0,)), ((), ())), preferred_element_type=F32)
@@ -250,14 +265,14 @@
     return pl.pallas_call(
         dense_kernel,
         in_specs=[SMEM] * 4 + [VMEM] * 8 + [HBM],
-        out_specs=[VMEM, HBM, HBM] + [VMEM] * 5,
+        out_specs=[VMEM, HBM, HBM] + [VMEM] * 6,
         out_shape=[
             pltpu.VMEM(((RB + 1) * BS, F), F32),
             jax.ShapeDtypeStruct((NODES, F), BF),
             jax.ShapeDtypeStruct((NODES, F), BF),
         ]
         + [jax.ShapeDtypeStruct((HALO, F), BF)] * 4
-        + [jax.ShapeDtypeStruct((PEERS, 24, BS), BF)],
+        + [jax.ShapeDtypeStruct((PEERS, 16, BS), BF), jax.ShapeDtypeStruct((8, BS), BF)],
         input_output_aliases={4: 0},
         scratch_shapes=[
             pltpu.VMEM((NODES, F), BF),
@@ -288,7 +303,7 @@
     for c in loads:
         c.start()
     zero_blocks(spread, RB + 1)
-    groups = slot_list(table, rows, cols, count[0], 0, RB << 16)
+    groups = slot_list(table, rows, cols, count[0], 0, RB << 16, UNROLL)
     for c in loads:
         c.wait()
 
@@ -315,12 +330,15 @@
     top.start()
     line = lax.broadcasted_iota(jnp.int32, (HALO, HALO), 0)
 
+    flip = flips()
+    lines = [pick_row(picks, k, flip) for k in range(4)]
+
     @pl.loop(0, HALF // HALO)
     def _(i):
         at = pl.ds(pl.multiple_of(i * HALO, HALO), HALO)
         got = spread[at, :]
         for k, r in enumerate((r0, r1, r2, r3)):
-            hit = jnp.where(line + i * HALO == picks[k : k + 1, :], F32(1.0), F32(0.0)).astype(BF)
+            hit = jnp.where(line + i * HALO == lines[k], F32(1.0), F32(0.0)).astype(BF)
             got = got + jnp.dot(hit, r[...], preferred_element_type=F32)
         outbuf[at, :] = got.astype(BF)
         pltpu.make_async_copy(outbuf.at[at], input_grad.at[at], sems.at[1]).start()
@@ -351,15 +369,11 @@
 
 
 def exchange(parts):
-    got = []
-    for k in range(4):
+    got = [None] * 4
+    for k in (1, 3, 0, 2):
         axis = AXES[k // 2]
-        count = lax.axis_size(axis)
-        if k % 2 == 0:
-            pairs = [(i, i + 1) for i in range(count - 1)]
-        else:
-            pairs = [(i + 1, i) for i in range(count - 1)]
-        got.append(lax.ppermute(parts[k ^ 1], axis, pairs))
+        pairs = [p for i in range(k % 2, lax.axis_size(axis) - 1, 2) for p in ((i, i + 1), (i + 1, i))]
+        got[k] = lax.ppermute(parts[k], axis, pairs)
     return got
 
 
@@ -370,19 +384,19 @@
     packed, adjacency = lax.optimization_barrier((packed, adjacency))
     acc, adj = own_part(*tables, features, adjacency)
     halos = exchange(packed)
-    output, back, r0, r1, r2, r3, terms = dense_part(
+    output, back, r0, r1, r2, r3, terms, lines = dense_part(
         *tables, acc, adj, halos, weight, bias.reshape(1, F), out_grad
     )
     returned = exchange((r0, r1, r2, r3))
     scale = 1.0 / math.sqrt(NODES * PEERS)
     gathered = lax.all_to_all(terms, AXES, 0, 0, tiled=True).astype(F32)
-    sums = jnp.sum(gathered, 0) * scale
-    share = sums[0:16].astype(BF)
-    bias_grad = (sums[16:20] + sums[20:24]).reshape(F)
-    tiles = jnp.broadcast_to(share[None], (PEERS, 16, BS))
+    share = (jnp.sum(gathered, 0) * scale).astype(BF)
+    tiles = jnp.broadcast_to(jnp.concatenate([share, lines], 0)[None], (PEERS, 24, BS))
     tiles, picks = lax.optimization_barrier((tiles, picks))
     tiles = lax.all_to_all(tiles, AXES, 0, 0, tiled=True)
-    weight_grad = tiles.astype(F32).reshape(64, 4, 8, BS).transpose(0, 2, 1, 3).reshape(F, F)
+    weight_grad = tiles[:, 0:16].astype(F32).reshape(64, 4, 8, BS).transpose(0, 2, 1, 3).reshape(F, F)
+    sums = jnp.sum(tiles[:, 16:24].astype(F32), 0)
+    bias_grad = (sums[0:4] + sums[4:8]).reshape(F) * scale
     input_grad = back_part(*tables, adjacency, back, picks, returned)
     return (output, input_grad, weight_grad, bias_grad)
 

time: 97.4 us -> 98.4 us (1.010)
  starting transfers between devices: 43.6 us -> 36.5 us
  waiting for transfers between devices: 12.8 us -> 17.9 us
  Pallas kernels: 34.6 us -> 37.4 us
    ppermute x8, starting transfers between devices: 21.9 us -> 13.5 us  [exchange(): got[k] = lax.ppermute(parts[k], axis, pairs)]
    all_to_all x1, waiting for transfers between devices: 3.21 us -> 9.31 us  [local(): tiles = lax.all_to_all(tiles, AXES, 0, 0, tiled=True)]
    all_to_all x1, starting transfers between devices: 13.7 us -> 18.1 us  [local(): gathered = lax.all_to_all(terms, AXES, 0, 0, tiled=True).astype(F32)]
    all_to_all x1, starting transfers between devices: 7.99 us -> 4.96 us  [local(): tiles = lax.all_to_all(tiles, AXES, 0, 0, tiled=True)]
    ppermute x8, waiting for transfers between devices: 3.56 us -> 1.18 us  [exchange(): got[k] = lax.ppermute(parts[k], axis, pairs)]
    all_to_all x1, waiting for transfers between devices: 6.06 us -> 7.44 us  [local(): gathered = lax.all_to_all(terms, AXES, 0, 0, tiled=True).astype(F32)]
    pallas_call x1, Pallas kernels: 9.9 us -> 11.3 us  [back_part(): pl.pallas_call(back_kernel, in_specs=[SMEM] * 4 + [HBM] * 2 + [VMEM] * 5,...]
    pallas_call x1, Pallas kernels: 5.48 us -> 6.65 us  [own_part(): pl.pallas_call(own_kernel, in_specs=[SMEM] * 4 + [HBM] * 2, out_specs=[VM...]
  transfers between devices with their start and end apart: 10 -> 10, of which waited for: 3 -> 3; matrix products, arithmetic and copies ran while one was open for 2% -> 1% of each run, Pallas kernels for 16% -> 18%
where the time goes in v3:
time: 98.4 us; the launch traced here: 97.7 us
  Pallas kernels  37.4 us (38%)
  starting transfers between devices  36.5 us (37%)
  waiting for transfers between devices  17.9 us (18%)
  between operations  2.14 us (2%)
  other arithmetic  1.97 us (2%)
  local copies, waits for them, and re-layouts  1.72 us (2%)
    all_to_all x1, starting transfers between devices, local(): gathered = lax.all_to_all(terms, AXES, 0, 0, tiled=True).astype(F32)  18.1 us
    pallas_call x1, Pallas kernels, dense_part(): pl.pallas_call(dense_kernel, in_specs=[SMEM] * 4 + [VMEM] * 8 + [HBM], ou...  15.5 us
    ppermute x8, starting transfers between devices, exchange(): got[k] = lax.ppermute(parts[k], axis, pairs)  13.5 us
    pallas_call x1, Pallas kernels, back_part(): pl.pallas_call(back_kernel, in_specs=[SMEM] * 4 + [HBM] * 2 + [VMEM] * 5,...  11.3 us
    all_to_all x1, waiting for transfers between devices, local(): tiles = lax.all_to_all(tiles, AXES, 0, 0, tiled=True)  9.31 us
    all_to_all x1, waiting for transfers between devices, local(): gathered = lax.all_to_all(terms, AXES, 0, 0, tiled=True).astype(F32)  7.44 us
    pallas_call x1, Pallas kernels, own_part(): pl.pallas_call(own_kernel, in_specs=[SMEM] * 4 + [HBM] * 2, out_specs=[VM...  6.65 us
    all_to_all x1, starting transfers between devices, local(): tiles = lax.all_to_all(tiles, AXES, 0, 0, tiled=True)  4.96 us
  transfers between devices with their start and end apart: 10, of which 3 were waited for; matrix products, arithmetic and copies ran while one was open for 1% of the time, Pallas kernels for 18%

profile of v3, /device:TPU:1, one launch (start us, length us, event | category | flops | bytes accessed | tf_op | source)
XLA Modules:
  0.0 97.7 jit_solution(1236078074740002665)
XLA Ops:
  0.6 0.0 copy-start.1
  0.6 0.7 copy-done.1
  1.3 4.0 %pack.1 = (bf16[256,512]{1,0:T(8,128)(2,1)S(1)}, bf16[256,512]{1,0:T(8,128)(2,1)S(1)}, bf16[256,512]{1,0:T(8,128)(2,1)S(1)}, bf16[256,512]{1,0:T(8,128)(2,1)S(1)}) custom-call(s32[4,256]{1,0:T(4,128)S(1)} %bitcast.10, bf16[4096,512]{1,0:T(8,128)(2,1)} %feats.1), custom_call_target="tpu_custom_call" | custom-call | flops 3000000000 | bytes 9000000 | tf_op jit(solution)/shard_map/pack/pallas_call | solution.py:83
  5.3 1.5 %collective-permute-start = (bf16[256,512]{1,0:T(8,128)(2,1)S(1)}, bf16[256,512]{1,0:T(8,128)(2,1)S(1)}, u32[]{:S(2)}, u32[]{:S(2)}) collective-permute-start(bf16[256,512]{1,0:T(8,128)(2,1)S(1)} %get-tuple-element.32), channel_id=1, source_target_pairs={{0,8},{8,0},{16,24},{24,16},{32,40},{40,32},{48,56},{56,48},{64,72... | collective-permute-start | bytes 786440 | tf_op jit(solution)/shard_map/ppermute | solution.py:376
  6.8 4.6 %collective-permute-start.1 = (bf16[256,512]{1,0:T(8,128)(2,1)S(1)}, bf16[256,512]{1,0:T(8,128)(2,1)S(1)}, u32[]{:S(2)}, u32[]{:S(2)}) collective-permute-start(bf16[256,512]{1,0:T(8,128)(2,1)S(1)} %get-tuple-element.33), channel_id=1, source_target_pairs={{8,16},{16,8},{24,32},{32,24},{40,48},{48,40},{56,64},{64,56},{72,... | collective-permute-start | bytes 786440 | tf_op jit(solution)/shard_map/ppermute | solution.py:376
  11.5 0.4 collective-permute-start.2
  11.9 0.7 collective-permute-start.3
  13.9 6.7 %own_part.1 = (f32[4224,512]{1,0:T(8,128)S(1)}, bf16[96,128,128]{2,1,0:T(8,128)(2,1)S(1)}) custom-call(s32[1,96]{1,0:T(1,128)S(1)} %copy-done.4, s32[1,96]{1,0:T(1,128)S(1)} %copy-done.5, s32[1]{0:T(128)S(6)} %copy.16.count, s32[1]{0:T(128)S(6)} %copy.17.nodes, bf16[4096,512]{1,0:T(8,128)(2,1)} %feats.1, bf16[96,128,128]{2,1,0:T(8,128)(2,1)} %adj_in.1), custom_call_target="tpu_custom_call" | custom-call | flops 8000000000 | bytes 24000000 | tf_op jit(solution)/shard_map/own_part/pallas_call | solution.py:163
  20.6 1.2 %collective-permute-done.2.h2 = bf16[256,512]{1,0:T(8,128)(2,1)S(1)} collective-permute-done((bf16[256,512]{1,0:T(8,128)(2,1)S(1)}, bf16[256,512]{1,0:T(8,128)(2,1)S(1)}, u32[]{:S(2)}, u32[]{:S(2)}) %collective-permute-start.2) | collective-permute-done | bytes 262176 | tf_op jit(solution)/shard_map/ppermute | solution.py:376
  21.7 15.5 %dense_part.1 = (f32[4224,512]{1,0:T(8,128)S(1)}, bf16[4096,512]{1,0:T(8,128)(2,1)}, bf16[4096,512]{1,0:T(8,128)(2,1)}, bf16[256,512]{1,0:T(8,128)(2,1)S(1)}, bf...) custom-call(s32[1,96]{1,0:T(1,128)S(1)} %copy-done.4, ...), custom_call_target="tpu_custom_call", output_to_operand_aliasing={{0}: (4, {})} | custom-call | flops 16000000000 | bytes 48000000 | tf_op jit(solution)/shard_map/dense_part/pallas_call | solution.py:265
  37.3 18.1 %all-to-all-start = ((bf16[128,16,128]{2,1,0:T(8,128)(2,1)}), bf16[128,16,128]{2,1,0:T(8,128)(2,1)S(1)}, u32[]{:S(2)}, u32[]{:S(2)}) async-start(bf16[128,16,128]{2,1,0:T(8,128)(2,1)} %get-tuple-element.38), calls=%async_computation | async-start | bytes 1048576 | tf_op jit(solution)/shard_map/all_to_all | solution.py:392
  55.4 1.1 %collective-permute-start.4 = (bf16[256,512]{1,0:T(8,128)(2,1)S(1)}, bf16[256,512]{1,0:T(8,128)(2,1)S(1)}, u32[]{:S(2)}, u32[]{:S(2)}) collective-permute-start(bf16[256,512]{1,0:T(8,128)(2,1)S(1)} %get-tuple-element.41), channel_id=1, source_target_pairs={{0,8},{8,0},{16,24},{24,16},{32,40},{40,32},{48,56},{56,48},{64,72... | collective-permute-start | bytes 786440 | tf_op jit(solution)/shard_map/ppermute | solution.py:376
  56.5 4.1 %collective-permute-start.5 = (bf16[256,512]{1,0:T(8,128)(2,1)S(1)}, bf16[256,512]{1,0:T(8,128)(2,1)S(1)}, u32[]{:S(2)}, u32[]{:S(2)}) collective-permute-start(bf16[256,512]{1,0:T(8,128)(2,1)S(1)} %get-tuple-element.42), channel_id=1, source_target_pairs={{8,16},{16,8},{24,32},{32,24},{40,48},{48,40},{56,64},{64,56},{72,... | collective-permute-start | bytes 786440 | tf_op jit(solution)/shard_map/ppermute | solution.py:376
  60.6 0.4 collective-permute-start.6
  61.0 0.7 collective-permute-start.7
  61.7 7.4 %all-to-all-done = bf16[128,16,128]{2,1,0:T(8,128)(2,1)S(1)} async-done(((bf16[128,16,128]{2,1,0:T(8,128)(2,1)}), bf16[128,16,128]{2,1,0:T(8,128)(2,1)S(1)}, u32[]{:S(2)}, u32[]{:S(2)}) %all-to-all-start) | async-done | bytes 524320 | tf_op jit(solution)/shard_map/all_to_all | solution.py:392
  69.1 0.1 convert_reduce_fusion
  69.3 1.0 %broadcast_in_dim.2 = bf16[128,24,128]{2,1,0:T(8,128)(2,1)} broadcast(bf16[24,128]{1,0:T(8,128)(2,1)S(1)} %pad_maximum_fusion), dimensions={1,2} | broadcast | bytes 792576 | tf_op jit(solution)/shard_map/broadcast_in_dim | solution.py:394
  70.3 5.0 %all-to-all-start.1 = ((bf16[128,24,128]{2,1,0:T(8,128)(2,1)}), bf16[128,24,128]{2,1,0:T(8,128)(2,1)S(1)}, u32[]{:S(2)}, u32[]{:S(2)}) async-start(bf16[128,24,128]{2,1,0:T(8,128)(2,1)} %broadcast_in_dim.2), calls=%async_computation.1 | async-start | bytes 1572864 | tf_op jit(solution)/shard_map/all_to_all | solution.py:396
  75.3 11.3 %back_part.1 = bf16[4096,512]{1,0:T(8,128)(2,1)} custom-call(s32[1,96]{1,0:T(1,128)S(1)} %copy-done.4, s32[1,96]{1,0:T(1,128)S(1)} %copy-done.5, s32[1]{0:T(128)S(6)} %copy.16.count, s32[1]{0:T(128)S(6)} %copy.17.nodes, bf16[96,128,128]{2,1,0:T(8,128)(2,1)} %adj_in.1, bf16[4096,512]{1,0:T(8,128)(2,1)} %get-tuple-element.37.back_in, s32[4,256]{1,0:T(4,128)S(1)} %bitcast.11, ...), custom_call_target="tpu_custom_call" | custom-call | flops 12000000000 | bytes 36000000 | tf_op jit(solution)/shard_map/back_part/pallas_call | solution.py:352
  86.6 9.3 %all-to-all-done.1 = bf16[128,24,128]{2,1,0:T(8,128)(2,1)S(1)} async-done(((bf16[128,24,128]{2,1,0:T(8,128)(2,1)}), bf16[128,24,128]{2,1,0:T(8,128)(2,1)S(1)}, u32[]{:S(2)}, u32[]{:S(2)}) %all-to-all-start.1) | async-done | bytes 786464 | tf_op jit(solution)/shard_map/all_to_all | solution.py:396
  95.9 0.1 convert_reduce_fusion.1
  96.0 0.6 multiply_bitcast_fusion
  96.6 1.1 %convert_bitcast_fusion = f32[512,512]{1,0:T(8,128)} fusion(bf16[64,4,8,128]{3,2,1,0:T(8,128)(2,1)S(1)} %bitcast.13), kind=kLoop, calls=%fused_computation | loop fusion | flops 262144 | bytes 1572864 | tf_op jit(solution)/shard_map/reshape | solution.py:397
  (20 shorter events, 0.1 us)
Async XLA Ops:
  0.6 0.7 copy-start.1
  1.3 12.5 %copy-start.4 = (s32[1,96]{1,0:T(1,128)S(1)}, s32[1,96]{1,0:T(1,128)}, u32[]{:S(2)}) copy-start(s32[1,96]{1,0:T(1,128)} %rows.5) | copy-start | bytes 1156
  1.3 12.5 %copy-start.5 = (s32[1,96]{1,0:T(1,128)S(1)}, s32[1,96]{1,0:T(1,128)}, u32[]{:S(2)}) copy-start(s32[1,96]{1,0:T(1,128)} %cols.5) | copy-start | bytes 1156
  5.3 15.2 %collective-permute-start = (bf16[256,512]{1,0:T(8,128)(2,1)S(1)}, bf16[256,512]{1,0:T(8,128)(2,1)S(1)}, u32[]{:S(2)}, u32[]{:S(2)}) collective-permute-start(bf16[256,512]{1,0:T(8,128)(2,1)S(1)} %get-tuple-element.32), channel_id=1, source_target_pairs={{0,8},{8,0},{16,24},{24,16},{32,40},{40,32},{48,56},{56,48},{64,72... | collective-permute-start | bytes 786440 | tf_op jit(solution)/shard_map/ppermute | solution.py:376
  6.8 13.7 %collective-permute-start.1 = (bf16[256,512]{1,0:T(8,128)(2,1)S(1)}, bf16[256,512]{1,0:T(8,128)(2,1)S(1)}, u32[]{:S(2)}, u32[]{:S(2)}) collective-permute-start(bf16[256,512]{1,0:T(8,128)(2,1)S(1)} %get-tuple-element.33), channel_id=1, source_target_pairs={{8,16},{16,8},{24,32},{32,24},{40,48},{48,40},{56,64},{64,56},{72,... | collective-permute-start | bytes 786440 | tf_op jit(solution)/shard_map/ppermute | solution.py:376
  11.5 10.2 %collective-permute-start.2 = (bf16[256,512]{1,0:T(8,128)(2,1)S(1)}, bf16[256,512]{1,0:T(8,128)(2,1)S(1)}, u32[]{:S(2)}, u32[]{:S(2)}) collective-permute-start(bf16[256,512]{1,0:T(8,128)(2,1)S(1)} %get-tuple-element.34), channel_id=1, source_target_pairs={{0,1},{1,0},{2,3},{3,2},{4,5},{5,4},{6,7},{7,6},{8,9},{9,8},{10,11... | collective-permute-start | bytes 786440 | tf_op jit(solution)/shard_map/ppermute | solution.py:376
  11.9 9.9 %collective-permute-start.3 = (bf16[256,512]{1,0:T(8,128)(2,1)S(1)}, bf16[256,512]{1,0:T(8,128)(2,1)S(1)}, u32[]{:S(2)}, u32[]{:S(2)}) collective-permute-start(bf16[256,512]{1,0:T(8,128)(2,1)S(1)} %get-tuple-element.35), channel_id=1, source_target_pairs={{1,2},{2,1},{3,4},{4,3},{5,6},{6,5},{9,10},{10,9},{11,12},{12,11},... | collective-permute-start | bytes 786440 | tf_op jit(solution)/shard_map/ppermute | solution.py:376
  13.9 7.9 %copy-start = (bf16[512,512]{1,0:T(8,128)(2,1)S(1)}, bf16[512,512]{1,0:T(8,128)(2,1)}, u32[]{:S(2)}) copy-start(bf16[512,512]{1,0:T(8,128)(2,1)} %weight.1) | copy-start | bytes 1572868
  13.9 7.9 %copy-start.3 = (f32[512]{0:T(512)S(1)}, f32[512]{0:T(512)}, u32[]{:S(2)}) copy-start(f32[512]{0:T(512)} %param.18) | copy-start | bytes 6148
  21.7 53.5 %copy-start.2 = (s32[1,4,256]{2,1,0:T(4,128)S(1)}, s32[1,4,256]{2,1,0:T(4,128)}, u32[]{:S(2)}) copy-start(s32[1,4,256]{2,1,0:T(4,128)} %param.16) | copy-start | bytes 12292
  37.3 31.8 %all-to-all-start = ((bf16[128,16,128]{2,1,0:T(8,128)(2,1)}), bf16[128,16,128]{2,1,0:T(8,128)(2,1)S(1)}, u32[]{:S(2)}, u32[]{:S(2)}) async-start(bf16[128,16,128]{2,1,0:T(8,128)(2,1)} %get-tuple-element.38), calls=%async_computation | async-start | bytes 1048576 | tf_op jit(solution)/shard_map/all_to_all | solution.py:392
  55.4 19.9 %collective-permute-start.4 = (bf16[256,512]{1,0:T(8,128)(2,1)S(1)}, bf16[256,512]{1,0:T(8,128)(2,1)S(1)}, u32[]{:S(2)}, u32[]{:S(2)}) collective-permute-start(bf16[256,512]{1,0:T(8,128)(2,1)S(1)} %get-tuple-element.41), channel_id=1, source_target_pairs={{0,8},{8,0},{16,24},{24,16},{32,40},{40,32},{48,56},{56,48},{64,72... | collective-permute-start | bytes 786440 | tf_op jit(solution)/shard_map/ppermute | solution.py:376
  56.5 18.7 %collective-permute-start.5 = (bf16[256,512]{1,0:T(8,128)(2,1)S(1)}, bf16[256,512]{1,0:T(8,128)(2,1)S(1)}, u32[]{:S(2)}, u32[]{:S(2)}) collective-permute-start(bf16[256,512]{1,0:T(8,128)(2,1)S(1)} %get-tuple-element.42), channel_id=1, source_target_pairs={{8,16},{16,8},{24,32},{32,24},{40,48},{48,40},{56,64},{64,56},{72,... | collective-permute-start | bytes 786440 | tf_op jit(solution)/shard_map/ppermute | solution.py:376
  60.6 14.6 %collective-permute-start.6 = (bf16[256,512]{1,0:T(8,128)(2,1)S(1)}, bf16[256,512]{1,0:T(8,128)(2,1)S(1)}, u32[]{:S(2)}, u32[]{:S(2)}) collective-permute-start(bf16[256,512]{1,0:T(8,128)(2,1)S(1)} %get-tuple-element.43), channel_id=1, source_target_pairs={{0,1},{1,0},{2,3},{3,2},{4,5},{5,4},{6,7},{7,6},{8,9},{9,8},{10,11... | collective-permute-start | bytes 786440 | tf_op jit(solution)/shard_map/ppermute | solution.py:376
  61.0 14.3 %collective-permute-start.7 = (bf16[256,512]{1,0:T(8,128)(2,1)S(1)}, bf16[256,512]{1,0:T(8,128)(2,1)S(1)}, u32[]{:S(2)}, u32[]{:S(2)}) collective-permute-start(bf16[256,512]{1,0:T(8,128)(2,1)S(1)} %get-tuple-element.44), channel_id=1, source_target_pairs={{1,2},{2,1},{3,4},{4,3},{5,6},{6,5},{9,10},{10,9},{11,12},{12,11},... | collective-permute-start | bytes 786440 | tf_op jit(solution)/shard_map/ppermute | solution.py:376
  70.3 25.6 %all-to-all-start.1 = ((bf16[128,24,128]{2,1,0:T(8,128)(2,1)}), bf16[128,24,128]{2,1,0:T(8,128)(2,1)S(1)}, u32[]{:S(2)}, u32[]{:S(2)}) async-start(bf16[128,24,128]{2,1,0:T(8,128)(2,1)} %broadcast_in_dim.2), calls=%async_computation.1 | async-start | bytes 1572864 | tf_op jit(solution)/shard_map/all_to_all | solution.py:396

commit v4 on v3

--- a/solution.py
+++ b/solution.py
@@ -24,7 +24,8 @@
 VMEM_BYTES = 24 * 1024 * 1024
 VMEM_OWN = 20 * 1024 * 1024
 VMEM_DENSE = 36 * 1024 * 1024
-VMEM_BACK = 28 * 1024 * 1024
+VMEM_BACK = 20 * 1024 * 1024
+VMEM_FINISH = 8 * 1024 * 1024
 AXES = ("wide", "narrow")
 
 
@@ -293,12 +294,12 @@
 
 
 def back_kernel(
-    rows, cols, count, nodes, adj_in, back_in, picks, r0, r1, r2, r3, input_grad, adj, back, spread, outbuf, table, sems
+    rows, cols, count, nodes, adj_in, back_in, spread, input_grad, adj, back, outbuf, table, sems
 ):
     alive = nodes[0]
     loads = [
-        pltpu.make_async_copy(adj_in, adj, sems.at[2]),
-        pltpu.make_async_copy(back_in, back, sems.at[3]),
+        pltpu.make_async_copy(adj_in, adj, sems.at[1]),
+        pltpu.make_async_copy(back_in, back, sems.at[2]),
     ]
     for c in loads:
         c.start()
@@ -323,13 +324,36 @@
     @pl.loop(HALF // BS, RB)
     def _(r):
         at = pl.ds(pl.multiple_of(r * BS, BS), BS)
+        to = pl.ds(pl.multiple_of(r * BS - HALF, BS), BS)
         line = lax.broadcasted_iota(jnp.int32, (BS, F), 0) + r * BS
-        outbuf[at, :] = jnp.where(line < alive, spread[at, :], F32(0.0)).astype(BF)
-
-    top = pltpu.make_async_copy(outbuf.at[pl.ds(HALF, HALF)], input_grad.at[pl.ds(HALF, HALF)], sems.at[0])
+        outbuf[to, :] = jnp.where(line < alive, spread[at, :], F32(0.0)).astype(BF)
+
+    top = pltpu.make_async_copy(outbuf, input_grad.at[pl.ds(HALF, HALF)], sems.at[0])
     top.start()
+    top.wait()
+
+
+def back_part(rows, cols, count, nodes, adj, back):
+    return pl.pallas_call(
+        back_kernel,
+        in_specs=[SMEM] * 4 + [HBM] * 2,
+        out_specs=[VMEM, HBM],
+        out_shape=[pltpu.VMEM(((RB + 1) * BS, F), F32), jax.ShapeDtypeStruct((NODES, F), BF)],
+        scratch_shapes=[
+            pltpu.VMEM((BLK, BS, BS), BF),
+            pltpu.VMEM((NODES, F), BF),
+            pltpu.VMEM((HALF, F), BF),
+            pltpu.SMEM((BLK + UNROLL,), jnp.int32),
+            pltpu.SemaphoreType.DMA((3,)),
+        ],
+        compiler_params=pltpu.CompilerParams(vmem_limit_bytes=VMEM_BACK),
+        cost_estimate=cost(9),
+        name="back_part",
+    )(rows, cols, count, nodes, in_hbm(adj), in_hbm(back))
+
+
+def finish_kernel(picks, spread, r0, r1, r2, r3, partial, input_grad, outbuf, sems):
     line = lax.broadcasted_iota(jnp.int32, (HALO, HALO), 0)
-
     flip = flips()
     lines = [pick_row(picks, k, flip) for k in range(4)]
 
@@ -341,31 +365,23 @@
             hit = jnp.where(line + i * HALO == lines[k], F32(1.0), F32(0.0)).astype(BF)
             got = got + jnp.dot(hit, r[...], preferred_element_type=F32)
         outbuf[at, :] = got.astype(BF)
-        pltpu.make_async_copy(outbuf.at[at], input_grad.at[at], sems.at[1]).start()
-
-    low = pl.ds(0, HALF)
-    pltpu.make_async_copy(outbuf.at[low], input_grad.at[low], sems.at[1]).wait()
-    top.wait()
-
-
-def back_part(rows, cols, count, nodes, adj, back, picks, returned):
+        pltpu.make_async_copy(outbuf.at[at], input_grad.at[at], sems.at[0]).start()
+
+    pltpu.make_async_copy(outbuf, input_grad.at[pl.ds(0, HALF)], sems.at[0]).wait()
+
+
+def finish(picks, spread, returned, input_grad):
     return pl.pallas_call(
-        back_kernel,
-        in_specs=[SMEM] * 4 + [HBM] * 2 + [VMEM] * 5,
+        finish_kernel,
+        in_specs=[VMEM] * 6 + [HBM],
         out_specs=HBM,
         out_shape=jax.ShapeDtypeStruct((NODES, F), BF),
-        scratch_shapes=[
-            pltpu.VMEM((BLK, BS, BS), BF),
-            pltpu.VMEM((NODES, F), BF),
-            pltpu.VMEM(((RB + 1) * BS, F), F32),
-            pltpu.VMEM((NODES, F), BF),
-            pltpu.SMEM((BLK + UNROLL,), jnp.int32),
-            pltpu.SemaphoreType.DMA((4,)),
-        ],
-        compiler_params=pltpu.CompilerParams(vmem_limit_bytes=VMEM_BACK),
-        cost_estimate=cost(12),
-        name="back_part",
-    )(rows, cols, count, nodes, in_hbm(adj), in_hbm(back), picks, *returned)
+        input_output_aliases={6: 0},
+        scratch_shapes=[pltpu.VMEM((HALF, F), BF), pltpu.SemaphoreType.DMA((1,))],
+        compiler_params=pltpu.CompilerParams(vmem_limit_bytes=VMEM_FINISH),
+        cost_estimate=cost(4),
+        name="finish",
+    )(picks, held(spread), *returned, input_grad)
 
 
 def exchange(parts):
@@ -392,12 +408,13 @@
     gathered = lax.all_to_all(terms, AXES, 0, 0, tiled=True).astype(F32)
     share = (jnp.sum(gathered, 0) * scale).astype(BF)
     tiles = jnp.broadcast_to(jnp.concatenate([share, lines], 0)[None], (PEERS, 24, BS))
-    tiles, picks = lax.optimization_barrier((tiles, picks))
+    tiles, adjacency = lax.optimization_barrier((tiles, adjacency))
     tiles = lax.all_to_all(tiles, AXES, 0, 0, tiled=True)
     weight_grad = tiles[:, 0:16].astype(F32).reshape(64, 4, 8, BS).transpose(0, 2, 1, 3).reshape(F, F)
     sums = jnp.sum(tiles[:, 16:24].astype(F32), 0)
     bias_grad = (sums[0:4] + sums[4:8]).reshape(F) * scale
-    input_grad = back_part(*tables, adjacency, back, picks, returned)
+    spread, partial_grad = back_part(*tables, adjacency, back)
+    input_grad = finish(picks, spread, returned, partial_grad)
     return (output, input_grad, weight_grad, bias_grad)
 
 

time: 98.4 us -> 98.7 us (level)
  Pallas kernels: 37.4 us -> 38.8 us
  waiting for transfers between devices: 17.9 us -> 16.6 us
    all_to_all x1, waiting for transfers between devices: 9.31 us -> 7.95 us  [local(): tiles = lax.all_to_all(tiles, AXES, 0, 0, tiled=True)]
    pallas_call x1 -> x2, Pallas kernels: 11.3 us -> 12.6 us  [the longest x1 8.33 us: back_part(): pl.pallas_call(back_kernel, in_specs=[SMEM] * 4 + [HBM] * 2, out_specs=[V...]
  transfers between devices with their start and end apart: 10 -> 10, of which waited for: 3 -> 3; matrix products, arithmetic and copies ran while one was open for 1% -> 1% of each run, Pallas kernels for 18% -> 20%
where the time goes in v4:
time: 98.7 us; the launch traced here: 98.1 us
  Pallas kernels  38.8 us (39%)
  starting transfers between devices  37 us (37%)
  waiting for transfers between devices  16.6 us (17%)
  between operations  2.15 us (2%)
  other arithmetic  1.97 us (2%)
  local copies, waits for them, and re-layouts  1.72 us (2%)
    all_to_all x1, starting transfers between devices, local(): gathered = lax.all_to_all(terms, AXES, 0, 0, tiled=True).astype(F32)  18.5 us
    pallas_call x1, Pallas kernels, dense_part(): pl.pallas_call(dense_kernel, in_specs=[SMEM] * 4 + [VMEM] * 8 + [HBM], ou...  15.5 us
    ppermute x8, starting transfers between devices, exchange(): got[k] = lax.ppermute(parts[k], axis, pairs)  13.5 us
    pallas_call x1, Pallas kernels, back_part(): pl.pallas_call(back_kernel, in_specs=[SMEM] * 4 + [HBM] * 2, out_specs=[V...  8.33 us
    all_to_all x1, waiting for transfers between devices, local(): tiles = lax.all_to_all(tiles, AXES, 0, 0, tiled=True)  7.95 us
    all_to_all x1, waiting for transfers between devices, local(): gathered = lax.all_to_all(terms, AXES, 0, 0, tiled=True).astype(F32)  7.44 us
    pallas_call x1, Pallas kernels, own_part(): pl.pallas_call(own_kernel, in_specs=[SMEM] * 4 + [HBM] * 2, out_specs=[VM...  6.65 us
    all_to_all x1, starting transfers between devices, local(): tiles = lax.all_to_all(tiles, AXES, 0, 0, tiled=True)  4.96 us
  transfers between devices with their start and end apart: 10, of which 3 were waited for; matrix products, arithmetic and copies ran while one was open for 1% of the time, Pallas kernels for 20%

profile of v4, /device:TPU:1, one launch (start us, length us, event | category | flops | bytes accessed | tf_op | source)
XLA Modules:
  0.0 98.1 jit_solution(5593758468683944057)
XLA Ops:
  0.6 0.7 copy-done
  1.3 4.0 %pack.1 = (bf16[256,512]{1,0:T(8,128)(2,1)S(1)}, bf16[256,512]{1,0:T(8,128)(2,1)S(1)}, bf16[256,512]{1,0:T(8,128)(2,1)S(1)}, bf16[256,512]{1,0:T(8,128)(2,1)S(1)}) custom-call(s32[4,256]{1,0:T(4,128)S(1)} %bitcast.10, bf16[4096,512]{1,0:T(8,128)(2,1)} %feats.1), custom_call_target="tpu_custom_call" | custom-call | flops 3000000000 | bytes 9000000 | tf_op jit(solution)/shard_map/pack/pallas_call | solution.py:84
  5.3 1.5 %collective-permute-start = (bf16[256,512]{1,0:T(8,128)(2,1)S(1)}, bf16[256,512]{1,0:T(8,128)(2,1)S(1)}, u32[]{:S(2)}, u32[]{:S(2)}) collective-permute-start(bf16[256,512]{1,0:T(8,128)(2,1)S(1)} %get-tuple-element.34), channel_id=1, source_target_pairs={{0,8},{8,0},{16,24},{24,16},{32,40},{40,32},{48,56},{56,48},{64,72... | collective-permute-start | bytes 786440 | tf_op jit(solution)/shard_map/ppermute | solution.py:392
  6.8 4.6 %collective-permute-start.1 = (bf16[256,512]{1,0:T(8,128)(2,1)S(1)}, bf16[256,512]{1,0:T(8,128)(2,1)S(1)}, u32[]{:S(2)}, u32[]{:S(2)}) collective-permute-start(bf16[256,512]{1,0:T(8,128)(2,1)S(1)} %get-tuple-element.35), channel_id=1, source_target_pairs={{8,16},{16,8},{24,32},{32,24},{40,48},{48,40},{56,64},{64,56},{72,... | collective-permute-start | bytes 786440 | tf_op jit(solution)/shard_map/ppermute | solution.py:392
  11.5 0.4 collective-permute-start.2
  11.9 0.7 collective-permute-start.3
  13.9 6.7 %own_part.1 = (f32[4224,512]{1,0:T(8,128)S(1)}, bf16[96,128,128]{2,1,0:T(8,128)(2,1)S(1)}) custom-call(s32[1,96]{1,0:T(1,128)S(1)} %copy-done.4, s32[1,96]{1,0:T(1,128)S(1)} %copy-done.5, s32[1]{0:T(128)S(6)} %copy.18.count, s32[1]{0:T(128)S(6)} %copy.19.nodes, bf16[4096,512]{1,0:T(8,128)(2,1)} %feats.1, bf16[96,128,128]{2,1,0:T(8,128)(2,1)} %adj_in.1), custom_call_target="tpu_custom_call" | custom-call | flops 8000000000 | bytes 24000000 | tf_op jit(solution)/shard_map/own_part/pallas_call | solution.py:164
  20.6 1.2 %collective-permute-done.2.h2 = bf16[256,512]{1,0:T(8,128)(2,1)S(1)} collective-permute-done((bf16[256,512]{1,0:T(8,128)(2,1)S(1)}, bf16[256,512]{1,0:T(8,128)(2,1)S(1)}, u32[]{:S(2)}, u32[]{:S(2)}) %collective-permute-start.2) | collective-permute-done | bytes 262176 | tf_op jit(solution)/shard_map/ppermute | solution.py:392
  21.7 15.5 %dense_part.1 = (f32[4224,512]{1,0:T(8,128)S(1)}, bf16[4096,512]{1,0:T(8,128)(2,1)}, bf16[4096,512]{1,0:T(8,128)(2,1)}, bf16[256,512]{1,0:T(8,128)(2,1)S(1)}, bf...) custom-call(s32[1,96]{1,0:T(1,128)S(1)} %copy-done.4, ...), custom_call_target="tpu_custom_call", output_to_operand_aliasing={{0}: (4, {})} | custom-call | flops 16000000000 | bytes 48000000 | tf_op jit(solution)/shard_map/dense_part/pallas_call | solution.py:266
  37.2 18.5 %all-to-all-start = ((bf16[128,16,128]{2,1,0:T(8,128)(2,1)}), bf16[128,16,128]{2,1,0:T(8,128)(2,1)S(1)}, u32[]{:S(2)}, u32[]{:S(2)}) async-start(bf16[128,16,128]{2,1,0:T(8,128)(2,1)} %get-tuple-element.39), calls=%async_computation | async-start | bytes 1048576 | tf_op jit(solution)/shard_map/all_to_all | solution.py:408
  55.8 1.1 %collective-permute-start.4 = (bf16[256,512]{1,0:T(8,128)(2,1)S(1)}, bf16[256,512]{1,0:T(8,128)(2,1)S(1)}, u32[]{:S(2)}, u32[]{:S(2)}) collective-permute-start(bf16[256,512]{1,0:T(8,128)(2,1)S(1)} %get-tuple-element.44), channel_id=1, source_target_pairs={{0,8},{8,0},{16,24},{24,16},{32,40},{40,32},{48,56},{56,48},{64,72... | collective-permute-start | bytes 786440 | tf_op jit(solution)/shard_map/ppermute | solution.py:392
  56.9 4.1 %collective-permute-start.5 = (bf16[256,512]{1,0:T(8,128)(2,1)S(1)}, bf16[256,512]{1,0:T(8,128)(2,1)S(1)}, u32[]{:S(2)}, u32[]{:S(2)}) collective-permute-start(bf16[256,512]{1,0:T(8,128)(2,1)S(1)} %get-tuple-element.45), channel_id=1, source_target_pairs={{8,16},{16,8},{24,32},{32,24},{40,48},{48,40},{56,64},{64,56},{72,... | collective-permute-start | bytes 786440 | tf_op jit(solution)/shard_map/ppermute | solution.py:392
  61.0 0.4 collective-permute-start.6
  61.4 0.7 collective-permute-start.7
  62.1 7.4 %all-to-all-done = bf16[128,16,128]{2,1,0:T(8,128)(2,1)S(1)} async-done(((bf16[128,16,128]{2,1,0:T(8,128)(2,1)}), bf16[128,16,128]{2,1,0:T(8,128)(2,1)S(1)}, u32[]{:S(2)}, u32[]{:S(2)}) %all-to-all-start) | async-done | bytes 524320 | tf_op jit(solution)/shard_map/all_to_all | solution.py:408
  69.5 0.1 convert_reduce_fusion
  69.7 1.0 %broadcast_in_dim.2 = bf16[128,24,128]{2,1,0:T(8,128)(2,1)} broadcast(bf16[24,128]{1,0:T(8,128)(2,1)S(1)} %pad_maximum_fusion), dimensions={1,2} | broadcast | bytes 792576 | tf_op jit(solution)/shard_map/broadcast_in_dim | solution.py:410
  70.7 5.0 %all-to-all-start.1 = ((bf16[128,24,128]{2,1,0:T(8,128)(2,1)}), bf16[128,24,128]{2,1,0:T(8,128)(2,1)S(1)}, u32[]{:S(2)}, u32[]{:S(2)}) async-start(bf16[128,24,128]{2,1,0:T(8,128)(2,1)} %broadcast_in_dim.2), calls=%async_computation.1 | async-start | bytes 1572864 | tf_op jit(solution)/shard_map/all_to_all | solution.py:412
  75.6 8.3 %back_part.1 = (f32[4224,512]{1,0:T(8,128)S(1)}, bf16[4096,512]{1,0:T(8,128)(2,1)}) custom-call(s32[1,96]{1,0:T(1,128)S(1)} %copy-done.4, s32[1,96]{1,0:T(1,128)S(1)} %copy-done.5, s32[1]{0:T(128)S(6)} %copy.18.count, s32[1]{0:T(128)S(6)} %copy.19.nodes, bf16[96,128,128]{2,1,0:T(8,128)(2,1)} %adj_in.1, bf16[4096,512]{1,0:T(8,128)(2,1)} %get-tuple-element.42.back_in), custom_call_target="tpu_custom_call" | custom-call | flops 8999999488 | bytes 27000000 | tf_op jit(solution)/shard_map/back_part/pallas_call | solution.py:337
  84.0 4.3 %finish.1 = bf16[4096,512]{1,0:T(8,128)(2,1)} custom-call(s32[4,256]{1,0:T(4,128)S(1)} %bitcast.11, f32[4224,512]{1,0:T(8,128)S(1)} %get-tuple-element.43.spread, bf16[256,512]{1,0:T(8,128)(2,1)S(1)} %collective-permute-done.4.r0, bf16[256,512]{1,0:T(8,128)(2,1)S(1)} %collective-permute-done.5.r1, ...), custom_call_target="tpu_custom_call", output_to_operand_aliasing={{}: (6, {})} | custom-call | flops 4000000000 | bytes 12000000 | tf_op jit(solution)/shard_map/finish/pallas_call | solution.py:374
  88.3 7.9 %all-to-all-done.1 = bf16[128,24,128]{2,1,0:T(8,128)(2,1)S(1)} async-done(((bf16[128,24,128]{2,1,0:T(8,128)(2,1)}), bf16[128,24,128]{2,1,0:T(8,128)(2,1)S(1)}, u32[]{:S(2)}, u32[]{:S(2)}) %all-to-all-start.1) | async-done | bytes 786464 | tf_op jit(solution)/shard_map/all_to_all | solution.py:412
  96.3 0.1 convert_reduce_fusion.1
  96.4 0.6 multiply_bitcast_fusion
  97.0 1.1 %convert_bitcast_fusion = f32[512,512]{1,0:T(8,128)} fusion(bf16[64,4,8,128]{3,2,1,0:T(8,128)(2,1)S(1)} %bitcast.13), kind=kLoop, calls=%fused_computation | loop fusion | flops 262144 | bytes 1572864 | tf_op jit(solution)/shard_map/reshape | solution.py:413
  (21 shorter events, 0.1 us)
Async XLA Ops:
  0.6 0.7 copy-start
  1.3 12.5 %copy-start.4 = (s32[1,96]{1,0:T(1,128)S(1)}, s32[1,96]{1,0:T(1,128)}, u32[]{:S(2)}) copy-start(s32[1,96]{1,0:T(1,128)} %rows.5) | copy-start | bytes 1156
  1.3 12.5 %copy-start.5 = (s32[1,96]{1,0:T(1,128)S(1)}, s32[1,96]{1,0:T(1,128)}, u32[]{:S(2)}) copy-start(s32[1,96]{1,0:T(1,128)} %cols.5) | copy-start | bytes 1156
  5.3 15.2 %collective-permute-start = (bf16[256,512]{1,0:T(8,128)(2,1)S(1)}, bf16[256,512]{1,0:T(8,128)(2,1)S(1)}, u32[]{:S(2)}, u32[]{:S(2)}) collective-permute-start(bf16[256,512]{1,0:T(8,128)(2,1)S(1)} %get-tuple-element.34), channel_id=1, source_target_pairs={{0,8},{8,0},{16,24},{24,16},{32,40},{40,32},{48,56},{56,48},{64,72... | collective-permute-start | bytes 786440 | tf_op jit(solution)/shard_map/ppermute | solution.py:392
  6.8 13.7 %collective-permute-start.1 = (bf16[256,512]{1,0:T(8,128)(2,1)S(1)}, bf16[256,512]{1,0:T(8,128)(2,1)S(1)}, u32[]{:S(2)}, u32[]{:S(2)}) collective-permute-start(bf16[256,512]{1,0:T(8,128)(2,1)S(1)} %get-tuple-element.35), channel_id=1, source_target_pairs={{8,16},{16,8},{24,32},{32,24},{40,48},{48,40},{56,64},{64,56},{72,... | collective-permute-start | bytes 786440 | tf_op jit(solution)/shard_map/ppermute | solution.py:392
  11.5 10.2 %collective-permute-start.2 = (bf16[256,512]{1,0:T(8,128)(2,1)S(1)}, bf16[256,512]{1,0:T(8,128)(2,1)S(1)}, u32[]{:S(2)}, u32[]{:S(2)}) collective-permute-start(bf16[256,512]{1,0:T(8,128)(2,1)S(1)} %get-tuple-element.36), channel_id=1, source_target_pairs={{0,1},{1,0},{2,3},{3,2},{4,5},{5,4},{6,7},{7,6},{8,9},{9,8},{10,11... | collective-permute-start | bytes 786440 | tf_op jit(solution)/shard_map/ppermute | solution.py:392
  11.9 9.9 %collective-permute-start.3 = (bf16[256,512]{1,0:T(8,128)(2,1)S(1)}, bf16[256,512]{1,0:T(8,128)(2,1)S(1)}, u32[]{:S(2)}, u32[]{:S(2)}) collective-permute-start(bf16[256,512]{1,0:T(8,128)(2,1)S(1)} %get-tuple-element.37), channel_id=1, source_target_pairs={{1,2},{2,1},{3,4},{4,3},{5,6},{6,5},{9,10},{10,9},{11,12},{12,11},... | collective-permute-start | bytes 786440 | tf_op jit(solution)/shard_map/ppermute | solution.py:392
  13.9 7.9 %copy-start.2 = (bf16[512,512]{1,0:T(8,128)(2,1)S(1)}, bf16[512,512]{1,0:T(8,128)(2,1)}, u32[]{:S(2)}) copy-start(bf16[512,512]{1,0:T(8,128)(2,1)} %weight.1) | copy-start | bytes 1572868
  13.9 7.9 %copy-start.3 = (f32[512]{0:T(512)S(1)}, f32[512]{0:T(512)}, u32[]{:S(2)}) copy-start(f32[512]{0:T(512)} %param.18) | copy-start | bytes 6148
  37.2 32.3 %all-to-all-start = ((bf16[128,16,128]{2,1,0:T(8,128)(2,1)}), bf16[128,16,128]{2,1,0:T(8,128)(2,1)S(1)}, u32[]{:S(2)}, u32[]{:S(2)}) async-start(bf16[128,16,128]{2,1,0:T(8,128)(2,1)} %get-tuple-element.39), calls=%async_computation | async-start | bytes 1048576 | tf_op jit(solution)/shard_map/all_to_all | solution.py:408
  55.8 28.2 %collective-permute-start.4 = (bf16[256,512]{1,0:T(8,128)(2,1)S(1)}, bf16[256,512]{1,0:T(8,128)(2,1)S(1)}, u32[]{:S(2)}, u32[]{:S(2)}) collective-permute-start(bf16[256,512]{1,0:T(8,128)(2,1)S(1)} %get-tuple-element.44), channel_id=1, source_target_pairs={{0,8},{8,0},{16,24},{24,16},{32,40},{40,32},{48,56},{56,48},{64,72... | collective-permute-start | bytes 786440 | tf_op jit(solution)/shard_map/ppermute | solution.py:392
  56.9 27.1 %collective-permute-start.5 = (bf16[256,512]{1,0:T(8,128)(2,1)S(1)}, bf16[256,512]{1,0:T(8,128)(2,1)S(1)}, u32[]{:S(2)}, u32[]{:S(2)}) collective-permute-start(bf16[256,512]{1,0:T(8,128)(2,1)S(1)} %get-tuple-element.45), channel_id=1, source_target_pairs={{8,16},{16,8},{24,32},{32,24},{40,48},{48,40},{56,64},{64,56},{72,... | collective-permute-start | bytes 786440 | tf_op jit(solution)/shard_map/ppermute | solution.py:392
  61.0 23.0 %collective-permute-start.6 = (bf16[256,512]{1,0:T(8,128)(2,1)S(1)}, bf16[256,512]{1,0:T(8,128)(2,1)S(1)}, u32[]{:S(2)}, u32[]{:S(2)}) collective-permute-start(bf16[256,512]{1,0:T(8,128)(2,1)S(1)} %get-tuple-element.46), channel_id=1, source_target_pairs={{0,1},{1,0},{2,3},{3,2},{4,5},{5,4},{6,7},{7,6},{8,9},{9,8},{10,11... | collective-permute-start | bytes 786440 | tf_op jit(solution)/shard_map/ppermute | solution.py:392
  61.4 22.6 %collective-permute-start.7 = (bf16[256,512]{1,0:T(8,128)(2,1)S(1)}, bf16[256,512]{1,0:T(8,128)(2,1)S(1)}, u32[]{:S(2)}, u32[]{:S(2)}) collective-permute-start(bf16[256,512]{1,0:T(8,128)(2,1)S(1)} %get-tuple-element.47), channel_id=1, source_target_pairs={{1,2},{2,1},{3,4},{4,3},{5,6},{6,5},{9,10},{10,9},{11,12},{12,11},... | collective-permute-start | bytes 786440 | tf_op jit(solution)/shard_map/ppermute | solution.py:392
  70.7 25.6 %all-to-all-start.1 = ((bf16[128,24,128]{2,1,0:T(8,128)(2,1)}), bf16[128,24,128]{2,1,0:T(8,128)(2,1)S(1)}, u32[]{:S(2)}, u32[]{:S(2)}) async-start(bf16[128,24,128]{2,1,0:T(8,128)(2,1)} %broadcast_in_dim.2), calls=%async_computation.1 | async-start | bytes 1572864 | tf_op jit(solution)/shard_map/all_to_all | solution.py:412
  75.6 8.4 %copy-start.1 = (s32[1,4,256]{2,1,0:T(4,128)S(1)}, s32[1,4,256]{2,1,0:T(4,128)}, u32[]{:S(2)}) copy-start(s32[1,4,256]{2,1,0:T(4,128)} %param.16) | copy-start | bytes 12292

commit v5 on v4

--- a/solution.py
+++ b/solution.py
@@ -16,7 +16,8 @@
 BLK = 96
 HALF = 2048
 CHUNK = 1024
-PEERS = 128
+DEVICES = 128
+PEERS = 64
 UNROLL = 16
 FEW = 8
 BF = jnp.bfloat16
@@ -26,7 +27,10 @@
 VMEM_DENSE = 36 * 1024 * 1024
 VMEM_BACK = 20 * 1024 * 1024
 VMEM_FINISH = 8 * 1024 * 1024
-AXES = ("wide", "narrow")
+WIDE = ("far", "core")
+AXES = ("far", "core", "narrow")
+CHIPS = ("far", "narrow")
+SIDES = (WIDE, "narrow")
 
 
 SMEM = pl.BlockSpec(memory_space=pltpu.SMEM)
@@ -47,7 +51,7 @@
 
 
 def flips():
-    return 1 - (lax.axis_index("wide") & 1), 1 - (lax.axis_index("narrow") & 1)
+    return 1 - lax.axis_index("core"), 1 - (lax.axis_index("narrow") & 1)
 
 
 def pick_row(picks, k, flip):
@@ -179,7 +183,7 @@
 
 def dense_kernel(
     rows, cols, count, nodes, acc_in, adj, h0, h1, h2, h3, weight, bias, grads_in,
-    acc, output, back_out, ret0, ret1, ret2, ret3, terms, lines_out,
+    acc, output, back_out, ret0, ret1, ret2, ret3, mine, give, lines_out,
     back, received, spread, grads, outbuf, wacc, bacc, table, gsems, osems,
 ):
     alive = nodes[0]
@@ -230,10 +234,13 @@
         ).astype(BF)
         pltpu.make_async_copy(back.at[at], back_out.at[at], osems.at[1]).start()
 
-    for p in range(PEERS):
-        for t in range(2):
-            a, c = p // 2, p % 2 * 2 + t
-            terms[p, 8 * t : 8 * t + 8, :] = wacc[a * 8 : (a + 1) * 8, c * BS : (c + 1) * BS].astype(BF)
+    core = lax.axis_index("core")
+    for out, half, kind in ((mine, core, F32), (give, 1 - core, BF)):
+        for p in range(PEERS):
+            for t in range(2):
+                a, c = p // 2, p % 2 * 2 + t
+                tile = wacc[pl.ds(pl.multiple_of(half * (F // 2) + a * 8, 8), 8), c * BS : (c + 1) * BS]
+                out[p, 8 * t : 8 * t + 8, :] = tile.astype(kind)
     total = jnp.sum(bacc[...], 0, keepdims=True)
     high = total.astype(BF).astype(F32)
     low = total - high
@@ -241,6 +248,7 @@
         [high[:, c * BS : (c + 1) * BS] for c in range(4)] + [low[:, c * BS : (c + 1) * BS] for c in range(4)], 0
     ).astype(BF)
     lines_out[...] = lines
+    give[PEERS] = jnp.concatenate([lines, lines], 0)
 
     @pl.loop(0, groups)
     def _(i):
@@ -266,14 +274,17 @@
     return pl.pallas_call(
         dense_kernel,
         in_specs=[SMEM] * 4 + [VMEM] * 8 + [HBM],
-        out_specs=[VMEM, HBM, HBM] + [VMEM] * 6,
+        out_specs=[VMEM, HBM, HBM] + [VMEM] * 7,
         out_shape=[
             pltpu.VMEM(((RB + 1) * BS, F), F32),
             jax.ShapeDtypeStruct((NODES, F), BF),
             jax.ShapeDtypeStruct((NODES, F), BF),
         ]
         + [jax.ShapeDtypeStruct((HALO, F), BF)] * 4
-        + [jax.ShapeDtypeStruct((PEERS, 16, BS), BF), jax.ShapeDtypeStruct((8, BS), BF)],
+        + [jax.ShapeDtypeStruct((PEERS, 16, BS), F32),
+            jax.ShapeDtypeStruct((PEERS + 1, 16, BS), BF),
+            jax.ShapeDtypeStruct((8, BS), BF),
+        ],
         input_output_aliases={4: 0},
         scratch_shapes=[
             pltpu.VMEM((NODES, F), BF),
@@ -384,10 +395,54 @@
     )(picks, held(spread), *returned, input_grad)
 
 
+def pair_kernel(mine, given, lines, pair, both_lines):
+    pair[...] = (mine[...] + given[0:PEERS].astype(F32)).astype(BF)
+    near, far = lines[...].astype(F32), given[PEERS, 0:8, :].astype(F32)
+    both = near[0:4] + near[4:8] + (far[0:4] + far[4:8])
+    high = both.astype(BF).astype(F32)
+    both_lines[...] = jnp.concatenate([high, both - high], 0).astype(BF)
+
+
+def pair_sum(mine, given, lines):
+    return pl.pallas_call(
+        pair_kernel,
+        in_specs=[VMEM] * 3,
+        out_specs=[VMEM] * 2,
+        out_shape=[jax.ShapeDtypeStruct((PEERS, 16, BS), BF), jax.ShapeDtypeStruct((8, BS), BF)],
+        compiler_params=pltpu.CompilerParams(vmem_limit_bytes=VMEM_FINISH),
+        cost_estimate=cost(1),
+        name="pair_sum",
+    )(mine, given, lines)
+
+
+def join_kernel(tiles, other, weight_grad, bias_grad):
+    core = lax.axis_index("core")
+    for half, src in ((core, tiles), (1 - core, other)):
+        for p in range(PEERS):
+            for t in range(2):
+                a, c = p // 2, p % 2 * 2 + t
+                at = pl.ds(pl.multiple_of(half * (F // 2) + a * 8, 8), 8)
+                weight_grad[at, c * BS : (c + 1) * BS] = src[p, 8 * t : 8 * t + 8, :].astype(F32)
+    sums = jnp.sum(tiles[:, 16:24, :].astype(F32), 0)
+    bias_grad[...] = (sums[0:4] + sums[4:8]) * (1.0 / math.sqrt(NODES * DEVICES))
+
+
+def join(tiles, other):
+    return pl.pallas_call(
+        join_kernel,
+        in_specs=[VMEM] * 2,
+        out_specs=[VMEM] * 2,
+        out_shape=[jax.ShapeDtypeStruct((F, F), F32), jax.ShapeDtypeStruct((F // BS, BS), F32)],
+        compiler_params=pltpu.CompilerParams(vmem_limit_bytes=VMEM_FINISH),
+        cost_estimate=cost(1),
+        name="join",
+    )(tiles, other)
+
+
 def exchange(parts):
     got = [None] * 4
     for k in (1, 3, 0, 2):
-        axis = AXES[k // 2]
+        axis = SIDES[k // 2]
         pairs = [p for i in range(k % 2, lax.axis_size(axis) - 1, 2) for p in ((i, i + 1), (i + 1, i))]
         got[k] = lax.ppermute(parts[k], axis, pairs)
     return got
@@ -400,25 +455,29 @@
     packed, adjacency = lax.optimization_barrier((packed, adjacency))
     acc, adj = own_part(*tables, features, adjacency)
     halos = exchange(packed)
-    output, back, r0, r1, r2, r3, terms, lines = dense_part(
+    output, back, r0, r1, r2, r3, mine, give, lines = dense_part(
         *tables, acc, adj, halos, weight, bias.reshape(1, F), out_grad
     )
+    scale = 1.0 / math.sqrt(NODES * DEVICES)
+    swap = [(0, 1), (1, 0)]
+    pair, lines = pair_sum(mine, lax.ppermute(give, "core", swap), lines)
+    pair, r0, r1, r2, r3 = lax.optimization_barrier((pair, r0, r1, r2, r3))
     returned = exchange((r0, r1, r2, r3))
-    scale = 1.0 / math.sqrt(NODES * PEERS)
-    gathered = lax.all_to_all(terms, AXES, 0, 0, tiled=True).astype(F32)
+    gathered = lax.all_to_all(pair, CHIPS, 0, 0, tiled=True).astype(F32)
     share = (jnp.sum(gathered, 0) * scale).astype(BF)
     tiles = jnp.broadcast_to(jnp.concatenate([share, lines], 0)[None], (PEERS, 24, BS))
     tiles, adjacency = lax.optimization_barrier((tiles, adjacency))
-    tiles = lax.all_to_all(tiles, AXES, 0, 0, tiled=True)
-    weight_grad = tiles[:, 0:16].astype(F32).reshape(64, 4, 8, BS).transpose(0, 2, 1, 3).reshape(F, F)
-    sums = jnp.sum(tiles[:, 16:24].astype(F32), 0)
-    bias_grad = (sums[0:4] + sums[4:8]).reshape(F) * scale
+    tiles = lax.all_to_all(tiles, CHIPS, 0, 0, tiled=True)
     spread, partial_grad = back_part(*tables, adjacency, back)
     input_grad = finish(picks, spread, returned, partial_grad)
-    return (output, input_grad, weight_grad, bias_grad)
+    tiles, input_grad = lax.optimization_barrier((tiles, input_grad))
+    weight_grad, bias_grad = join(tiles, lax.ppermute(tiles[:, 0:16], "core", swap))
+    return (output, input_grad, weight_grad, bias_grad.reshape(F))
 
 
 def solution(mesh):
+    wide, narrow = mesh.devices.shape
+    mesh = jax.sharding.Mesh(mesh.devices.reshape(wide // 2, 2, narrow), AXES)
     placed = (
         P(AXES, None),
         P(AXES, None, None),

time: 98.7 us -> 94.4 us (0.956)
  waiting for transfers between devices: 16.6 us -> 7.39 us
  starting transfers between devices: 37 us -> 41.3 us
  Pallas kernels: 38.8 us -> 41.3 us
  other arithmetic: 1.97 us -> 0.08 us
    all_to_all x2, waiting for transfers between devices: 15.4 us -> 4.38 us  [the longest x1 3.53 us: local(): gathered = lax.all_to_all(pair, CHIPS, 0, 0, tiled=True).astype(F32)]
    all_to_all x2, starting transfers between devices: 23.5 us -> 27.4 us  [the longest x1 19.1 us: local(): gathered = lax.all_to_all(pair, CHIPS, 0, 0, tiled=True).astype(F32)]
    ppermute x0 -> x2, waiting for transfers between devices: none -> 2.69 us  [the longest x1 1.53 us: local(): pair, lines = pair_sum(mine, lax.ppermute(give, 'core', swap), lines)]
    pallas_call x0 -> x2, Pallas kernels: none -> 1.81 us  [the longest x1 1.05 us: join(): pl.pallas_call(join_kernel, in_specs=[VMEM] * 2, out_specs=[VMEM] * 2, ou...]
    reshape x1 -> x0, other arithmetic: 1.1 us -> none  [local(): tiles[:, 0:16].astype(F32).reshape(64, 4, 8, BS).transpose(0, 2, 1, 3)]
  transfers between devices with their start and end apart: 10 -> 12, of which waited for: 3 -> 5; matrix products, arithmetic and copies ran while one was open for 1% -> 1% of each run, Pallas kernels for 20% -> 22%
where the time goes in v5:
time: 94.4 us; the launch traced here: 93.8 us
  Pallas kernels  41.3 us (44%)
  starting transfers between devices  41.3 us (44%)
  waiting for transfers between devices  7.39 us (8%)
  between operations  2.16 us (2%)
  local copies, waits for them, and re-layouts  1.52 us (2%)
    all_to_all x1, starting transfers between devices, local(): gathered = lax.all_to_all(pair, CHIPS, 0, 0, tiled=True).astype(F32)  19.1 us
    pallas_call x1, Pallas kernels, dense_part(): pl.pallas_call(dense_kernel, in_specs=[SMEM] * 4 + [VMEM] * 8 + [HBM], ou...  14.6 us
    ppermute x8, starting transfers between devices, exchange(): got[k] = lax.ppermute(parts[k], axis, pairs)  13.3 us
    pallas_call x1, Pallas kernels, back_part(): pl.pallas_call(back_kernel, in_specs=[SMEM] * 4 + [HBM] * 2, out_specs=[V...  9.16 us
    all_to_all x1, starting transfers between devices, local(): tiles = lax.all_to_all(tiles, CHIPS, 0, 0, tiled=True)  8.34 us
    pallas_call x1, Pallas kernels, own_part(): pl.pallas_call(own_kernel, in_specs=[SMEM] * 4 + [HBM] * 2, out_specs=[VM...  7.51 us
    pallas_call x1, Pallas kernels, finish(): pl.pallas_call(finish_kernel, in_specs=[VMEM] * 6 + [HBM], out_specs=HBM,...  4.27 us
    pallas_call x1, Pallas kernels, pack(): pl.pallas_call(pack_kernel, in_specs=[VMEM, HBM], out_specs=[VMEM] * 4, o...  3.99 us
  transfers between devices with their start and end apart: 12, of which 5 were waited for; matrix products, arithmetic and copies ran while one was open for 1% of the time, Pallas kernels for 22%

profile of v5, /device:TPU:1, one launch (start us, length us, event | category | flops | bytes accessed | tf_op | source)
XLA Modules:
  0.0 93.8 jit_solution(2996067404186493350)
XLA Ops:
  0.6 0.7 copy-done
  1.3 4.0 %pack.1 = (bf16[256,512]{1,0:T(8,128)(2,1)S(1)}, bf16[256,512]{1,0:T(8,128)(2,1)S(1)}, bf16[256,512]{1,0:T(8,128)(2,1)S(1)}, bf16[256,512]{1,0:T(8,128)(2,1)S(1)}) custom-call(s32[4,256]{1,0:T(4,128)S(1)} %bitcast.3, bf16[4096,512]{1,0:T(8,128)(2,1)} %feats.1), custom_call_target="tpu_custom_call" | custom-call | flops 3000000000 | bytes 9000000 | tf_op jit(solution)/shard_map/pack/pallas_call | solution.py:88
  5.3 1.5 %collective-permute-start = (bf16[256,512]{1,0:T(8,128)(2,1)S(1)}, bf16[256,512]{1,0:T(8,128)(2,1)S(1)}, u32[]{:S(2)}, u32[]{:S(2)}) collective-permute-start(bf16[256,512]{1,0:T(8,128)(2,1)S(1)} %get-tuple-element.46), channel_id=1, source_target_pairs={{0,8},{8,0},{16,24},{24,16},{32,40},{40,32},{48,56},{56,48},{64,72... | collective-permute-start | bytes 786440 | tf_op jit(solution)/shard_map/ppermute | solution.py:447
  6.8 4.6 %collective-permute-start.1 = (bf16[256,512]{1,0:T(8,128)(2,1)S(1)}, bf16[256,512]{1,0:T(8,128)(2,1)S(1)}, u32[]{:S(2)}, u32[]{:S(2)}) collective-permute-start(bf16[256,512]{1,0:T(8,128)(2,1)S(1)} %get-tuple-element.47), channel_id=1, source_target_pairs={{8,16},{16,8},{24,32},{32,24},{40,48},{48,40},{56,64},{64,56},{72,... | collective-permute-start | bytes 786440 | tf_op jit(solution)/shard_map/ppermute | solution.py:447
  11.5 0.4 collective-permute-start.2
  11.9 0.7 collective-permute-start.3
  13.9 7.5 %own_part.1 = (f32[4224,512]{1,0:T(8,128)S(1)}, bf16[96,128,128]{2,1,0:T(8,128)(2,1)S(1)}) custom-call(s32[1,96]{1,0:T(1,128)S(1)} %copy-done.4, s32[1,96]{1,0:T(1,128)S(1)} %copy-done.5, s32[1]{0:T(128)S(6)} %copy.18.count, s32[1]{0:T(128)S(6)} %copy.19.nodes, bf16[4096,512]{1,0:T(8,128)(2,1)} %feats.1, bf16[96,128,128]{2,1,0:T(8,128)(2,1)} %adj_in.1), custom_call_target="tpu_custom_call" | custom-call | flops 8000000000 | bytes 24000000 | tf_op jit(solution)/shard_map/own_part/pallas_call | solution.py:168
  21.7 14.6 %dense_part.1 = (f32[4224,512]{1,0:T(8,128)S(1)}, bf16[4096,512]{1,0:T(8,128)(2,1)}, bf16[4096,512]{1,0:T(8,128)(2,1)}, bf16[256,512]{1,0:T(8,128)(2,1)S(1)}, bf...) custom-call(s32[1,96]{1,0:T(1,128)S(1)} %copy-done.4, ...), custom_call_target="tpu_custom_call", output_to_operand_aliasing={{0}: (4, {})} | custom-call | flops 16000000000 | bytes 48000000 | tf_op jit(solution)/shard_map/dense_part/pallas_call | solution.py:274
  36.4 1.5 %collective-permute-done.4.given = bf16[65,16,128]{2,1,0:T(8,128)(2,1)S(1)} collective-permute-done((bf16[65,16,128]{2,1,0:T(8,128)(2,1)S(1)}, bf16[65,16,128]{2,1,0:T(8,128)(2,1)S(1)}, u32[]{:S(2)}, u32[]{:S(2)}) %collective-permute-start.4) | collective-permute-done | bytes 266272 | tf_op jit(solution)/shard_map/ppermute | solution.py:463
  37.9 0.8 pair_sum.1
  38.7 19.1 %all-to-all-start = ((bf16[64,16,128]{2,1,0:T(8,128)(2,1)}), bf16[64,16,128]{2,1,0:T(8,128)(2,1)S(1)}, u32[]{:S(2)}, u32[]{:S(2)}) async-start(bf16[64,16,128]{2,1,0:T(8,128)(2,1)} %get-tuple-element.59), calls=%async_computation | async-start | bytes 524288 | tf_op jit(solution)/shard_map/all_to_all | solution.py:466
  57.8 0.5 collective-permute-start.5
  58.3 4.6 %collective-permute-start.6 = (bf16[256,512]{1,0:T(8,128)(2,1)S(1)}, bf16[256,512]{1,0:T(8,128)(2,1)S(1)}, u32[]{:S(2)}, u32[]{:S(2)}) collective-permute-start(bf16[256,512]{1,0:T(8,128)(2,1)S(1)} %get-tuple-element.66), channel_id=1, source_target_pairs={{8,16},{16,8},{24,32},{32,24},{40,48},{48,40},{56,64},{64,56},{72,... | collective-permute-start | bytes 786440 | tf_op jit(solution)/shard_map/ppermute | solution.py:447
  62.9 0.4 collective-permute-start.7
  63.3 0.7 collective-permute-start.8
  63.9 3.5 %all-to-all-done = bf16[64,16,128]{2,1,0:T(8,128)(2,1)S(1)} async-done(((bf16[64,16,128]{2,1,0:T(8,128)(2,1)}), bf16[64,16,128]{2,1,0:T(8,128)(2,1)S(1)}, u32[]{:S(2)}, u32[]{:S(2)}) %all-to-all-start) | async-done | bytes 262176 | tf_op jit(solution)/shard_map/all_to_all | solution.py:466
  67.6 0.8 broadcast_in_dim.2
  68.4 8.3 %all-to-all-start.1 = ((bf16[64,24,128]{2,1,0:T(8,128)(2,1)}), bf16[64,24,128]{2,1,0:T(8,128)(2,1)S(1)}, u32[]{:S(2)}, u32[]{:S(2)}) async-start(bf16[64,24,128]{2,1,0:T(8,128)(2,1)} %broadcast_in_dim.2), calls=%async_computation.1 | async-start | bytes 786432 | tf_op jit(solution)/shard_map/all_to_all | solution.py:470
  76.7 9.2 %back_part.1 = (f32[4224,512]{1,0:T(8,128)S(1)}, bf16[4096,512]{1,0:T(8,128)(2,1)}) custom-call(s32[1,96]{1,0:T(1,128)S(1)} %copy-done.4, s32[1,96]{1,0:T(1,128)S(1)} %copy-done.5, s32[1]{0:T(128)S(6)} %copy.18.count, s32[1]{0:T(128)S(6)} %copy.19.nodes, bf16[96,128,128]{2,1,0:T(8,128)(2,1)} %adj_in.1, bf16[4096,512]{1,0:T(8,128)(2,1)} %get-tuple-element.63.back_in), custom_call_target="tpu_custom_call" | custom-call | flops 8999999488 | bytes 27000000 | tf_op jit(solution)/shard_map/back_part/pallas_call | solution.py:348
  86.0 4.3 %finish.1 = bf16[4096,512]{1,0:T(8,128)(2,1)} custom-call(s32[4,256]{1,0:T(4,128)S(1)} %bitcast.4, f32[4224,512]{1,0:T(8,128)S(1)} %get-tuple-element.64.spread, bf16[256,512]{1,0:T(8,128)(2,1)S(1)} %collective-permute-done.5.r0, bf16[256,512]{1,0:T(8,128)(2,1)S(1)} %collective-permute-done.6.r1, ...), custom_call_target="tpu_custom_call", output_to_operand_aliasing={{}: (6, {})} | custom-call | flops 4000000000 | bytes 12000000 | tf_op jit(solution)/shard_map/finish/pallas_call | solution.py:385
  90.2 0.9 all-to-all-done.1.tiles
  91.1 0.5 collective-permute-start.9
  91.6 1.2 %collective-permute-done.9.other = bf16[64,16,128]{2,1,0:T(8,128)(2,1)S(1)} collective-permute-done((bf16[64,16,128]{2,1,0:T(8,128)(2,1)S(1)}, bf16[64,16,128]{2,1,0:T(8,128)(2,1)S(1)}, u32[]{:S(2)}, u32[]{:S(2)}) %collective-permute-start.9) | collective-permute-done | bytes 262176 | tf_op jit(solution)/shard_map/ppermute | solution.py:474
  92.7 1.0 %join.1 = (f32[512,512]{1,0:T(8,128)}, f32[4,128]{1,0:T(4,128)}) custom-call(bf16[64,24,128]{2,1,0:T(8,128)(2,1)S(1)} %all-to-all-done.1.tiles, bf16[64,16,128]{2,1,0:T(8,128)(2,1)S(1)} %collective-permute-done.9.other), custom_call_target="tpu_custom_call" | custom-call | flops 1000000000 | bytes 3000000 | tf_op jit(solution)/shard_map/join/pallas_call | solution.py:431
  (24 shorter events, 0.5 us)
Async XLA Ops:
  0.6 0.7 copy-start
  1.3 12.5 %copy-start.4 = (s32[1,96]{1,0:T(1,128)S(1)}, s32[1,96]{1,0:T(1,128)}, u32[]{:S(2)}) copy-start(s32[1,96]{1,0:T(1,128)} %rows.5) | copy-start | bytes 1156
  1.3 12.5 %copy-start.5 = (s32[1,96]{1,0:T(1,128)S(1)}, s32[1,96]{1,0:T(1,128)}, u32[]{:S(2)}) copy-start(s32[1,96]{1,0:T(1,128)} %cols.5) | copy-start | bytes 1156
  5.3 16.1 %collective-permute-start = (bf16[256,512]{1,0:T(8,128)(2,1)S(1)}, bf16[256,512]{1,0:T(8,128)(2,1)S(1)}, u32[]{:S(2)}, u32[]{:S(2)}) collective-permute-start(bf16[256,512]{1,0:T(8,128)(2,1)S(1)} %get-tuple-element.46), channel_id=1, source_target_pairs={{0,8},{8,0},{16,24},{24,16},{32,40},{40,32},{48,56},{56,48},{64,72... | collective-permute-start | bytes 786440 | tf_op jit(solution)/shard_map/ppermute | solution.py:447
  6.8 14.6 %collective-permute-start.1 = (bf16[256,512]{1,0:T(8,128)(2,1)S(1)}, bf16[256,512]{1,0:T(8,128)(2,1)S(1)}, u32[]{:S(2)}, u32[]{:S(2)}) collective-permute-start(bf16[256,512]{1,0:T(8,128)(2,1)S(1)} %get-tuple-element.47), channel_id=1, source_target_pairs={{8,16},{16,8},{24,32},{32,24},{40,48},{48,40},{56,64},{64,56},{72,... | collective-permute-start | bytes 786440 | tf_op jit(solution)/shard_map/ppermute | solution.py:447
  11.5 10.2 %collective-permute-start.2 = (bf16[256,512]{1,0:T(8,128)(2,1)S(1)}, bf16[256,512]{1,0:T(8,128)(2,1)S(1)}, u32[]{:S(2)}, u32[]{:S(2)}) collective-permute-start(bf16[256,512]{1,0:T(8,128)(2,1)S(1)} %get-tuple-element.48), channel_id=1, source_target_pairs={{0,1},{1,0},{2,3},{3,2},{4,5},{5,4},{6,7},{7,6},{8,9},{9,8},{10,11... | collective-permute-start | bytes 786440 | tf_op jit(solution)/shard_map/ppermute | solution.py:447
  11.9 9.9 %collective-permute-start.3 = (bf16[256,512]{1,0:T(8,128)(2,1)S(1)}, bf16[256,512]{1,0:T(8,128)(2,1)S(1)}, u32[]{:S(2)}, u32[]{:S(2)}) collective-permute-start(bf16[256,512]{1,0:T(8,128)(2,1)S(1)} %get-tuple-element.49), channel_id=1, source_target_pairs={{1,2},{2,1},{3,4},{4,3},{5,6},{6,5},{9,10},{10,9},{11,12},{12,11},... | collective-permute-start | bytes 786440 | tf_op jit(solution)/shard_map/ppermute | solution.py:447
  13.9 7.9 %copy-start.2 = (bf16[512,512]{1,0:T(8,128)(2,1)S(1)}, bf16[512,512]{1,0:T(8,128)(2,1)}, u32[]{:S(2)}) copy-start(bf16[512,512]{1,0:T(8,128)(2,1)} %weight.1) | copy-start | bytes 1572868
  13.9 7.9 %copy-start.3 = (f32[512]{0:T(512)S(1)}, f32[512]{0:T(512)}, u32[]{:S(2)}) copy-start(f32[512]{0:T(512)} %param.18) | copy-start | bytes 6148
  36.3 1.6 %collective-permute-start.4 = (bf16[65,16,128]{2,1,0:T(8,128)(2,1)S(1)}, bf16[65,16,128]{2,1,0:T(8,128)(2,1)S(1)}, u32[]{:S(2)}, u32[]{:S(2)}) collective-permute-start(bf16[65,16,128]{2,1,0:T(8,128)(2,1)S(1)} %get-tuple-element.52), channel_id=1, source_target_pairs={{0,8},{8,0},{1,9},{9,1},{2,10},{10,2},{3,11},{11,3},{4,12},{12,4},... | collective-permute-start | bytes 798728 | tf_op jit(solution)/shard_map/ppermute | solution.py:463
  38.7 28.8 %all-to-all-start = ((bf16[64,16,128]{2,1,0:T(8,128)(2,1)}), bf16[64,16,128]{2,1,0:T(8,128)(2,1)S(1)}, u32[]{:S(2)}, u32[]{:S(2)}) async-start(bf16[64,16,128]{2,1,0:T(8,128)(2,1)} %get-tuple-element.59), calls=%async_computation | async-start | bytes 524288 | tf_op jit(solution)/shard_map/all_to_all | solution.py:466
  57.8 28.1 %collective-permute-start.5 = (bf16[256,512]{1,0:T(8,128)(2,1)S(1)}, bf16[256,512]{1,0:T(8,128)(2,1)S(1)}, u32[]{:S(2)}, u32[]{:S(2)}) collective-permute-start(bf16[256,512]{1,0:T(8,128)(2,1)S(1)} %get-tuple-element.65), channel_id=1, source_target_pairs={{0,8},{8,0},{16,24},{24,16},{32,40},{40,32},{48,56},{56,48},{64,72... | collective-permute-start | bytes 786440 | tf_op jit(solution)/shard_map/ppermute | solution.py:447
  58.3 27.6 %collective-permute-start.6 = (bf16[256,512]{1,0:T(8,128)(2,1)S(1)}, bf16[256,512]{1,0:T(8,128)(2,1)S(1)}, u32[]{:S(2)}, u32[]{:S(2)}) collective-permute-start(bf16[256,512]{1,0:T(8,128)(2,1)S(1)} %get-tuple-element.66), channel_id=1, source_target_pairs={{8,16},{16,8},{24,32},{32,24},{40,48},{48,40},{56,64},{64,56},{72,... | collective-permute-start | bytes 786440 | tf_op jit(solution)/shard_map/ppermute | solution.py:447
  62.9 23.0 %collective-permute-start.7 = (bf16[256,512]{1,0:T(8,128)(2,1)S(1)}, bf16[256,512]{1,0:T(8,128)(2,1)S(1)}, u32[]{:S(2)}, u32[]{:S(2)}) collective-permute-start(bf16[256,512]{1,0:T(8,128)(2,1)S(1)} %get-tuple-element.67), channel_id=1, source_target_pairs={{0,1},{1,0},{2,3},{3,2},{4,5},{5,4},{6,7},{7,6},{8,9},{9,8},{10,11... | collective-permute-start | bytes 786440 | tf_op jit(solution)/shard_map/ppermute | solution.py:447
  63.3 22.7 %collective-permute-start.8 = (bf16[256,512]{1,0:T(8,128)(2,1)S(1)}, bf16[256,512]{1,0:T(8,128)(2,1)S(1)}, u32[]{:S(2)}, u32[]{:S(2)}) collective-permute-start(bf16[256,512]{1,0:T(8,128)(2,1)S(1)} %get-tuple-element.68), channel_id=1, source_target_pairs={{1,2},{2,1},{3,4},{4,3},{5,6},{6,5},{9,10},{10,9},{11,12},{12,11},... | collective-permute-start | bytes 786440 | tf_op jit(solution)/shard_map/ppermute | solution.py:447
  68.4 22.7 %all-to-all-start.1 = ((bf16[64,24,128]{2,1,0:T(8,128)(2,1)}), bf16[64,24,128]{2,1,0:T(8,128)(2,1)S(1)}, u32[]{:S(2)}, u32[]{:S(2)}) async-start(bf16[64,24,128]{2,1,0:T(8,128)(2,1)} %broadcast_in_dim.2), calls=%async_computation.1 | async-start | bytes 786432 | tf_op jit(solution)/shard_map/all_to_all | solution.py:470
  76.7 9.2 %copy-start.1 = (s32[1,4,256]{2,1,0:T(4,128)S(1)}, s32[1,4,256]{2,1,0:T(4,128)}, u32[]{:S(2)}) copy-start(s32[1,4,256]{2,1,0:T(4,128)} %param.16) | copy-start | bytes 12292
  91.1 1.6 %collective-permute-start.9 = (bf16[64,16,128]{2,1,0:T(8,128)(2,1)S(1)}, bf16[64,16,128]{2,1,0:T(8,128)(2,1)S(1)}, u32[]{:S(2)}, u32[]{:S(2)}) collective-permute-start(bf16[64,16,128]{2,1,0:T(8,128)(2,1)S(1)} %slice.3), channel_id=1, source_target_pairs={{0,8},{8,0},{1,9},{9,1},{2,10},{10,2},{3,11},{11,3},{4,12},{12,4},... | collective-permute-start | bytes 786440 | tf_op jit(solution)/shard_map/ppermute | solution.py:474

commit v6 on v5

--- a/solution.py
+++ b/solution.py
@@ -15,7 +15,9 @@
 ECB = 40
 BLK = 96
 HALF = 2048
-CHUNK = 1024
+GROUP = 8
+EARLY = 2
+LAST = 127
 DEVICES = 128
 PEERS = 64
 UNROLL = 16
@@ -23,8 +25,8 @@
 BF = jnp.bfloat16
 F32 = jnp.float32
 VMEM_BYTES = 24 * 1024 * 1024
-VMEM_OWN = 20 * 1024 * 1024
-VMEM_DENSE = 36 * 1024 * 1024
+VMEM_OWN = 24 * 1024 * 1024
+VMEM_DENSE = 26 * 1024 * 1024
 VMEM_BACK = 20 * 1024 * 1024
 VMEM_FINISH = 8 * 1024 * 1024
 WIDE = ("far", "core")
@@ -119,38 +121,101 @@
         ref[pl.ds(pl.multiple_of(r * BS, BS), BS), :] = jnp.zeros((BS, F), F32)
 
 
-def slot_list(table, rows, cols, live, halo, spare, unroll):
+def slot_lists(table, few, order, flag, rows, cols, live):
     flip = flips()
-
-    def step(b, n):
-        c = cols[0, b]
-        take = jnp.logical_and(b < live, (c >= RB) == (halo == 1))
+    for r in range(RB):
+        flag[r] = jnp.int32(0)
+
+    def step(b, sizes):
+        n, m = sizes
+        r, c = rows[0, b], cols[0, b]
         turn = jnp.where(c < RB, 0, jnp.where(c < RB + 4, flip[0], flip[1]) * 2)
-        table[n] = b + (rows[0, b] << 8) + ((c ^ turn) << 16)
-        return n + take.astype(jnp.int32)
-
-    n = lax.fori_loop(0, BLK, step, jnp.int32(0))
-    for u in range(unroll):
-        table[n + u] = jnp.int32(spare)
-    return (n + unroll - 1) // unroll
+        code = b + (r << 8) + ((c ^ turn) << 16)
+        alive = (b < live).astype(jnp.int32)
+        far = (c >= RB).astype(jnp.int32) * alive
+        table[n] = code
+        few[m] = code
+        flag[r] = flag[r] | far
+        return n + alive - far, m + far
+
+    n, m = lax.fori_loop(0, BLK, step, (jnp.int32(0), jnp.int32(0)), unroll=4)
+    for u in range(UNROLL):
+        table[n + u] = jnp.int32((RB << 8) + (RB << 16))
+    for u in range(FEW):
+        few[m + u] = jnp.int32((RB << 8) + (ECB << 16))
+    table[LAST] = (n + UNROLL - 1) // UNROLL
+    few[LAST] = (m + FEW - 1) // FEW
+    at = jnp.int32(0)
+    for r in range(RB):
+        order[at] = jnp.int32(r)
+        at = at + 1 - flag[r]
+    order[LAST] = jnp.minimum(at // GROUP, EARLY)
+    for r in range(RB):
+        order[at] = jnp.int32(r)
+        at = at + flag[r]
 
 
 def unpack(code):
     return code & 255, (code >> 8) & 255, code >> 16
 
 
-def own_kernel(rows, cols, count, nodes, feats, adj_in, acc, adj, ext, table, sems):
+def group_blocks(order, i):
+    return [order[i * GROUP + j] for j in range(GROUP)]
+
+
+def dense_group(ids, alive, acc, weight, bias, grads, outbuf, back, wacc, bacc, output, back_out, osems):
+    ats = [pl.ds(pl.multiple_of(r * BS, BS), BS) for r in ids]
+    agg = jnp.concatenate([acc[at, :].astype(BF) for at in ats], 0)
+    pre = jnp.dot(agg, weight[...], preferred_element_type=F32) + bias[...]
+    sig = jax.nn.sigmoid(pre)
+    out = pre * sig
+    slope = sig * (1.0 + pre * (1.0 - sig))
+    dpres = []
+    for j, (r, at) in enumerate(zip(ids, ats)):
+        part = slice(j * BS, (j + 1) * BS)
+        keep = lax.broadcasted_iota(jnp.int32, (BS, F), 0) + r * BS < alive
+        outbuf[at, :] = jnp.where(keep, out[part], F32(0.0)).astype(BF)
+        dpres.append(jnp.where(keep, grads[at, :].astype(F32) * slope[part], F32(0.0)).astype(BF))
+    dpre = jnp.concatenate(dpres, 0)
+    bacc[...] += jnp.sum(dpre.astype(F32).reshape(GROUP * BS // 8, 8, F), 0)
+    wacc[...] += lax.dot_general(agg, dpre, (((0,), (0,)), ((), ())), preferred_element_type=F32)
+    got = lax.dot_general(dpre, weight[...], (((1,), (1,)), ((), ())), preferred_element_type=F32).astype(BF)
+    for j, (r, at) in enumerate(zip(ids, ats)):
+        back[at, :] = got[j * BS : (j + 1) * BS]
+    for r, at in zip(ids, ats):
+        pltpu.make_async_copy(outbuf.at[at], output.at[at], osems.at[r]).start()
+        pltpu.make_async_copy(back.at[at], back_out.at[at], osems.at[RB + r]).start()
+
+
+def wait_group(ids, outbuf, back, output, back_out, osems):
+    for r in ids:
+        at = pl.ds(pl.multiple_of(r * BS, BS), BS)
+        pltpu.make_async_copy(outbuf.at[at], output.at[at], osems.at[r]).wait()
+        pltpu.make_async_copy(back.at[at], back_out.at[at], osems.at[RB + r]).wait()
+
+
+def own_kernel(
+    rows, cols, count, nodes, feats, adj_in, weight, bias, grads_in,
+    acc, adj, wacc, bacc, output, back_out, order, few_table, table,
+    ext, grads, outbuf, back, flag, sems, osems,
+):
+    alive = nodes[0]
     loads = [
         pltpu.make_async_copy(adj_in, adj, sems.at[0]),
-        pltpu.make_async_copy(feats, ext, sems.at[1]),
+        pltpu.make_async_copy(feats, ext.at[pl.ds(0, NODES)], sems.at[1]),
     ]
+    late = pltpu.make_async_copy(grads_in, grads, sems.at[2])
     for c in loads:
         c.start()
+    late.start()
     zero_blocks(acc, RB + 1)
-    groups = slot_list(table, rows, cols, count[0], 0, RB << 8, UNROLL)
+    wacc[...] = jnp.zeros_like(wacc)
+    bacc[...] = jnp.zeros_like(bacc)
+    slot_lists(table, few_table, order, flag, rows, cols, count[0])
+    groups, early = table[LAST], order[LAST]
     for c in loads:
         c.wait()
-    tail_mask(ext, nodes[0] // BS, nodes[0])
+    tail_mask(ext, alive // BS, alive)
 
     @pl.loop(0, groups)
     def _(i):
@@ -163,45 +228,64 @@
             at = pl.ds(pl.multiple_of(r * BS, BS), BS)
             acc[at, :] += prod
 
-
-def own_part(rows, cols, count, nodes, features, adjacency):
+    late.wait()
+
+    @pl.loop(0, early)
+    def _(i):
+        ids = group_blocks(order, i)
+        dense_group(ids, alive, acc, weight, bias, grads, outbuf, back, wacc, bacc, output, back_out, osems)
+
+    @pl.loop(0, early)
+    def _(i):
+        wait_group(group_blocks(order, i), outbuf, back, output, back_out, osems)
+
+
+def own_part(rows, cols, count, nodes, features, adjacency, weight, bias, out_grad):
     return pl.pallas_call(
         own_kernel,
-        in_specs=[SMEM] * 4 + [HBM] * 2,
-        out_specs=[VMEM] * 2,
-        out_shape=[pltpu.VMEM(((RB + 1) * BS, F), F32), pltpu.VMEM((BLK, BS, BS), BF)],
+        in_specs=[SMEM] * 4 + [HBM] * 2 + [VMEM] * 2 + [HBM],
+        out_specs=[VMEM] * 4 + [HBM] * 2 + [SMEM] * 3,
+        out_shape=[
+            pltpu.VMEM(((RB + 1) * BS, F), F32),
+            pltpu.VMEM((BLK, BS, BS), BF),
+            pltpu.VMEM((F, F), F32),
+            pltpu.VMEM((8, F), F32),
+            pltpu.HBM((NODES, F), BF),
+            pltpu.HBM((NODES, F), BF),
+            jax.ShapeDtypeStruct((128,), jnp.int32),
+            jax.ShapeDtypeStruct((128,), jnp.int32),
+            jax.ShapeDtypeStruct((128,), jnp.int32),
+        ],
         scratch_shapes=[
+            pltpu.VMEM(((RB + 1) * BS, F), BF),
             pltpu.VMEM((NODES, F), BF),
-            pltpu.SMEM((BLK + UNROLL,), jnp.int32),
-            pltpu.SemaphoreType.DMA((2,)),
+            pltpu.VMEM((NODES, F), BF),
+            pltpu.VMEM((NODES, F), BF),
+            pltpu.SMEM((RB,), jnp.int32),
+            pltpu.SemaphoreType.DMA((3,)),
+            pltpu.SemaphoreType.DMA((2 * RB,)),
         ],
         compiler_params=pltpu.CompilerParams(vmem_limit_bytes=VMEM_OWN),
-        cost_estimate=cost(8),
+        cost_estimate=cost(13),
         name="own_part",
-    )(rows, cols, count, nodes, in_hbm(features), in_hbm(adjacency))
+    )(rows, cols, count, nodes, in_hbm(features), in_hbm(adjacency), weight, bias, in_hbm(out_grad))
 
 
 def dense_kernel(
-    rows, cols, count, nodes, acc_in, adj, h0, h1, h2, h3, weight, bias, grads_in,
+    nodes, order, table, acc_in, adj, wacc_in, bacc_in, h0, h1, h2, h3, weight, bias, grads_in, output_in, back_in,
     acc, output, back_out, ret0, ret1, ret2, ret3, mine, give, lines_out,
-    back, received, spread, grads, outbuf, wacc, bacc, table, gsems, osems,
+    back, received, spread, grads, outbuf, wacc, bacc, gsem, osems,
 ):
     alive = nodes[0]
-    halos = (h0, h1, h2, h3)
-
-    def grad_copy(i):
-        at = pl.ds(pl.multiple_of(i * CHUNK, CHUNK), CHUNK)
-        return pltpu.make_async_copy(grads_in.at[at], grads.at[at], gsems.at[i])
-
-    for i in range(NODES // CHUNK):
-        grad_copy(i).start()
-    groups = slot_list(table, rows, cols, count[0], 1, (RB << 8) + (ECB << 16), FEW)
+    late = pltpu.make_async_copy(grads_in, grads, gsem.at[0])
+    late.start()
+    early = order[LAST]
+    groups = table[LAST]
     zero_blocks(spread, ECB - RB + 1)
-    wacc[...] = jnp.zeros_like(wacc)
-    bacc[...] = jnp.zeros_like(bacc)
-    for k in range(4):
-        hal_at = pl.ds(k * HALO, HALO)
-        received[hal_at, :] = halos[k][...]
+    wacc[...] = wacc_in[...]
+    bacc[...] = bacc_in[...]
+    for k, h in enumerate((h0, h1, h2, h3)):
+        received[pl.ds(k * HALO, HALO), :] = h[...]
 
     @pl.loop(0, groups)
     def _(i):
@@ -214,25 +298,12 @@
             at = pl.ds(pl.multiple_of(r * BS, BS), BS)
             acc[at, :] += prod
 
-    @pl.loop(0, NODES // CHUNK)
-    def _(i):
-        base = pl.multiple_of(i * CHUNK, CHUNK)
-        at = pl.ds(base, CHUNK)
-        grad_copy(i).wait()
-        agg = acc[at, :].astype(BF)
-        pre = jnp.dot(agg, weight[...], preferred_element_type=F32) + bias[...]
-        sig = jax.nn.sigmoid(pre)
-        keep = lax.broadcasted_iota(jnp.int32, (CHUNK, F), 0) + base < alive
-        outbuf[at, :] = jnp.where(keep, pre * sig, F32(0.0)).astype(BF)
-        pltpu.make_async_copy(outbuf.at[at], output.at[at], osems.at[0]).start()
-        g = grads[at, :].astype(F32)
-        dpre = jnp.where(keep, g * sig * (1.0 + pre * (1.0 - sig)), F32(0.0)).astype(BF)
-        bacc[...] += jnp.sum(dpre.astype(F32).reshape(CHUNK // 8, 8, F), 0)
-        wacc[...] += lax.dot_general(agg, dpre, (((0,), (0,)), ((), ())), preferred_element_type=F32)
-        back[at, :] = lax.dot_general(
-            dpre, weight[...], (((1,), (1,)), ((), ())), preferred_element_type=F32
-        ).astype(BF)
-        pltpu.make_async_copy(back.at[at], back_out.at[at], osems.at[1]).start()
+    late.wait()
+
+    @pl.loop(early, RB // GROUP)
+    def _(i):
+        ids = group_blocks(order, i)
+        dense_group(ids, alive, acc, weight, bias, grads, outbuf, back, wacc, bacc, output, back_out, osems)
 
     core = lax.axis_index("core")
     for out, half, kind in ((mine, core, F32), (give, 1 - core, BF)):
@@ -266,26 +337,29 @@
 
     for k, ret in enumerate((ret0, ret1, ret2, ret3)):
         ret[...] = spread[k * HALO : (k + 1) * HALO, :].astype(BF)
-    pltpu.make_async_copy(outbuf, output, osems.at[0]).wait()
-    pltpu.make_async_copy(back, back_out, osems.at[1]).wait()
-
-
-def dense_part(rows, cols, count, nodes, acc, adj, halos, weight, bias, out_grad):
+
+    @pl.loop(early, RB // GROUP)
+    def _(i):
+        wait_group(group_blocks(order, i), outbuf, back, output, back_out, osems)
+
+
+def dense_part(nodes, order, table, acc, adj, wacc, bacc, halos, weight, bias, out_grad, output, back):
     return pl.pallas_call(
         dense_kernel,
-        in_specs=[SMEM] * 4 + [VMEM] * 8 + [HBM],
+        in_specs=[SMEM] * 3 + [VMEM] * 10 + [HBM] * 3,
         out_specs=[VMEM, HBM, HBM] + [VMEM] * 7,
         out_shape=[
             pltpu.VMEM(((RB + 1) * BS, F), F32),
-            jax.ShapeDtypeStruct((NODES, F), BF),
-            jax.ShapeDtypeStruct((NODES, F), BF),
+            pltpu.HBM((NODES, F), BF),
+            pltpu.HBM((NODES, F), BF),
         ]
         + [jax.ShapeDtypeStruct((HALO, F), BF)] * 4
-        + [jax.ShapeDtypeStruct((PEERS, 16, BS), F32),
+        + [
+            jax.ShapeDtypeStruct((PEERS, 16, BS), F32),
             jax.ShapeDtypeStruct((PEERS + 1, 16, BS), BF),
             jax.ShapeDtypeStruct((8, BS), BF),
         ],
-        input_output_aliases={4: 0},
+        input_output_aliases={3: 0, 14: 1, 15: 2},
         scratch_shapes=[
             pltpu.VMEM((NODES, F), BF),
             pltpu.VMEM(((ECB - RB + 1) * BS, F), BF),
@@ -294,28 +368,30 @@
             pltpu.VMEM((NODES, F), BF),
             pltpu.VMEM((F, F), F32),
             pltpu.VMEM((8, F), F32),
-            pltpu.SMEM((BLK + UNROLL,), jnp.int32),
-            pltpu.SemaphoreType.DMA((NODES // CHUNK,)),
-            pltpu.SemaphoreType.DMA((2,)),
+            pltpu.SemaphoreType.DMA((1,)),
+            pltpu.SemaphoreType.DMA((2 * RB,)),
         ],
         compiler_params=pltpu.CompilerParams(vmem_limit_bytes=VMEM_DENSE),
-        cost_estimate=cost(16),
+        cost_estimate=cost(10),
         name="dense_part",
-    )(rows, cols, count, nodes, held(acc), held(adj), *halos, weight, bias, in_hbm(out_grad))[1:]
+    )(
+        nodes, order, table, held(acc), held(adj), held(wacc), held(bacc), *halos,
+        weight, bias, in_hbm(out_grad), in_hbm(output), in_hbm(back),
+    )[1:]
 
 
 def back_kernel(
-    rows, cols, count, nodes, adj_in, back_in, spread, input_grad, adj, back, outbuf, table, sems
+    nodes, table, adj_in, back_in, spread, input_grad, adj, back, outbuf, sems
 ):
     alive = nodes[0]
     loads = [
         pltpu.make_async_copy(adj_in, adj, sems.at[1]),
-        pltpu.make_async_copy(back_in, back, sems.at[2]),
+        pltpu.make_async_copy(back_in, back.at[pl.ds(0, NODES)], sems.at[2]),
     ]
     for c in loads:
         c.start()
     zero_blocks(spread, RB + 1)
-    groups = slot_list(table, rows, cols, count[0], 0, RB << 16, UNROLL)
+    groups = table[LAST]
     for c in loads:
         c.wait()
 
@@ -344,23 +420,22 @@
     top.wait()
 
 
-def back_part(rows, cols, count, nodes, adj, back):
+def back_part(nodes, table, adj, back):
     return pl.pallas_call(
         back_kernel,
-        in_specs=[SMEM] * 4 + [HBM] * 2,
+        in_specs=[SMEM] * 2 + [HBM] * 2,
         out_specs=[VMEM, HBM],
         out_shape=[pltpu.VMEM(((RB + 1) * BS, F), F32), jax.ShapeDtypeStruct((NODES, F), BF)],
         scratch_shapes=[
             pltpu.VMEM((BLK, BS, BS), BF),
-            pltpu.VMEM((NODES, F), BF),
+            pltpu.VMEM(((RB + 1) * BS, F), BF),
             pltpu.VMEM((HALF, F), BF),
-            pltpu.SMEM((BLK + UNROLL,), jnp.int32),
             pltpu.SemaphoreType.DMA((3,)),
         ],
         compiler_params=pltpu.CompilerParams(vmem_limit_bytes=VMEM_BACK),
         cost_estimate=cost(9),
         name="back_part",
-    )(rows, cols, count, nodes, in_hbm(adj), in_hbm(back))
+    )(nodes, table, in_hbm(adj), in_hbm(back))
 
 
 def finish_kernel(picks, spread, r0, r1, r2, r3, partial, input_grad, outbuf, sems):
@@ -453,10 +528,11 @@
     tables = (block_rows, block_cols, block_count, node_count)
     packed = pack(picks, features)
     packed, adjacency = lax.optimization_barrier((packed, adjacency))
-    acc, adj = own_part(*tables, features, adjacency)
+    bias = bias.reshape(1, F)
+    acc, adj, wacc, bacc, output, back, order, few, table = own_part(*tables, features, adjacency, weight, bias, out_grad)
     halos = exchange(packed)
     output, back, r0, r1, r2, r3, mine, give, lines = dense_part(
-        *tables, acc, adj, halos, weight, bias.reshape(1, F), out_grad
+        node_count, order, few, acc, adj, wacc, bacc, halos, weight, bias, out_grad, output, back
     )
     scale = 1.0 / math.sqrt(NODES * DEVICES)
     swap = [(0, 1), (1, 0)]
@@ -468,7 +544,7 @@
     tiles = jnp.broadcast_to(jnp.concatenate([share, lines], 0)[None], (PEERS, 24, BS))
     tiles, adjacency = lax.optimization_barrier((tiles, adjacency))
     tiles = lax.all_to_all(tiles, CHIPS, 0, 0, tiled=True)
-    spread, partial_grad = back_part(*tables, adjacency, back)
+    spread, partial_grad = back_part(node_count, table, adjacency, back)
     input_grad = finish(picks, spread, returned, partial_grad)
     tiles, input_grad = lax.optimization_barrier((tiles, input_grad))
     weight_grad, bias_grad = join(tiles, lax.ppermute(tiles[:, 0:16], "core", swap))

time: 94.4 us -> 91.4 us (0.968)
  starting transfers between devices: 41.3 us -> 36.3 us
  Pallas kernels: 41.3 us -> 43.4 us
    all_to_all x1, starting transfers between devices: 19.1 us -> 13.3 us  [local(): gathered = lax.all_to_all(pair, CHIPS, 0, 0, tiled=True).astype(F32)]
    pallas_call x3, Pallas kernels: 31.2 us -> 33.3 us  [the longest x1 14.8 us: own_part(): pl.pallas_call(own_kernel, in_specs=[SMEM] * 4 + [HBM] * 2 + [VMEM] * 2 +...]
  transfers between devices with their start and end apart: 12 -> 12, of which waited for: 5 -> 4; matrix products, arithmetic and copies ran while one was open for 1% -> 1% of each run, Pallas kernels for 22% -> 30%
where the time goes in v6:
time: 91.4 us; the launch traced here: 90.5 us
  Pallas kernels  43.4 us (47%)
  starting transfers between devices  36.3 us (40%)
  waiting for transfers between devices  7.04 us (8%)
  between operations  2.17 us (2%)
  local copies, waits for them, and re-layouts  1.52 us (2%)
    pallas_call x1, Pallas kernels, own_part(): pl.pallas_call(own_kernel, in_specs=[SMEM] * 4 + [HBM] * 2 + [VMEM] * 2 +...  14.8 us
    ppermute x8, starting transfers between devices, exchange(): got[k] = lax.ppermute(parts[k], axis, pairs)  13.7 us
    all_to_all x1, starting transfers between devices, local(): gathered = lax.all_to_all(pair, CHIPS, 0, 0, tiled=True).astype(F32)  13.3 us
    pallas_call x1, Pallas kernels, dense_part(): pl.pallas_call(dense_kernel, in_specs=[SMEM] * 3 + [VMEM] * 10 + [HBM] *...  9.98 us
    all_to_all x1, starting transfers between devices, local(): tiles = lax.all_to_all(tiles, CHIPS, 0, 0, tiled=True)  8.71 us
    pallas_call x1, Pallas kernels, back_part(): pl.pallas_call(back_kernel, in_specs=[SMEM] * 2 + [HBM] * 2, out_specs=[V...  8.46 us
    pallas_call x1, Pallas kernels, finish(): pl.pallas_call(finish_kernel, in_specs=[VMEM] * 6 + [HBM], out_specs=HBM,...  4.27 us
    pallas_call x1, Pallas kernels, pack(): pl.pallas_call(pack_kernel, in_specs=[VMEM, HBM], out_specs=[VMEM] * 4, o...  4.04 us
  transfers between devices with their start and end apart: 12, of which 4 were waited for; matrix products, arithmetic and copies ran while one was open for 1% of the time, Pallas kernels for 30%

profile of v6, /device:TPU:1, one launch (start us, length us, event | category | flops | bytes accessed | tf_op | source)
XLA Modules:
  0.0 90.5 jit_solution(15410751527219640830)
XLA Ops:
  0.6 0.7 copy-done
  1.3 4.0 %pack.1 = (bf16[256,512]{1,0:T(8,128)(2,1)S(1)}, bf16[256,512]{1,0:T(8,128)(2,1)S(1)}, bf16[256,512]{1,0:T(8,128)(2,1)S(1)}, bf16[256,512]{1,0:T(8,128)(2,1)S(1)}) custom-call(s32[4,256]{1,0:T(4,128)S(1)} %bitcast.3, bf16[4096,512]{1,0:T(8,128)(2,1)} %feats.1), custom_call_target="tpu_custom_call" | custom-call | flops 3000000000 | bytes 9000000 | tf_op jit(solution)/shard_map/pack/pallas_call | solution.py:90
  5.4 1.5 %collective-permute-start = (bf16[256,512]{1,0:T(8,128)(2,1)S(1)}, bf16[256,512]{1,0:T(8,128)(2,1)S(1)}, u32[]{:S(2)}, u32[]{:S(2)}) collective-permute-start(bf16[256,512]{1,0:T(8,128)(2,1)S(1)} %get-tuple-element.57), channel_id=1, source_target_pairs={{0,8},{8,0},{16,24},{24,16},{32,40},{40,32},{48,56},{56,48},{64,72... | collective-permute-start | bytes 786440 | tf_op jit(solution)/shard_map/ppermute | solution.py:522
  6.9 4.6 %collective-permute-start.1 = (bf16[256,512]{1,0:T(8,128)(2,1)S(1)}, bf16[256,512]{1,0:T(8,128)(2,1)S(1)}, u32[]{:S(2)}, u32[]{:S(2)}) collective-permute-start(bf16[256,512]{1,0:T(8,128)(2,1)S(1)} %get-tuple-element.58), channel_id=1, source_target_pairs={{8,16},{16,8},{24,32},{32,24},{40,48},{48,40},{56,64},{64,56},{72,... | collective-permute-start | bytes 786440 | tf_op jit(solution)/shard_map/ppermute | solution.py:522
  11.5 0.4 collective-permute-start.2
  11.9 0.7 collective-permute-start.3
  13.9 14.8 %own_part.1 = (f32[4224,512]{1,0:T(8,128)S(1)}, bf16[96,128,128]{2,1,0:T(8,128)(2,1)S(1)}, f32[512,512]{1,0:T(8,128)S(1)}, f32[8,512]{1,0:T(8,128)S(1)}, bf16[40...) custom-call(s32[1,96]{1,0:T(1,128)S(1)} %copy-done.4, ...), custom_call_target="tpu_custom_call" | custom-call | flops 12999999488 | bytes 39000000 | tf_op jit(solution)/shard_map/own_part/pallas_call | solution.py:244
  28.8 10.0 %dense_part.1 = (f32[4224,512]{1,0:T(8,128)S(1)}, bf16[4096,512]{1,0:T(8,128)(2,1)}, bf16[4096,512]{1,0:T(8,128)(2,1)}, bf16[256,512]{1,0:T(8,128)(2,1)S(1)}, bf...) custom-call(s32[1]{0:T(128)S(6)} %copy.23.nodes, ...), custom_call_target="tpu_custom_call", output_to_operand_aliasing={{0}: (3, {}), {1}: (14, {}), {2}: (15, {})} | custom-call | flops 10000000000 | bytes 30000000 | tf_op jit(solution)/shard_map/dense_part/pallas_call | solution.py:347
  38.9 1.5 %collective-permute-done.4.given = bf16[65,16,128]{2,1,0:T(8,128)(2,1)S(1)} collective-permute-done((bf16[65,16,128]{2,1,0:T(8,128)(2,1)S(1)}, bf16[65,16,128]{2,1,0:T(8,128)(2,1)S(1)}, u32[]{:S(2)}, u32[]{:S(2)}) %collective-permute-start.4) | collective-permute-done | bytes 266272 | tf_op jit(solution)/shard_map/ppermute | solution.py:539
  40.4 0.8 pair_sum.1
  41.2 13.3 %all-to-all-start = ((bf16[64,16,128]{2,1,0:T(8,128)(2,1)}), bf16[64,16,128]{2,1,0:T(8,128)(2,1)S(1)}, u32[]{:S(2)}, u32[]{:S(2)}) async-start(bf16[64,16,128]{2,1,0:T(8,128)(2,1)} %get-tuple-element.72), calls=%async_computation | async-start | bytes 524288 | tf_op jit(solution)/shard_map/all_to_all | solution.py:542
  54.5 0.7 collective-permute-start.5
  55.2 4.6 %collective-permute-start.6 = (bf16[256,512]{1,0:T(8,128)(2,1)S(1)}, bf16[256,512]{1,0:T(8,128)(2,1)S(1)}, u32[]{:S(2)}, u32[]{:S(2)}) collective-permute-start(bf16[256,512]{1,0:T(8,128)(2,1)S(1)} %get-tuple-element.80), channel_id=1, source_target_pairs={{8,16},{16,8},{24,32},{32,24},{40,48},{48,40},{56,64},{64,56},{72,... | collective-permute-start | bytes 786440 | tf_op jit(solution)/shard_map/ppermute | solution.py:522
  59.8 0.5 collective-permute-start.7
  60.4 0.7 collective-permute-start.8
  61.1 3.2 %all-to-all-done = bf16[64,16,128]{2,1,0:T(8,128)(2,1)S(1)} async-done(((bf16[64,16,128]{2,1,0:T(8,128)(2,1)}), bf16[64,16,128]{2,1,0:T(8,128)(2,1)S(1)}, u32[]{:S(2)}, u32[]{:S(2)}) %all-to-all-start) | async-done | bytes 262176 | tf_op jit(solution)/shard_map/all_to_all | solution.py:542
  64.3 0.8 broadcast_in_dim.2
  65.1 8.7 %all-to-all-start.1 = ((bf16[64,24,128]{2,1,0:T(8,128)(2,1)}), bf16[64,24,128]{2,1,0:T(8,128)(2,1)S(1)}, u32[]{:S(2)}, u32[]{:S(2)}) async-start(bf16[64,24,128]{2,1,0:T(8,128)(2,1)} %broadcast_in_dim.2), calls=%async_computation.1 | async-start | bytes 786432 | tf_op jit(solution)/shard_map/all_to_all | solution.py:546
  73.9 8.5 %back_part.1 = (f32[4224,512]{1,0:T(8,128)S(1)}, bf16[4096,512]{1,0:T(8,128)(2,1)}) custom-call(s32[1]{0:T(128)S(6)} %copy.23.nodes, s32[128]{0:T(128)S(1)} %get-tuple-element.75.table, bf16[96,128,128]{2,1,0:T(8,128)(2,1)} %adj_in.1, bf16[4096,512]{1,0:T(8,128)(2,1)} %get-tuple-element.77.back_in), custom_call_target="tpu_custom_call" | custom-call | flops 8999999488 | bytes 27000000 | tf_op jit(solution)/shard_map/back_part/pallas_call | solution.py:424
  82.4 4.3 %finish.1 = bf16[4096,512]{1,0:T(8,128)(2,1)} custom-call(s32[4,256]{1,0:T(4,128)S(1)} %bitcast.4, f32[4224,512]{1,0:T(8,128)S(1)} %get-tuple-element.78.spread, bf16[256,512]{1,0:T(8,128)(2,1)S(1)} %collective-permute-done.5.r0, bf16[256,512]{1,0:T(8,128)(2,1)S(1)} %collective-permute-done.6.r1, ...), custom_call_target="tpu_custom_call", output_to_operand_aliasing={{}: (6, {})} | custom-call | flops 4000000000 | bytes 12000000 | tf_op jit(solution)/shard_map/finish/pallas_call | solution.py:460
  86.6 1.2 %all-to-all-done.1.tiles = bf16[64,24,128]{2,1,0:T(8,128)(2,1)S(1)} async-done(((bf16[64,24,128]{2,1,0:T(8,128)(2,1)}), bf16[64,24,128]{2,1,0:T(8,128)(2,1)S(1)}, u32[]{:S(2)}, u32[]{:S(2)}) %all-to-all-start.1) | async-done | bytes 393248 | tf_op jit(solution)/shard_map/all_to_all | solution.py:546
  87.8 0.5 collective-permute-start.9
  88.3 1.2 %collective-permute-done.9.other = bf16[64,16,128]{2,1,0:T(8,128)(2,1)S(1)} collective-permute-done((bf16[64,16,128]{2,1,0:T(8,128)(2,1)S(1)}, bf16[64,16,128]{2,1,0:T(8,128)(2,1)S(1)}, u32[]{:S(2)}, u32[]{:S(2)}) %collective-permute-start.9) | collective-permute-done | bytes 262176 | tf_op jit(solution)/shard_map/ppermute | solution.py:550
  89.5 1.0 %join.1 = (f32[512,512]{1,0:T(8,128)}, f32[4,128]{1,0:T(4,128)}) custom-call(bf16[64,24,128]{2,1,0:T(8,128)(2,1)S(1)} %all-to-all-done.1.tiles, bf16[64,16,128]{2,1,0:T(8,128)(2,1)S(1)} %collective-permute-done.9.other), custom_call_target="tpu_custom_call" | custom-call | flops 1000000000 | bytes 3000000 | tf_op jit(solution)/shard_map/join/pallas_call | solution.py:506
  (24 shorter events, 0.2 us)
Async XLA Ops:
  0.6 0.7 copy-start
  1.3 12.6 %copy-start.2 = (bf16[512,512]{1,0:T(8,128)(2,1)S(1)}, bf16[512,512]{1,0:T(8,128)(2,1)}, u32[]{:S(2)}) copy-start(bf16[512,512]{1,0:T(8,128)(2,1)} %weight.3) | copy-start | bytes 1572868
  1.3 12.6 %copy-start.3 = (f32[512]{0:T(512)S(1)}, f32[512]{0:T(512)}, u32[]{:S(2)}) copy-start(f32[512]{0:T(512)} %param.18) | copy-start | bytes 6148
  1.3 12.6 %copy-start.4 = (s32[1,96]{1,0:T(1,128)S(1)}, s32[1,96]{1,0:T(1,128)}, u32[]{:S(2)}) copy-start(s32[1,96]{1,0:T(1,128)} %rows.1) | copy-start | bytes 1156
  1.3 12.6 %copy-start.5 = (s32[1,96]{1,0:T(1,128)S(1)}, s32[1,96]{1,0:T(1,128)}, u32[]{:S(2)}) copy-start(s32[1,96]{1,0:T(1,128)} %cols.1) | copy-start | bytes 1156
  5.4 23.4 %collective-permute-start = (bf16[256,512]{1,0:T(8,128)(2,1)S(1)}, bf16[256,512]{1,0:T(8,128)(2,1)S(1)}, u32[]{:S(2)}, u32[]{:S(2)}) collective-permute-start(bf16[256,512]{1,0:T(8,128)(2,1)S(1)} %get-tuple-element.57), channel_id=1, source_target_pairs={{0,8},{8,0},{16,24},{24,16},{32,40},{40,32},{48,56},{56,48},{64,72... | collective-permute-start | bytes 786440 | tf_op jit(solution)/shard_map/ppermute | solution.py:522
  6.9 21.9 %collective-permute-start.1 = (bf16[256,512]{1,0:T(8,128)(2,1)S(1)}, bf16[256,512]{1,0:T(8,128)(2,1)S(1)}, u32[]{:S(2)}, u32[]{:S(2)}) collective-permute-start(bf16[256,512]{1,0:T(8,128)(2,1)S(1)} %get-tuple-element.58), channel_id=1, source_target_pairs={{8,16},{16,8},{24,32},{32,24},{40,48},{48,40},{56,64},{64,56},{72,... | collective-permute-start | bytes 786440 | tf_op jit(solution)/shard_map/ppermute | solution.py:522
  11.5 17.3 %collective-permute-start.2 = (bf16[256,512]{1,0:T(8,128)(2,1)S(1)}, bf16[256,512]{1,0:T(8,128)(2,1)S(1)}, u32[]{:S(2)}, u32[]{:S(2)}) collective-permute-start(bf16[256,512]{1,0:T(8,128)(2,1)S(1)} %get-tuple-element.59), channel_id=1, source_target_pairs={{0,1},{1,0},{2,3},{3,2},{4,5},{5,4},{6,7},{7,6},{8,9},{9,8},{10,11... | collective-permute-start | bytes 786440 | tf_op jit(solution)/shard_map/ppermute | solution.py:522
  11.9 16.9 %collective-permute-start.3 = (bf16[256,512]{1,0:T(8,128)(2,1)S(1)}, bf16[256,512]{1,0:T(8,128)(2,1)S(1)}, u32[]{:S(2)}, u32[]{:S(2)}) collective-permute-start(bf16[256,512]{1,0:T(8,128)(2,1)S(1)} %get-tuple-element.60), channel_id=1, source_target_pairs={{1,2},{2,1},{3,4},{4,3},{5,6},{6,5},{9,10},{10,9},{11,12},{12,11},... | collective-permute-start | bytes 786440 | tf_op jit(solution)/shard_map/ppermute | solution.py:522
  38.8 1.6 %collective-permute-start.4 = (bf16[65,16,128]{2,1,0:T(8,128)(2,1)S(1)}, bf16[65,16,128]{2,1,0:T(8,128)(2,1)S(1)}, u32[]{:S(2)}, u32[]{:S(2)}) collective-permute-start(bf16[65,16,128]{2,1,0:T(8,128)(2,1)S(1)} %get-tuple-element.65), channel_id=1, source_target_pairs={{0,8},{8,0},{1,9},{9,1},{2,10},{10,2},{3,11},{11,3},{4,12},{12,4},... | collective-permute-start | bytes 798728 | tf_op jit(solution)/shard_map/ppermute | solution.py:539
  41.2 23.0 %all-to-all-start = ((bf16[64,16,128]{2,1,0:T(8,128)(2,1)}), bf16[64,16,128]{2,1,0:T(8,128)(2,1)S(1)}, u32[]{:S(2)}, u32[]{:S(2)}) async-start(bf16[64,16,128]{2,1,0:T(8,128)(2,1)} %get-tuple-element.72), calls=%async_computation | async-start | bytes 524288 | tf_op jit(solution)/shard_map/all_to_all | solution.py:542
  54.5 27.8 %collective-permute-start.5 = (bf16[256,512]{1,0:T(8,128)(2,1)S(1)}, bf16[256,512]{1,0:T(8,128)(2,1)S(1)}, u32[]{:S(2)}, u32[]{:S(2)}) collective-permute-start(bf16[256,512]{1,0:T(8,128)(2,1)S(1)} %get-tuple-element.79), channel_id=1, source_target_pairs={{0,8},{8,0},{16,24},{24,16},{32,40},{40,32},{48,56},{56,48},{64,72... | collective-permute-start | bytes 786440 | tf_op jit(solution)/shard_map/ppermute | solution.py:522
  55.2 27.1 %collective-permute-start.6 = (bf16[256,512]{1,0:T(8,128)(2,1)S(1)}, bf16[256,512]{1,0:T(8,128)(2,1)S(1)}, u32[]{:S(2)}, u32[]{:S(2)}) collective-permute-start(bf16[256,512]{1,0:T(8,128)(2,1)S(1)} %get-tuple-element.80), channel_id=1, source_target_pairs={{8,16},{16,8},{24,32},{32,24},{40,48},{48,40},{56,64},{64,56},{72,... | collective-permute-start | bytes 786440 | tf_op jit(solution)/shard_map/ppermute | solution.py:522
  59.8 22.5 %collective-permute-start.7 = (bf16[256,512]{1,0:T(8,128)(2,1)S(1)}, bf16[256,512]{1,0:T(8,128)(2,1)S(1)}, u32[]{:S(2)}, u32[]{:S(2)}) collective-permute-start(bf16[256,512]{1,0:T(8,128)(2,1)S(1)} %get-tuple-element.81), channel_id=1, source_target_pairs={{0,1},{1,0},{2,3},{3,2},{4,5},{5,4},{6,7},{7,6},{8,9},{9,8},{10,11... | collective-permute-start | bytes 786440 | tf_op jit(solution)/shard_map/ppermute | solution.py:522
  60.4 22.0 %collective-permute-start.8 = (bf16[256,512]{1,0:T(8,128)(2,1)S(1)}, bf16[256,512]{1,0:T(8,128)(2,1)S(1)}, u32[]{:S(2)}, u32[]{:S(2)}) collective-permute-start(bf16[256,512]{1,0:T(8,128)(2,1)S(1)} %get-tuple-element.82), channel_id=1, source_target_pairs={{1,2},{2,1},{3,4},{4,3},{5,6},{6,5},{9,10},{10,9},{11,12},{12,11},... | collective-permute-start | bytes 786440 | tf_op jit(solution)/shard_map/ppermute | solution.py:522
  65.1 22.7 %all-to-all-start.1 = ((bf16[64,24,128]{2,1,0:T(8,128)(2,1)}), bf16[64,24,128]{2,1,0:T(8,128)(2,1)S(1)}, u32[]{:S(2)}, u32[]{:S(2)}) async-start(bf16[64,24,128]{2,1,0:T(8,128)(2,1)} %broadcast_in_dim.2), calls=%async_computation.1 | async-start | bytes 786432 | tf_op jit(solution)/shard_map/all_to_all | solution.py:546
  73.8 8.5 %copy-start.1 = (s32[1,4,256]{2,1,0:T(4,128)S(1)}, s32[1,4,256]{2,1,0:T(4,128)}, u32[]{:S(2)}) copy-start(s32[1,4,256]{2,1,0:T(4,128)} %param.16) | copy-start | bytes 12292
  87.8 1.6 %collective-permute-start.9 = (bf16[64,16,128]{2,1,0:T(8,128)(2,1)S(1)}, bf16[64,16,128]{2,1,0:T(8,128)(2,1)S(1)}, u32[]{:S(2)}, u32[]{:S(2)}) collective-permute-start(bf16[64,16,128]{2,1,0:T(8,128)(2,1)S(1)} %slice.3), channel_id=1, source_target_pairs={{0,8},{8,0},{1,9},{9,1},{2,10},{10,2},{3,11},{11,3},{4,12},{12,4},... | collective-permute-start | bytes 786440 | tf_op jit(solution)/shard_map/ppermute | solution.py:550

commit v7 on v6

--- a/solution.py
+++ b/solution.py
@@ -20,7 +20,7 @@
 LAST = 127
 DEVICES = 128
 PEERS = 64
-UNROLL = 16
+UNROLL = 20
 FEW = 8
 BF = jnp.bfloat16
 F32 = jnp.float32

time: 91.4 us -> 91.1 us (level)
  Pallas kernels: 43.4 us -> 40.8 us
  starting transfers between devices: 36.3 us -> 37.7 us
  waiting for transfers between devices: 7.04 us -> 8.28 us
    pallas_call x1, Pallas kernels: 14.8 us -> 13.4 us  [own_part(): pl.pallas_call(own_kernel, in_specs=[SMEM] * 4 + [HBM] * 2 + [VMEM] * 2 +...]
    all_to_all x1, starting transfers between devices: 13.3 us -> 14.7 us  [local(): gathered = lax.all_to_all(pair, CHIPS, 0, 0, tiled=True).astype(F32)]
    pallas_call x1, Pallas kernels: 8.46 us -> 7.21 us  [back_part(): pl.pallas_call(back_kernel, in_specs=[SMEM] * 2 + [HBM] * 2, out_specs=[V...]
    all_to_all x1, waiting for transfers between devices: 1.17 us -> 2.41 us  [local(): tiles = lax.all_to_all(tiles, CHIPS, 0, 0, tiled=True)]
  transfers between devices with their start and end apart: 12 -> 12, of which waited for: 4 -> 4; matrix products, arithmetic and copies ran while one was open for 1% -> 1% of each run, Pallas kernels for 30% -> 28%
where the time goes in v7:
time: 91.1 us; the launch traced here: 90.5 us
  Pallas kernels  40.8 us (45%)
  starting transfers between devices  37.7 us (41%)
  waiting for transfers between devices  8.28 us (9%)
  between operations  2.17 us (2%)
  local copies, waits for them, and re-layouts  1.52 us (2%)
    all_to_all x1, starting transfers between devices, local(): gathered = lax.all_to_all(pair, CHIPS, 0, 0, tiled=True).astype(F32)  14.7 us
    ppermute x8, starting transfers between devices, exchange(): got[k] = lax.ppermute(parts[k], axis, pairs)  13.7 us
    pallas_call x1, Pallas kernels, own_part(): pl.pallas_call(own_kernel, in_specs=[SMEM] * 4 + [HBM] * 2 + [VMEM] * 2 +...  13.4 us
    pallas_call x1, Pallas kernels, dense_part(): pl.pallas_call(dense_kernel, in_specs=[SMEM] * 3 + [VMEM] * 10 + [HBM] *...  10 us
    all_to_all x1, starting transfers between devices, local(): tiles = lax.all_to_all(tiles, CHIPS, 0, 0, tiled=True)  8.71 us
    pallas_call x1, Pallas kernels, back_part(): pl.pallas_call(back_kernel, in_specs=[SMEM] * 2 + [HBM] * 2, out_specs=[V...  7.21 us
    pallas_call x1, Pallas kernels, finish(): pl.pallas_call(finish_kernel, in_specs=[VMEM] * 6 + [HBM], out_specs=HBM,...  4.27 us
    pallas_call x1, Pallas kernels, pack(): pl.pallas_call(pack_kernel, in_specs=[VMEM, HBM], out_specs=[VMEM] * 4, o...  4.04 us
  transfers between devices with their start and end apart: 12, of which 4 were waited for; matrix products, arithmetic and copies ran while one was open for 1% of the time, Pallas kernels for 28%

profile of v7, /device:TPU:1, one launch (start us, length us, event | category | flops | bytes accessed | tf_op | source)
XLA Modules:
  0.0 90.5 jit_solution(6480196574127396935)
XLA Ops:
  0.6 0.7 copy-done
  1.3 4.0 %pack.1 = (bf16[256,512]{1,0:T(8,128)(2,1)S(1)}, bf16[256,512]{1,0:T(8,128)(2,1)S(1)}, bf16[256,512]{1,0:T(8,128)(2,1)S(1)}, bf16[256,512]{1,0:T(8,128)(2,1)S(1)}) custom-call(s32[4,256]{1,0:T(4,128)S(1)} %bitcast.3, bf16[4096,512]{1,0:T(8,128)(2,1)} %feats.1), custom_call_target="tpu_custom_call" | custom-call | flops 3000000000 | bytes 9000000 | tf_op jit(solution)/shard_map/pack/pallas_call | solution.py:90
  5.4 1.5 %collective-permute-start = (bf16[256,512]{1,0:T(8,128)(2,1)S(1)}, bf16[256,512]{1,0:T(8,128)(2,1)S(1)}, u32[]{:S(2)}, u32[]{:S(2)}) collective-permute-start(bf16[256,512]{1,0:T(8,128)(2,1)S(1)} %get-tuple-element.57), channel_id=1, source_target_pairs={{0,8},{8,0},{16,24},{24,16},{32,40},{40,32},{48,56},{56,48},{64,72... | collective-permute-start | bytes 786440 | tf_op jit(solution)/shard_map/ppermute | solution.py:522
  6.9 4.6 %collective-permute-start.1 = (bf16[256,512]{1,0:T(8,128)(2,1)S(1)}, bf16[256,512]{1,0:T(8,128)(2,1)S(1)}, u32[]{:S(2)}, u32[]{:S(2)}) collective-permute-start(bf16[256,512]{1,0:T(8,128)(2,1)S(1)} %get-tuple-element.58), channel_id=1, source_target_pairs={{8,16},{16,8},{24,32},{32,24},{40,48},{48,40},{56,64},{64,56},{72,... | collective-permute-start | bytes 786440 | tf_op jit(solution)/shard_map/ppermute | solution.py:522
  11.5 0.4 collective-permute-start.2
  11.9 0.7 collective-permute-start.3
  13.9 13.4 %own_part.1 = (f32[4224,512]{1,0:T(8,128)S(1)}, bf16[96,128,128]{2,1,0:T(8,128)(2,1)S(1)}, f32[512,512]{1,0:T(8,128)S(1)}, f32[8,512]{1,0:T(8,128)S(1)}, bf16[40...) custom-call(s32[1,96]{1,0:T(1,128)S(1)} %copy-done.4, ...), custom_call_target="tpu_custom_call" | custom-call | flops 12999999488 | bytes 39000000 | tf_op jit(solution)/shard_map/own_part/pallas_call | solution.py:244
  27.4 10.0 %dense_part.1 = (f32[4224,512]{1,0:T(8,128)S(1)}, bf16[4096,512]{1,0:T(8,128)(2,1)}, bf16[4096,512]{1,0:T(8,128)(2,1)}, bf16[256,512]{1,0:T(8,128)(2,1)S(1)}, bf...) custom-call(s32[1]{0:T(128)S(6)} %copy.23.nodes, ...), custom_call_target="tpu_custom_call", output_to_operand_aliasing={{0}: (3, {}), {1}: (14, {}), {2}: (15, {})} | custom-call | flops 10000000000 | bytes 30000000 | tf_op jit(solution)/shard_map/dense_part/pallas_call | solution.py:347
  37.5 1.5 %collective-permute-done.4.given = bf16[65,16,128]{2,1,0:T(8,128)(2,1)S(1)} collective-permute-done((bf16[65,16,128]{2,1,0:T(8,128)(2,1)S(1)}, bf16[65,16,128]{2,1,0:T(8,128)(2,1)S(1)}, u32[]{:S(2)}, u32[]{:S(2)}) %collective-permute-start.4) | collective-permute-done | bytes 266272 | tf_op jit(solution)/shard_map/ppermute | solution.py:539
  39.0 0.8 pair_sum.1
  39.8 14.7 %all-to-all-start = ((bf16[64,16,128]{2,1,0:T(8,128)(2,1)}), bf16[64,16,128]{2,1,0:T(8,128)(2,1)S(1)}, u32[]{:S(2)}, u32[]{:S(2)}) async-start(bf16[64,16,128]{2,1,0:T(8,128)(2,1)} %get-tuple-element.72), calls=%async_computation | async-start | bytes 524288 | tf_op jit(solution)/shard_map/all_to_all | solution.py:542
  54.5 0.7 collective-permute-start.5
  55.2 4.8 %collective-permute-start.6 = (bf16[256,512]{1,0:T(8,128)(2,1)S(1)}, bf16[256,512]{1,0:T(8,128)(2,1)S(1)}, u32[]{:S(2)}, u32[]{:S(2)}) collective-permute-start(bf16[256,512]{1,0:T(8,128)(2,1)S(1)} %get-tuple-element.80), channel_id=1, source_target_pairs={{8,16},{16,8},{24,32},{32,24},{40,48},{48,40},{56,64},{64,56},{72,... | collective-permute-start | bytes 786440 | tf_op jit(solution)/shard_map/ppermute | solution.py:522
  60.0 0.4 collective-permute-start.7
  60.4 0.7 collective-permute-start.8
  61.1 3.2 %all-to-all-done = bf16[64,16,128]{2,1,0:T(8,128)(2,1)S(1)} async-done(((bf16[64,16,128]{2,1,0:T(8,128)(2,1)}), bf16[64,16,128]{2,1,0:T(8,128)(2,1)S(1)}, u32[]{:S(2)}, u32[]{:S(2)}) %all-to-all-start) | async-done | bytes 262176 | tf_op jit(solution)/shard_map/all_to_all | solution.py:542
  64.3 0.8 broadcast_in_dim.2
  65.1 8.7 %all-to-all-start.1 = ((bf16[64,24,128]{2,1,0:T(8,128)(2,1)}), bf16[64,24,128]{2,1,0:T(8,128)(2,1)S(1)}, u32[]{:S(2)}, u32[]{:S(2)}) async-start(bf16[64,24,128]{2,1,0:T(8,128)(2,1)} %broadcast_in_dim.2), calls=%async_computation.1 | async-start | bytes 786432 | tf_op jit(solution)/shard_map/all_to_all | solution.py:546
  73.9 7.2 %back_part.1 = (f32[4224,512]{1,0:T(8,128)S(1)}, bf16[4096,512]{1,0:T(8,128)(2,1)}) custom-call(s32[1]{0:T(128)S(6)} %copy.23.nodes, s32[128]{0:T(128)S(1)} %get-tuple-element.75.table, bf16[96,128,128]{2,1,0:T(8,128)(2,1)} %adj_in.1, bf16[4096,512]{1,0:T(8,128)(2,1)} %get-tuple-element.77.back_in), custom_call_target="tpu_custom_call" | custom-call | flops 8999999488 | bytes 27000000 | tf_op jit(solution)/shard_map/back_part/pallas_call | solution.py:424
  81.1 4.3 %finish.1 = bf16[4096,512]{1,0:T(8,128)(2,1)} custom-call(s32[4,256]{1,0:T(4,128)S(1)} %bitcast.4, f32[4224,512]{1,0:T(8,128)S(1)} %get-tuple-element.78.spread, bf16[256,512]{1,0:T(8,128)(2,1)S(1)} %collective-permute-done.5.r0, bf16[256,512]{1,0:T(8,128)(2,1)S(1)} %collective-permute-done.6.r1, ...), custom_call_target="tpu_custom_call", output_to_operand_aliasing={{}: (6, {})} | custom-call | flops 4000000000 | bytes 12000000 | tf_op jit(solution)/shard_map/finish/pallas_call | solution.py:460
  85.4 2.4 %all-to-all-done.1.tiles = bf16[64,24,128]{2,1,0:T(8,128)(2,1)S(1)} async-done(((bf16[64,24,128]{2,1,0:T(8,128)(2,1)}), bf16[64,24,128]{2,1,0:T(8,128)(2,1)S(1)}, u32[]{:S(2)}, u32[]{:S(2)}) %all-to-all-start.1) | async-done | bytes 393248 | tf_op jit(solution)/shard_map/all_to_all | solution.py:546
  87.9 0.5 collective-permute-start.9
  88.3 1.2 %collective-permute-done.9.other = bf16[64,16,128]{2,1,0:T(8,128)(2,1)S(1)} collective-permute-done((bf16[64,16,128]{2,1,0:T(8,128)(2,1)S(1)}, bf16[64,16,128]{2,1,0:T(8,128)(2,1)S(1)}, u32[]{:S(2)}, u32[]{:S(2)}) %collective-permute-start.9) | collective-permute-done | bytes 262176 | tf_op jit(solution)/shard_map/ppermute | solution.py:550
  89.5 1.0 %join.1 = (f32[512,512]{1,0:T(8,128)}, f32[4,128]{1,0:T(4,128)}) custom-call(bf16[64,24,128]{2,1,0:T(8,128)(2,1)S(1)} %all-to-all-done.1.tiles, bf16[64,16,128]{2,1,0:T(8,128)(2,1)S(1)} %collective-permute-done.9.other), custom_call_target="tpu_custom_call" | custom-call | flops 1000000000 | bytes 3000000 | tf_op jit(solution)/shard_map/join/pallas_call | solution.py:506
  (24 shorter events, 0.2 us)
Async XLA Ops:
  0.6 0.7 copy-start
  1.3 12.6 %copy-start.2 = (bf16[512,512]{1,0:T(8,128)(2,1)S(1)}, bf16[512,512]{1,0:T(8,128)(2,1)}, u32[]{:S(2)}) copy-start(bf16[512,512]{1,0:T(8,128)(2,1)} %weight.3) | copy-start | bytes 1572868
  1.3 12.6 %copy-start.3 = (f32[512]{0:T(512)S(1)}, f32[512]{0:T(512)}, u32[]{:S(2)}) copy-start(f32[512]{0:T(512)} %param.18) | copy-start | bytes 6148
  1.3 12.6 %copy-start.4 = (s32[1,96]{1,0:T(1,128)S(1)}, s32[1,96]{1,0:T(1,128)}, u32[]{:S(2)}) copy-start(s32[1,96]{1,0:T(1,128)} %rows.1) | copy-start | bytes 1156
  1.3 12.6 %copy-start.5 = (s32[1,96]{1,0:T(1,128)S(1)}, s32[1,96]{1,0:T(1,128)}, u32[]{:S(2)}) copy-start(s32[1,96]{1,0:T(1,128)} %cols.1) | copy-start | bytes 1156
  5.4 22.0 %collective-permute-start = (bf16[256,512]{1,0:T(8,128)(2,1)S(1)}, bf16[256,512]{1,0:T(8,128)(2,1)S(1)}, u32[]{:S(2)}, u32[]{:S(2)}) collective-permute-start(bf16[256,512]{1,0:T(8,128)(2,1)S(1)} %get-tuple-element.57), channel_id=1, source_target_pairs={{0,8},{8,0},{16,24},{24,16},{32,40},{40,32},{48,56},{56,48},{64,72... | collective-permute-start | bytes 786440 | tf_op jit(solution)/shard_map/ppermute | solution.py:522
  6.9 20.5 %collective-permute-start.1 = (bf16[256,512]{1,0:T(8,128)(2,1)S(1)}, bf16[256,512]{1,0:T(8,128)(2,1)S(1)}, u32[]{:S(2)}, u32[]{:S(2)}) collective-permute-start(bf16[256,512]{1,0:T(8,128)(2,1)S(1)} %get-tuple-element.58), channel_id=1, source_target_pairs={{8,16},{16,8},{24,32},{32,24},{40,48},{48,40},{56,64},{64,56},{72,... | collective-permute-start | bytes 786440 | tf_op jit(solution)/shard_map/ppermute | solution.py:522
  11.5 15.9 %collective-permute-start.2 = (bf16[256,512]{1,0:T(8,128)(2,1)S(1)}, bf16[256,512]{1,0:T(8,128)(2,1)S(1)}, u32[]{:S(2)}, u32[]{:S(2)}) collective-permute-start(bf16[256,512]{1,0:T(8,128)(2,1)S(1)} %get-tuple-element.59), channel_id=1, source_target_pairs={{0,1},{1,0},{2,3},{3,2},{4,5},{5,4},{6,7},{7,6},{8,9},{9,8},{10,11... | collective-permute-start | bytes 786440 | tf_op jit(solution)/shard_map/ppermute | solution.py:522
  11.9 15.5 %collective-permute-start.3 = (bf16[256,512]{1,0:T(8,128)(2,1)S(1)}, bf16[256,512]{1,0:T(8,128)(2,1)S(1)}, u32[]{:S(2)}, u32[]{:S(2)}) collective-permute-start(bf16[256,512]{1,0:T(8,128)(2,1)S(1)} %get-tuple-element.60), channel_id=1, source_target_pairs={{1,2},{2,1},{3,4},{4,3},{5,6},{6,5},{9,10},{10,9},{11,12},{12,11},... | collective-permute-start | bytes 786440 | tf_op jit(solution)/shard_map/ppermute | solution.py:522
  37.4 1.6 %collective-permute-start.4 = (bf16[65,16,128]{2,1,0:T(8,128)(2,1)S(1)}, bf16[65,16,128]{2,1,0:T(8,128)(2,1)S(1)}, u32[]{:S(2)}, u32[]{:S(2)}) collective-permute-start(bf16[65,16,128]{2,1,0:T(8,128)(2,1)S(1)} %get-tuple-element.65), channel_id=1, source_target_pairs={{0,8},{8,0},{1,9},{9,1},{2,10},{10,2},{3,11},{11,3},{4,12},{12,4},... | collective-permute-start | bytes 798728 | tf_op jit(solution)/shard_map/ppermute | solution.py:539
  39.8 24.4 %all-to-all-start = ((bf16[64,16,128]{2,1,0:T(8,128)(2,1)}), bf16[64,16,128]{2,1,0:T(8,128)(2,1)S(1)}, u32[]{:S(2)}, u32[]{:S(2)}) async-start(bf16[64,16,128]{2,1,0:T(8,128)(2,1)} %get-tuple-element.72), calls=%async_computation | async-start | bytes 524288 | tf_op jit(solution)/shard_map/all_to_all | solution.py:542
  54.5 26.6 %collective-permute-start.5 = (bf16[256,512]{1,0:T(8,128)(2,1)S(1)}, bf16[256,512]{1,0:T(8,128)(2,1)S(1)}, u32[]{:S(2)}, u32[]{:S(2)}) collective-permute-start(bf16[256,512]{1,0:T(8,128)(2,1)S(1)} %get-tuple-element.79), channel_id=1, source_target_pairs={{0,8},{8,0},{16,24},{24,16},{32,40},{40,32},{48,56},{56,48},{64,72... | collective-permute-start | bytes 786440 | tf_op jit(solution)/shard_map/ppermute | solution.py:522
  55.2 25.9 %collective-permute-start.6 = (bf16[256,512]{1,0:T(8,128)(2,1)S(1)}, bf16[256,512]{1,0:T(8,128)(2,1)S(1)}, u32[]{:S(2)}, u32[]{:S(2)}) collective-permute-start(bf16[256,512]{1,0:T(8,128)(2,1)S(1)} %get-tuple-element.80), channel_id=1, source_target_pairs={{8,16},{16,8},{24,32},{32,24},{40,48},{48,40},{56,64},{64,56},{72,... | collective-permute-start | bytes 786440 | tf_op jit(solution)/shard_map/ppermute | solution.py:522
  60.0 21.1 %collective-permute-start.7 = (bf16[256,512]{1,0:T(8,128)(2,1)S(1)}, bf16[256,512]{1,0:T(8,128)(2,1)S(1)}, u32[]{:S(2)}, u32[]{:S(2)}) collective-permute-start(bf16[256,512]{1,0:T(8,128)(2,1)S(1)} %get-tuple-element.81), channel_id=1, source_target_pairs={{0,1},{1,0},{2,3},{3,2},{4,5},{5,4},{6,7},{7,6},{8,9},{9,8},{10,11... | collective-permute-start | bytes 786440 | tf_op jit(solution)/shard_map/ppermute | solution.py:522
  60.4 20.7 %collective-permute-start.8 = (bf16[256,512]{1,0:T(8,128)(2,1)S(1)}, bf16[256,512]{1,0:T(8,128)(2,1)S(1)}, u32[]{:S(2)}, u32[]{:S(2)}) collective-permute-start(bf16[256,512]{1,0:T(8,128)(2,1)S(1)} %get-tuple-element.82), channel_id=1, source_target_pairs={{1,2},{2,1},{3,4},{4,3},{5,6},{6,5},{9,10},{10,9},{11,12},{12,11},... | collective-permute-start | bytes 786440 | tf_op jit(solution)/shard_map/ppermute | solution.py:522
  65.1 22.7 %all-to-all-start.1 = ((bf16[64,24,128]{2,1,0:T(8,128)(2,1)}), bf16[64,24,128]{2,1,0:T(8,128)(2,1)S(1)}, u32[]{:S(2)}, u32[]{:S(2)}) async-start(bf16[64,24,128]{2,1,0:T(8,128)(2,1)} %broadcast_in_dim.2), calls=%async_computation.1 | async-start | bytes 786432 | tf_op jit(solution)/shard_map/all_to_all | solution.py:546
  73.9 7.3 %copy-start.1 = (s32[1,4,256]{2,1,0:T(4,128)S(1)}, s32[1,4,256]{2,1,0:T(4,128)}, u32[]{:S(2)}) copy-start(s32[1,4,256]{2,1,0:T(4,128)} %param.16) | copy-start | bytes 12292
  87.9 1.6 %collective-permute-start.9 = (bf16[64,16,128]{2,1,0:T(8,128)(2,1)S(1)}, bf16[64,16,128]{2,1,0:T(8,128)(2,1)S(1)}, u32[]{:S(2)}, u32[]{:S(2)}) collective-permute-start(bf16[64,16,128]{2,1,0:T(8,128)(2,1)S(1)} %slice.3), channel_id=1, source_target_pairs={{0,8},{8,0},{1,9},{9,1},{2,10},{10,2},{3,11},{11,3},{4,12},{12,4},... | collective-permute-start | bytes 786440 | tf_op jit(solution)/shard_map/ppermute | solution.py:550
